TPU v7x, 32 devices: a whole 2x2x4 slice. The times are simulated.
32 devices in a mesh: axial: 8 (over z, x), azim: 4 (over y, core).
Axes of the slice: x: 2, y: 2, z: 4, core: 2. Of those that a mesh axis runs over, the one named last changes fastest.
Arguments:
- source: float32 [12, 32, 64, 256], P(None, 'axial', 'azim'), may hold values from -24 to 24
- storage: float32 [12, 32, 64, 256], P(None, 'axial', 'azim'), may hold values from 0.5 to 2
- materials: int32 [32, 64, 256], P('axial', 'azim'), may hold values from 0 to 3
- conductance: float32 [12], replicated, may hold values from 0.3 to 2
- mixing: float32 [4, 12, 12], replicated, may hold values from -0.9 to 0.9
- counts: int32 [8, 4], P('axial', 'azim'), may hold values from 30 to 120, as said below
- vis_owner: int32 [8, 4, 120, 4], P('axial', 'azim'), may hold values from 0 to 7, as said below
- vis_slot: int32 [8, 4, 120, 4], P('axial', 'azim'), may hold values from 0 to 119, as said below
- vis_block: int32 [8, 4, 120, 4], P('axial', 'azim'), may hold values from 0 to 7
- radiosity_old: bfloat16 [8, 4, 120, 128], P('axial', 'azim'), may hold values from -6 to 6
- view_blocks: bfloat16 [8, 128, 128], replicated, may hold values from -0.25 to 0.25
- emission: float32 [8, 4, 120, 128], P('axial', 'azim'), may hold values from 0.5 to 1.5
- reflect: float32 [8, 4, 120, 128], P('axial', 'azim'), may hold values from 0.2 to 0.8
Outputs:
- solution: float32 [12, 32, 64, 256], P(None, 'axial', 'azim')
- residual: float32 [12, 32, 64, 256], P(None, 'axial', 'azim')
- radiosity_new: float32 [8, 4, 120, 128], P('axial', 'azim')
Inputs may be any that keep to these rules, and one draw needn't show every extreme that they name: Slots 0 to counts - 1 of a device hold its panels; some device has exactly 120. `vis_owner`: owners lie in the same azimuthal column as the panel. Among the entries of the live panels of one device, no owner is named more than 60 times; some device names every owner exactly 60 times, and some owner is named exactly 60 times by every device. `vis_slot`: every entry is below the count of the named owner in the same azimuthal column.
All inputs are finite; a program needn't handle non-finite values.
Results may differ from a plain program's by a relative error of at most 0.0004.
Values may be sent and summed in bfloat16 or wider, within the bound.
No kernel may reach another device: no remote copies, remote signals or barrier semaphores. Data moves between devices by JAX's collectives and lax.ppermute only.
A program may use at most 128 MiB of HBM per device.

v0:
```python
import jax
import jax.numpy as jnp
from jax import lax
from jax.sharding import PartitionSpec as P

ITERS = 3


center_value = 14.2
half_width = 13.8


def extended(cells, sides, width, closed):
    for axis, dim in sides:
        count = lax.axis_size(axis)
        ends = count if closed else count - 1
        head = lax.slice_in_dim(cells, 0, width, axis=dim)
        tail = lax.slice_in_dim(cells, cells.shape[dim] - width, cells.shape[dim], axis=dim)
        cells = jnp.concatenate(
            [
                lax.ppermute(tail, axis, [(i, (i + 1) % count) for i in range(ends)]),
                cells,
                lax.ppermute(head, axis, [((i + 1) % count, i) for i in range(ends)]),
            ],
            axis=dim,
        )
    return cells


def combine(field, axial_ext, azim_ext, storage, masks, mixing, conductance):
    radial_pad = jnp.pad(field, ((0, 0), (0, 0), (0, 0), (1, 1)))
    beside = axial_ext[:, 2:] + axial_ext[:, :-2] + azim_ext[:, :, 2:] + azim_ext[:, :, :-2]
    beside = beside + radial_pad[..., 2:] + radial_pad[..., :-2]
    weighted = masks[:, None] * field[None]
    mixed = jnp.einsum("mfg,mgazr->fazr", mixing, weighted, precision=lax.Precision.HIGHEST)
    return storage * field + mixed + conductance[:, None, None, None] * (6.0 * field - beside)


def chebyshev(source, operator_fn):
    spread_ratio = center_value / half_width
    ratio_now = 1.0 / spread_ratio
    solution = jnp.zeros_like(source)
    residual = source
    direction = source / center_value
    for iteration in range(ITERS):
        solution = solution + direction
        residual = residual - operator_fn(direction)
        if iteration + 1 < ITERS:
            ratio_next = 1.0 / (2.0 * spread_ratio - ratio_now)
            direction = (
                ratio_next * ratio_now * direction + 2.0 * ratio_next / half_width * residual
            )
            ratio_now = ratio_next
    return (solution, residual)


def body(
    source,
    storage,
    materials,
    conductance,
    mixing,
    counts,
    vis_owner,
    vis_slot,
    vis_block,
    radiosity_old,
    view_blocks,
    emission,
    reflect,
):
    kinds = mixing.shape[0]
    masks = (materials[None] == jnp.arange(kinds, dtype=jnp.int32)[:, None, None, None]).astype(
        jnp.float32
    )

    def operator_step(direction):
        axial_ext = extended(direction, (("axial", 1),), 1, False)
        azim_ext = extended(direction, (("azim", 2),), 1, True)
        return combine(direction, axial_ext, azim_ext, storage, masks, mixing, conductance)

    solution, residual = chebyshev(source, operator_step)
    slot_count = vis_owner.shape[2]
    visible = vis_owner.shape[3]
    values = radiosity_old.shape[3]
    requests_total = slot_count * visible
    live_count = counts[0, 0]
    owner_flat = vis_owner.reshape(requests_total)
    slot_flat = vis_slot.reshape(requests_total)
    live = jnp.arange(requests_total, dtype=jnp.int32) < visible * live_count
    owners_total = lax.axis_size("axial")
    local_panels = radiosity_old[0, 0]
    cap_slots = requests_total // owners_total
    hits = (
        (owner_flat[:, None] == jnp.arange(owners_total, dtype=jnp.int32)[None, :]) & live[:, None]
    ).astype(jnp.int32)
    earlier = jnp.cumsum(hits, axis=0) - hits
    rank = jnp.sum(earlier * hits, axis=1)
    target = jnp.where(live, owner_flat, owners_total)
    asked = (
        jnp.full((owners_total, cap_slots), -1, jnp.int32)
        .at[target, rank]
        .set(slot_flat, mode="drop")
    )
    requested = lax.all_to_all(asked, "axial", split_axis=0, concat_axis=0, tiled=True)
    rows_out = local_panels[jnp.clip(requested, 0)]
    rows_out = jnp.where(requested[..., None] >= 0, rows_out, jnp.zeros_like(rows_out))
    returned = lax.all_to_all(rows_out, "axial", split_axis=0, concat_axis=0, tiled=True)
    flat_rows = returned.reshape(owners_total * cap_slots, values)
    picked = flat_rows[jnp.where(live, owner_flat * cap_slots + rank, 0)]
    gathered = jnp.where(live[:, None], picked.astype(jnp.float32), 0.0)
    block_types = view_blocks.shape[0]
    block_hot = (
        (
            vis_block.reshape(requests_total)[:, None]
            == jnp.arange(block_types, dtype=jnp.int32)[None, :]
        )
        & live[:, None]
    ).astype(jnp.float32)
    grouped = jnp.einsum(
        "pkb,pkr->bpr",
        block_hot.reshape(slot_count, visible, block_types),
        gathered.reshape(slot_count, visible, values),
        precision=lax.Precision.HIGHEST,
    )
    incoming = jnp.einsum(
        "bij,bpj->pi", view_blocks.astype(jnp.float32), grouped, precision=lax.Precision.HIGHEST
    )
    wall = solution[0, :, :, -1].reshape(-1)
    wall_temp = wall[jnp.arange(slot_count, dtype=jnp.int32) % wall.shape[0]]
    panel_live = jnp.arange(slot_count, dtype=jnp.int32) < live_count
    radiosity_new = jnp.where(
        panel_live[:, None], emission[0, 0] * wall_temp[:, None] + reflect[0, 0] * incoming, 0.0
    )
    return (solution, residual, radiosity_new[None, None])


def solution(mesh):
    return jax.shard_map(
        body,
        mesh=mesh,
        in_specs=(
            P(None, "axial", "azim", None),
            P(None, "axial", "azim", None),
            P("axial", "azim", None),
            P(),
            P(),
            P("axial", "azim"),
            P("axial", "azim", None, None),
            P("axial", "azim", None, None),
            P("axial", "azim", None, None),
            P("axial", "azim", None, None),
            P(),
            P("axial", "azim", None, None),
            P("axial", "azim", None, None),
        ),
        out_specs=(
            P(None, "axial", "azim", None),
            P(None, "axial", "azim", None),
            P("axial", "azim", None, None),
        ),
        check_vma=False,
    )
```

profile of v0, /device:TPU:7, one launch (start us, length us, event | category | flops | bytes accessed | tf_op | source)
XLA Modules:
  0.0 155.7 jit_solution(2506336664460121216)
XLA Ops:
  0.6 0.0 copy-start
  0.6 1.7 %copy_multiply_fusion.2 = f32[12,4,16,256]{3,0,2,1:T(8,128)S(1)} fusion(f32[12,4,16,256]{3,2,1,0:T(8,128)} %param.13), kind=kLoop, calls=%fused_computation.36 | loop fusion | flops 196608 | bytes 1572864 | tf_op jit(solution)/shard_map/div | solution.py:44
  2.3 0.0 copy-start.10
  2.4 0.0 copy-start.11
  2.4 2.2 %collective-permute-start = (f32[12,1,16,256]{3,0,2,1:T(8,128)S(1)}, f32[12,1,16,256]{3,0,2,1:T(8,128)}, u32[]{:S(2)}, u32[]{:S(2)}) collective-permute-start(f32[12,1,16,256]{3,0,2,1:T(8,128)S(1)} %get-tuple-element.25), channel_id=1, source_target_pairs={{4,0},{8,4},{12,8},{16,12},{20,16},{24,20},{28,24},{5,1},{9,5},{13... | collective-permute-start | bytes 589832 | tf_op jit(solution)/shard_map/ppermute | solution.py:23
  4.6 4.0 %collective-permute-start.1 = (f32[12,1,16,256]{3,0,2,1:T(8,128)S(1)}, f32[12,1,16,256]{3,0,2,1:T(8,128)}, u32[]{:S(2)}, u32[]{:S(2)}) collective-permute-start(f32[12,1,16,256]{3,0,2,1:T(8,128)S(1)} %get-tuple-element.26), channel_id=1, source_target_pairs={{0,4},{4,8},{8,12},{12,16},{16,20},{20,24},{24,28},{1,5},{5,9},{9,... | collective-permute-start | bytes 589832 | tf_op jit(solution)/shard_map/ppermute | solution.py:21
  8.6 1.3 collective-permute-start.2
  9.9 0.5 collective-permute-start.3
  10.4 0.1 copy.73
  10.5 0.1 eq.60
  10.7 0.1 reshape.190
  11.5 1.1 reduce-window.6
  12.6 0.2 slice_reduce_fusion.1
  12.9 0.1 add_bitcast_fusion
  13.0 0.1 copy.75
  13.1 0.1 reshape.223
  13.2 0.6 broadcast_in_dim.41
  13.8 71.8 %scatter_fusion = s32[8,60]{1,0:T(8,128)} fusion(s32[8,60]{1,0:T(8,128)} %broadcast_in_dim.41, s32[480]{0:T(512)S(1)} %bitcast.91, s32[480]{0:T(512)S(1)} %reshape.223), kind=kCustom, calls=%fused_computation.3 | custom fusion | bytes 9600 | tf_op jit(solution)/shard_map/scatter | solution.py:103
  85.7 0.0 copy-start.1
  85.7 4.9 %all-to-all-start = ((s32[8,1,60]{2,1,0:T(1,128)}), s32[8,1,60]{2,1,0:T(1,128)S(1)}, u32[]{:S(2)}, u32[]{:S(2)}) async-start(s32[8,1,60]{2,1,0:T(1,128)} %bitcast.22), calls=%async_computation | async-start | bytes 8192 | tf_op jit(solution)/shard_map/all_to_all | solution.py:105
  90.7 0.1 fusion.75
  90.8 0.1 copy.79
  90.9 3.7 %all-to-all-done = s32[8,1,60]{2,1,0:T(1,128)S(1)} async-done(((s32[8,1,60]{2,1,0:T(1,128)}), s32[8,1,60]{2,1,0:T(1,128)S(1)}, u32[]{:S(2)}, u32[]{:S(2)}) %all-to-all-start) | async-done | bytes 1952 | tf_op jit(solution)/shard_map/all_to_all | solution.py:105
  94.7 0.1 reshape.207
  94.8 1.5 gather_fusion.1
  96.3 0.8 broadcast_select_fusion
  97.1 4.5 %all-to-all-start.1 = ((bf16[8,60,128]{2,1,0:T(8,128)(2,1)}), bf16[8,60,128]{2,1,0:T(8,128)(2,1)S(1)}, u32[]{:S(2)}, u32[]{:S(2)}) async-start(bf16[8,60,128]{2,1,0:T(8,128)(2,1)} %broadcast_select_fusion), calls=%async_computation.1 | async-start | bytes 262144 | tf_op jit(solution)/shard_map/all_to_all | solution.py:108
  101.7 6.8 %fusion.52 = (f32[12,4,16,256]{3,0,2,1:T(8,128)S(1)}, f32[12,4,16,256]{3,0,2,1:T(8,128)}) fusion(f32[12,4,16,256]{3,2,1,0:T(8,128)S(1)} %copy-done.2, f32[12,4,16,256]{3,0,2,1:T(8,128)S(1)} %copy_multiply_fusion.2, f32[12,4,1,256]{3,0,2,1:T(8,128)} %collective-permute-done.3, f32[12,4,1,256]{3,0,2,1:T(8,128)S(1)} %collective-permute-done.2, ...), kind=kOutput, calls=%fused_computation.46 | convolution fusion | flops 117768192 | bytes 6038016 | tf_op jit(solution)/shard_map/mfg,mgazr->fazr/dot_general | solution.py:35
  108.5 2.0 %collective-permute-start.4 = (f32[12,1,16,256]{3,0,2,1:T(8,128)S(1)}, f32[12,1,16,256]{3,0,2,1:T(8,128)S(1)}, u32[]{:S(2)}, u32[]{:S(2)}) collective-permute-start(f32[12,1,16,256]{3,0,2,1:T(8,128)S(1)} %get-tuple-element.21), channel_id=1, source_target_pairs={{4,0},{8,4},{12,8},{16,12},{20,16},{24,20},{28,24},{5,1},{9,5},{13... | collective-permute-start | bytes 589832 | tf_op jit(solution)/shard_map/ppermute | solution.py:23
  110.6 4.2 %collective-permute-start.5 = (f32[12,1,16,256]{3,0,2,1:T(8,128)S(1)}, f32[12,1,16,256]{3,0,2,1:T(8,128)S(1)}, u32[]{:S(2)}, u32[]{:S(2)}) collective-permute-start(f32[12,1,16,256]{3,0,2,1:T(8,128)S(1)} %get-tuple-element.22), channel_id=1, source_target_pairs={{0,4},{4,8},{8,12},{12,16},{16,20},{20,24},{24,28},{1,5},{5,9},{9,... | collective-permute-start | bytes 589832 | tf_op jit(solution)/shard_map/ppermute | solution.py:21
  114.7 0.1 collective-permute-start.6
  114.8 2.6 %collective-permute-start.7 = (f32[12,4,1,256]{3,0,2,1:T(8,128)S(1)}, f32[12,4,1,256]{3,0,2,1:T(8,128)}, u32[]{:S(2)}, u32[]{:S(2)}) collective-permute-start(f32[12,4,1,256]{3,0,2,1:T(8,128)S(1)} %get-tuple-element.24), channel_id=1, source_target_pairs={{0,1},{1,2},{2,3},{3,0},{4,5},{5,6},{6,7},{7,4},{8,9},{9,10},{10,1... | collective-permute-start | bytes 147464 | tf_op jit(solution)/shard_map/ppermute | solution.py:21
  117.5 1.5 gather_fusion.2
  119.0 1.1 convolution_bitcast_fusion
  120.1 4.9 %collective-permute-done.5 = f32[12,1,16,256]{3,0,2,1:T(8,128)S(1)} collective-permute-done((f32[12,1,16,256]{3,0,2,1:T(8,128)S(1)}, f32[12,1,16,256]{3,0,2,1:T(8,128)S(1)}, u32[]{:S(2)}, u32[]{:S(2)}) %collective-permute-start.5) | collective-permute-done | bytes 196640 | tf_op jit(solution)/shard_map/ppermute | solution.py:21
  125.0 7.3 %multiply_add_fusion = (f32[12,4,16,256]{3,0,2,1:T(8,128)S(1)}, f32[12,4,16,256]{3,0,2,1:T(8,128)S(1)}, f32[12,4,16,256]{3,0,2,1:T(8,128)}) fusion(f32[12,4,16,256]{3,0,2,1:T(8,128)S(1)} %copy-done.4, f32[12,4,16,256]{3,2,1,0:T(8,128)S(1)} %copy-done.2, f32[12,4,16,256]{3,0,2,1:T(8,128)} %get-tuple-element.32, ...), kind=kOutput, calls=%fused_computation.80 | convolution fusion | flops 118358016 | bytes 7725568 | tf_op jit(solution)/shard_map/mfg,mgazr->fazr/dot_general | solution.py:35
  132.3 2.1 %collective-permute-start.8 = (f32[12,1,16,256]{3,0,2,1:T(8,128)S(1)}, f32[12,1,16,256]{3,0,2,1:T(8,128)S(1)}, u32[]{:S(2)}, u32[]{:S(2)}) collective-permute-start(f32[12,1,16,256]{3,0,2,1:T(8,128)S(1)} %get-tuple-element.17), channel_id=1, source_target_pairs={{4,0},{8,4},{12,8},{16,12},{20,16},{24,20},{28,24},{5,1},{9,5},{13... | collective-permute-start | bytes 589832 | tf_op jit(solution)/shard_map/ppermute | solution.py:23
  134.4 4.3 %collective-permute-start.9 = (f32[12,1,16,256]{3,0,2,1:T(8,128)S(1)}, f32[12,1,16,256]{3,0,2,1:T(8,128)S(1)}, u32[]{:S(2)}, u32[]{:S(2)}) collective-permute-start(f32[12,1,16,256]{3,0,2,1:T(8,128)S(1)} %get-tuple-element.18), channel_id=1, source_target_pairs={{0,4},{4,8},{8,12},{12,16},{16,20},{20,24},{24,28},{1,5},{5,9},{9,... | collective-permute-start | bytes 589832 | tf_op jit(solution)/shard_map/ppermute | solution.py:21
  138.7 1.0 collective-permute-start.10
  139.7 0.8 collective-permute-start.11
  140.5 0.5 slice_reduce_fusion
  140.9 0.1 reshape_squeeze.3
  141.0 1.2 gather_fusion
  142.3 1.1 fusion.51
  143.3 1.3 copy.81
  144.7 4.4 %collective-permute-done.9 = f32[12,1,16,256]{3,0,2,1:T(8,128)S(1)} collective-permute-done((f32[12,1,16,256]{3,0,2,1:T(8,128)S(1)}, f32[12,1,16,256]{3,0,2,1:T(8,128)S(1)}, u32[]{:S(2)}, u32[]{:S(2)}) %collective-permute-start.9) | collective-permute-done | bytes 196640 | tf_op jit(solution)/shard_map/ppermute | solution.py:21
  149.1 5.2 %fusion.45 = f32[12,4,16,256]{3,0,2,1:T(8,128)S(1)} fusion(f32[12,4,16,256]{3,0,2,1:T(8,128)} %get-tuple-element.33, f32[12,4,16,256]{3,0,2,1:T(8,128)S(1)} %copy-done.6, f32[4,4,16,256]{3,0,2,1:T(4,128)S(1)} %fusion.75, f32[12,4,16,256]{3,2,1,0:T(8,128)S(1)} %copy-done.14, f32[12,4,1,256]{3,0,2,1:T(8,128)} %collective-permute-done.11, ...), kind=kOutput, calls=%fused_computation.33 | convolution fusion | flops 117178368 | bytes 5382656 | tf_op jit(solution)/shard_map/mfg,mgazr->fazr/dot_general | solution.py:35
  154.4 1.3 copy.82
  (64 shorter events, 0.5 us)
Async XLA Ops:
  0.6 141.6 %copy-start = (bf16[8,128,128]{2,1,0:T(8,128)(2,1)S(1)}, bf16[8,128,128]{2,1,0:T(8,128)(2,1)}, u32[]{:S(2)}) copy-start(bf16[8,128,128]{2,1,0:T(8,128)(2,1)} %param.23) | copy-start | bytes 786436
  2.3 8.1 %copy-start.10 = (s32[1,1,120,4]{2,3,1,0:T(4,128)S(1)}, s32[1,1,120,4]{2,3,1,0:T(4,128)}, u32[]{:S(2)}) copy-start(s32[1,1,120,4]{2,3,1,0:T(4,128)} %param.19) | copy-start | bytes 5764
  2.4 10.6 %copy-start.11 = (s32[1,1,120,4]{2,3,1,0:T(4,128)S(1)}, s32[1,1,120,4]{2,3,1,0:T(4,128)}, u32[]{:S(2)}) copy-start(s32[1,1,120,4]{2,3,1,0:T(4,128)} %param.20) | copy-start | bytes 5764
  2.4 99.2 %collective-permute-start = (f32[12,1,16,256]{3,0,2,1:T(8,128)S(1)}, f32[12,1,16,256]{3,0,2,1:T(8,128)}, u32[]{:S(2)}, u32[]{:S(2)}) collective-permute-start(f32[12,1,16,256]{3,0,2,1:T(8,128)S(1)} %get-tuple-element.25), channel_id=1, source_target_pairs={{4,0},{8,4},{12,8},{16,12},{20,16},{24,20},{28,24},{5,1},{9,5},{13... | collective-permute-start | bytes 589832 | tf_op jit(solution)/shard_map/ppermute | solution.py:23
  4.6 97.0 %collective-permute-start.1 = (f32[12,1,16,256]{3,0,2,1:T(8,128)S(1)}, f32[12,1,16,256]{3,0,2,1:T(8,128)}, u32[]{:S(2)}, u32[]{:S(2)}) collective-permute-start(f32[12,1,16,256]{3,0,2,1:T(8,128)S(1)} %get-tuple-element.26), channel_id=1, source_target_pairs={{0,4},{4,8},{8,12},{12,16},{16,20},{20,24},{24,28},{1,5},{5,9},{9,... | collective-permute-start | bytes 589832 | tf_op jit(solution)/shard_map/ppermute | solution.py:21
  8.6 93.0 %collective-permute-start.2 = (f32[12,4,1,256]{3,0,2,1:T(8,128)S(1)}, f32[12,4,1,256]{3,0,2,1:T(8,128)S(1)}, u32[]{:S(2)}, u32[]{:S(2)}) collective-permute-start(f32[12,4,1,256]{3,0,2,1:T(8,128)S(1)} %get-tuple-element.27), channel_id=1, source_target_pairs={{1,0},{2,1},{3,2},{0,3},{5,4},{6,5},{7,6},{4,7},{9,8},{10,9},{11,1... | collective-permute-start | bytes 147464 | tf_op jit(solution)/shard_map/ppermute | solution.py:23
  9.9 91.7 %collective-permute-start.3 = (f32[12,4,1,256]{3,0,2,1:T(8,128)S(1)}, f32[12,4,1,256]{3,0,2,1:T(8,128)}, u32[]{:S(2)}, u32[]{:S(2)}) collective-permute-start(f32[12,4,1,256]{3,0,2,1:T(8,128)S(1)} %get-tuple-element.28), channel_id=1, source_target_pairs={{0,1},{1,2},{2,3},{3,0},{4,5},{5,6},{6,7},{7,4},{8,9},{9,10},{10,1... | collective-permute-start | bytes 147464 | tf_op jit(solution)/shard_map/ppermute | solution.py:21
  13.8 76.8 %copy-start.7 = (s32[4,16,256]{2,1,0:T(8,128)S(1)}, s32[4,16,256]{2,1,0:T(8,128)}, u32[]{:S(2)}) copy-start(s32[4,16,256]{2,1,0:T(8,128)} %param.15) | copy-start | bytes 196612
  13.8 77.0 %copy-start.12 = (s32[1,1,120,4]{2,3,1,0:T(4,128)S(1)}, s32[1,1,120,4]{2,3,1,0:T(4,128)}, u32[]{:S(2)}) copy-start(s32[1,1,120,4]{2,3,1,0:T(4,128)} %param.21) | copy-start | bytes 5764
  85.7 9.1 %copy-start.1 = (bf16[1,1,120,128]{3,2,1,0:T(8,128)(2,1)S(1)}, bf16[1,1,120,128]{3,2,1,0:T(8,128)(2,1)}, u32[]{:S(2)}) copy-start(bf16[1,1,120,128]{3,2,1,0:T(8,128)(2,1)} %param.22) | copy-start | bytes 92164
  85.7 9.0 %all-to-all-start = ((s32[8,1,60]{2,1,0:T(1,128)}), s32[8,1,60]{2,1,0:T(1,128)S(1)}, u32[]{:S(2)}, u32[]{:S(2)}) async-start(s32[8,1,60]{2,1,0:T(1,128)} %bitcast.22), calls=%async_computation | async-start | bytes 8192 | tf_op jit(solution)/shard_map/all_to_all | solution.py:105
  90.7 10.9 %copy-start.2 = (f32[12,4,16,256]{3,2,1,0:T(8,128)S(1)}, f32[12,4,16,256]{3,2,1,0:T(8,128)}, u32[]{:S(2)}) copy-start(f32[12,4,16,256]{3,2,1,0:T(8,128)} %param.13) | copy-start | bytes 2359300
  90.8 10.9 %copy-start.15 = (f32[4,12,12]{2,0,1:T(4,128)S(1)}, f32[4,12,12]{2,0,1:T(4,128)}, u32[]{:S(2)}) copy-start(f32[4,12,12]{2,0,1:T(4,128)} %param.17) | copy-start | bytes 6916
  90.8 10.9 %copy-start.16 = (f32[12]{0:T(128)S(1)}, f32[12]{0:T(128)}, u32[]{:S(2)}) copy-start(f32[12]{0:T(128)} %param.16) | copy-start | bytes 148
  97.1 20.3 %all-to-all-start.1 = ((bf16[8,60,128]{2,1,0:T(8,128)(2,1)}), bf16[8,60,128]{2,1,0:T(8,128)(2,1)S(1)}, u32[]{:S(2)}, u32[]{:S(2)}) async-start(bf16[8,60,128]{2,1,0:T(8,128)(2,1)} %broadcast_select_fusion), calls=%async_computation.1 | async-start | bytes 262144 | tf_op jit(solution)/shard_map/all_to_all | solution.py:108
  108.5 6.3 %copy-start.3 = (f32[12,4,16,256]{3,0,2,1:T(8,128)}, f32[12,4,16,256]{3,0,2,1:T(8,128)S(1)}, u32[]{:S(2)}) copy-start(f32[12,4,16,256]{3,0,2,1:T(8,128)S(1)} %get-tuple-element.31) | copy-start | bytes 2359300
  108.5 11.6 %collective-permute-start.4 = (f32[12,1,16,256]{3,0,2,1:T(8,128)S(1)}, f32[12,1,16,256]{3,0,2,1:T(8,128)S(1)}, u32[]{:S(2)}, u32[]{:S(2)}) collective-permute-start(f32[12,1,16,256]{3,0,2,1:T(8,128)S(1)} %get-tuple-element.21), channel_id=1, source_target_pairs={{4,0},{8,4},{12,8},{16,12},{20,16},{24,20},{28,24},{5,1},{9,5},{13... | collective-permute-start | bytes 589832 | tf_op jit(solution)/shard_map/ppermute | solution.py:23
  110.6 14.4 %collective-permute-start.5 = (f32[12,1,16,256]{3,0,2,1:T(8,128)S(1)}, f32[12,1,16,256]{3,0,2,1:T(8,128)S(1)}, u32[]{:S(2)}, u32[]{:S(2)}) collective-permute-start(f32[12,1,16,256]{3,0,2,1:T(8,128)S(1)} %get-tuple-element.22), channel_id=1, source_target_pairs={{0,4},{4,8},{8,12},{12,16},{16,20},{20,24},{24,28},{1,5},{5,9},{9,... | collective-permute-start | bytes 589832 | tf_op jit(solution)/shard_map/ppermute | solution.py:21
  114.7 5.3 %collective-permute-start.6 = (f32[12,4,1,256]{3,0,2,1:T(8,128)S(1)}, f32[12,4,1,256]{3,0,2,1:T(8,128)}, u32[]{:S(2)}, u32[]{:S(2)}) collective-permute-start(f32[12,4,1,256]{3,0,2,1:T(8,128)S(1)} %get-tuple-element.23), channel_id=1, source_target_pairs={{1,0},{2,1},{3,2},{0,3},{5,4},{6,5},{7,6},{4,7},{9,8},{10,9},{11,1... | collective-permute-start | bytes 147464 | tf_op jit(solution)/shard_map/ppermute | solution.py:23
  114.8 5.3 %collective-permute-start.7 = (f32[12,4,1,256]{3,0,2,1:T(8,128)S(1)}, f32[12,4,1,256]{3,0,2,1:T(8,128)}, u32[]{:S(2)}, u32[]{:S(2)}) collective-permute-start(f32[12,4,1,256]{3,0,2,1:T(8,128)S(1)} %get-tuple-element.24), channel_id=1, source_target_pairs={{0,1},{1,2},{2,3},{3,0},{4,5},{5,6},{6,7},{7,4},{8,9},{9,10},{10,1... | collective-permute-start | bytes 147464 | tf_op jit(solution)/shard_map/ppermute | solution.py:21
  119.0 6.0 %copy-start.4 = (f32[12,4,16,256]{3,0,2,1:T(8,128)S(1)}, f32[12,4,16,256]{3,0,2,1:T(8,128)}, u32[]{:S(2)}) copy-start(f32[12,4,16,256]{3,0,2,1:T(8,128)} %copy-done.3) | copy-start | bytes 2359300
  119.0 6.0 %copy-start.13 = (f32[12,4,16,256]{3,2,1,0:T(8,128)S(1)}, f32[12,4,16,256]{3,2,1,0:T(8,128)}, u32[]{:S(2)}) copy-start(f32[12,4,16,256]{3,2,1,0:T(8,128)} %param.14) | copy-start | bytes 2359300
  132.3 8.2 %copy-start.5 = (f32[12,4,16,256]{3,0,2,1:T(8,128)}, f32[12,4,16,256]{3,0,2,1:T(8,128)S(1)}, u32[]{:S(2)}) copy-start(f32[12,4,16,256]{3,0,2,1:T(8,128)S(1)} %get-tuple-element.15) | copy-start | bytes 2359300
  132.3 10.0 %copy-start.8 = (f32[1,1,120,128]{3,2,1,0:T(8,128)S(1)}, f32[1,1,120,128]{3,2,1,0:T(8,128)}, u32[]{:S(2)}) copy-start(f32[1,1,120,128]{3,2,1,0:T(8,128)} %param.25) | copy-start | bytes 184324
  132.3 10.0 %copy-start.9 = (f32[1,1,120,128]{3,2,1,0:T(8,128)S(1)}, f32[1,1,120,128]{3,2,1,0:T(8,128)}, u32[]{:S(2)}) copy-start(f32[1,1,120,128]{3,2,1,0:T(8,128)} %param.24) | copy-start | bytes 184324
  132.3 12.3 %collective-permute-start.8 = (f32[12,1,16,256]{3,0,2,1:T(8,128)S(1)}, f32[12,1,16,256]{3,0,2,1:T(8,128)S(1)}, u32[]{:S(2)}, u32[]{:S(2)}) collective-permute-start(f32[12,1,16,256]{3,0,2,1:T(8,128)S(1)} %get-tuple-element.17), channel_id=1, source_target_pairs={{4,0},{8,4},{12,8},{16,12},{20,16},{24,20},{28,24},{5,1},{9,5},{13... | collective-permute-start | bytes 589832 | tf_op jit(solution)/shard_map/ppermute | solution.py:23
  134.4 14.7 %collective-permute-start.9 = (f32[12,1,16,256]{3,0,2,1:T(8,128)S(1)}, f32[12,1,16,256]{3,0,2,1:T(8,128)S(1)}, u32[]{:S(2)}, u32[]{:S(2)}) collective-permute-start(f32[12,1,16,256]{3,0,2,1:T(8,128)S(1)} %get-tuple-element.18), channel_id=1, source_target_pairs={{0,4},{4,8},{8,12},{12,16},{16,20},{20,24},{24,28},{1,5},{5,9},{9,... | collective-permute-start | bytes 589832 | tf_op jit(solution)/shard_map/ppermute | solution.py:21
  138.7 6.0 %collective-permute-start.10 = (f32[12,4,1,256]{3,0,2,1:T(8,128)S(1)}, f32[12,4,1,256]{3,0,2,1:T(8,128)S(1)}, u32[]{:S(2)}, u32[]{:S(2)}) collective-permute-start(f32[12,4,1,256]{3,0,2,1:T(8,128)S(1)} %get-tuple-element.19), channel_id=1, source_target_pairs={{1,0},{2,1},{3,2},{0,3},{5,4},{6,5},{7,6},{4,7},{9,8},{10,9},{11,1... | collective-permute-start | bytes 147464 | tf_op jit(solution)/shard_map/ppermute | solution.py:23
  139.7 5.0 %collective-permute-start.11 = (f32[12,4,1,256]{3,0,2,1:T(8,128)S(1)}, f32[12,4,1,256]{3,0,2,1:T(8,128)}, u32[]{:S(2)}, u32[]{:S(2)}) collective-permute-start(f32[12,4,1,256]{3,0,2,1:T(8,128)S(1)} %get-tuple-element.20), channel_id=1, source_target_pairs={{0,1},{1,2},{2,3},{3,0},{4,5},{5,6},{6,7},{7,4},{8,9},{9,10},{10,1... | collective-permute-start | bytes 147464 | tf_op jit(solution)/shard_map/ppermute | solution.py:21
  143.3 5.8 %copy-start.6 = (f32[12,4,16,256]{3,0,2,1:T(8,128)S(1)}, f32[12,4,16,256]{3,0,2,1:T(8,128)}, u32[]{:S(2)}) copy-start(f32[12,4,16,256]{3,0,2,1:T(8,128)} %copy-done.5) | copy-start | bytes 2359300
  143.3 5.8 %copy-start.14 = (f32[12,4,16,256]{3,2,1,0:T(8,128)S(1)}, f32[12,4,16,256]{3,2,1,0:T(8,128)}, u32[]{:S(2)}) copy-start(f32[12,4,16,256]{3,2,1,0:T(8,128)} %param.14) | copy-start | bytes 2359300
where the time goes:
time: 158 us; the launch traced here: 156 us
  local copies, waits for them, and re-layouts  81.1 us (51%)
  starting transfers between devices  34.3 us (22%)
  matrix products  21.4 us (14%)
  waiting for transfers between devices  13.1 us (8%)
  other arithmetic  3.94 us (2%)
  between operations  1.74 us (1%)
    scatter x1, local copies, waits for them, and re-layouts, body(): asked = jnp.full((owners_total, cap_slots), -1, jnp.int32).at[target, ran...  71.8 us
    dot_general x3, matrix products, combine(): jnp.einsum('mfg,mgazr->fazr', mixing, weighted, precision=lax.Precision.H...  19.3 us
    ppermute x6, starting transfers between devices, extended(): lax.ppermute(tail, axis, [(i, (i + 1) % count) for i in range(ends)])  16.3 us
    ppermute x6, waiting for transfers between devices, extended(): lax.ppermute(tail, axis, [(i, (i + 1) % count) for i in range(ends)])  9.35 us
    ppermute x6, starting transfers between devices, extended(): lax.ppermute(head, axis, [((i + 1) % count, i) for i in range(ends)])  8.6 us
    all_to_all x1, starting transfers between devices, body(): lax.all_to_all(asked, 'axial', split_axis=0, concat_axis=0, tiled=True)  4.94 us
    all_to_all x1, starting transfers between devices, body(): lax.all_to_all(rows_out, 'axial', split_axis=0, concat_axis=0, tiled=True)  4.47 us
    all_to_all x1, waiting for transfers between devices, body(): lax.all_to_all(asked, 'axial', split_axis=0, concat_axis=0, tiled=True)  3.75 us
  transfers between devices with their start and end apart: 14, of which 3 were waited for; matrix products, arithmetic and copies ran while one was open for 58% of the time, Pallas kernels for 0%

commit v1 on v0

v1 whole, which is shorter than its diff:
```python
import functools
import jax
import jax.numpy as jnp
from jax import lax
from jax.experimental import pallas as pl
from jax.experimental.pallas import tpu as pltpu
from jax.sharding import PartitionSpec as P

center_value = 14.2
half_width = 13.8
sigma = center_value / half_width
ratio_0 = 1.0 / sigma
ratio_1 = 1.0 / (2.0 * sigma - ratio_0)
ratio_2 = 1.0 / (2.0 * sigma - ratio_1)
ALPHA = (None, ratio_1 * ratio_0, ratio_2 * ratio_1)
BETA = (None, 2.0 * ratio_1 / half_width, 2.0 * ratio_2 / half_width)
INV_CENTER = 1.0 / center_value

ROWS = 8
LINK = jnp.float16
f32, bf16 = jnp.float32, jnp.bfloat16

VMEM = pl.BlockSpec(memory_space=pltpu.VMEM)
SMEM = pl.BlockSpec(memory_space=pltpu.SMEM)
PARAMS = pltpu.CompilerParams(vmem_limit_bytes=24 * 1024 * 1024)


def mixed_part(cells, kinds, coef_two, coef_one):
    nf, rows, cr = cells.shape
    flat = cells.reshape(nf * rows, cr)
    high = flat.astype(bf16)
    low = (flat - high.astype(f32)).astype(bf16)
    out = jnp.dot(coef_two, jnp.concatenate([high, high], axis=0), preferred_element_type=f32)
    out = out + jnp.dot(coef_one, low, preferred_element_type=f32)
    mats = out.shape[0] // (nf * rows)
    out = out.reshape(mats, nf, rows, cr)
    picked = out[mats - 1]
    for m in range(mats - 1):
        picked = jnp.where((kinds == m)[None], out[m], picked)
    return picked


def radial_sum(cells):
    cr = cells.shape[-1]
    lane = lax.broadcasted_iota(jnp.int32, cells.shape, cells.ndim - 1)
    inner = jnp.where(lane == 0, 0.0, pltpu.roll(cells, 1, cells.ndim - 1))
    outer = jnp.where(lane == cr - 1, 0.0, pltpu.roll(cells, cr - 1, cells.ndim - 1))
    return inner + outer


def azim_sum(cells):
    rows = cells.shape[1]
    return pltpu.roll(cells, 1, 1) + pltpu.roll(cells, rows - 1, 1)


def apply_local(planes, store, kinds, cond, coef_two, coef_one, tiles, emit):
    ca = len(planes)
    for a in range(ca):
        around = azim_sum(planes[a])
        if a > 0:
            around = around + planes[a - 1]
        if a + 1 < ca:
            around = around + planes[a + 1]
        for t in tiles:
            rows = slice(t * ROWS, (t + 1) * ROWS)
            cells = planes[a][:, rows]
            beside = around[:, rows] + radial_sum(cells)
            image = store(a, t) * cells + mixed_part(cells, kinds(a, t), coef_two, coef_one)
            emit(a, t, image - cond * beside)


def first_kernel(
    even_ref, source_ref, store_ref, kinds_ref, wing_ref, wing_kinds_ref, mix_ref, cond_ref,
    rest_ref, next_ref, edge1_ref, edge0_ref, two_ref, one_ref,
):
    nf, ca, cz, cr = source_ref.shape
    own = cz // ROWS
    mixes = mix_ref[...]
    high = mixes.astype(bf16)
    low = (mixes - high.astype(f32)).astype(bf16)
    wide = mixes.shape[0] * ROWS
    inner = nf * ROWS
    row = lax.broadcasted_iota(jnp.int32, (wide, mixes.shape[0]), 0)
    col = lax.broadcasted_iota(jnp.int32, (wide, mixes.shape[0]), 1)
    down = (row // ROWS == col).astype(bf16)
    row = lax.broadcasted_iota(jnp.int32, (mixes.shape[1], inner), 0)
    col = lax.broadcasted_iota(jnp.int32, (mixes.shape[1], inner), 1)
    across = (col // ROWS == row).astype(bf16)
    row = lax.broadcasted_iota(jnp.int32, (wide, inner), 0)
    col = lax.broadcasted_iota(jnp.int32, (wide, inner), 1)
    same = row % ROWS == col % ROWS

    def spread(part):
        tall = jnp.dot(down, part, preferred_element_type=f32).astype(bf16)
        full = jnp.dot(tall, across, preferred_element_type=f32)
        return jnp.where(same, full, 0.0).astype(bf16)

    coef_one = spread(high)
    coef_two = jnp.concatenate([coef_one, spread(low)], axis=1)
    one_ref[...] = coef_one
    two_ref[...] = coef_two

    cond = cond_ref[...]
    planes = [
        jnp.concatenate([source_ref[:, a] * INV_CENTER, wing_ref[0, :, a]], axis=1)
        for a in range(ca)
    ]

    def store(a, t):
        return store_ref[:, a, t * ROWS : (t + 1) * ROWS] if t < own else wing_ref[1, :, a]

    def kinds(a, t):
        return kinds_ref[a, t * ROWS : (t + 1) * ROWS] if t < own else wing_kinds_ref[a]

    def emit(a, t, image):
        rows = slice(t * ROWS, (t + 1) * ROWS)
        direction = planes[a][:, rows]
        if t < own:
            rest = source_ref[:, a, rows] - image
        else:
            rest = center_value * direction - image
        rest_ref[:, a, rows] = rest
        next_ref[:, a, rows] = ALPHA[1] * direction + BETA[1] * rest

    apply_local(planes, store, kinds, cond, coef_two, coef_one, range(own + 1), emit)

    even = even_ref[0] == 1
    for ref, first in ((edge1_ref, True), (edge0_ref, False)):
        below, above = (0, ca - 1) if first else (ca - 1, 0)
        ref[:, :cz] = jnp.where(even, next_ref[:, below, :cz], next_ref[:, above, :cz])
        ahead = jnp.where(even, next_ref[:, below, cz:], next_ref[:, above, cz:])
        wing = jnp.where(even, wing_ref[0, :, below], wing_ref[0, :, above])
        place = lax.broadcasted_iota(jnp.int32, wing.shape, 1)
        moved = jnp.where(place < 4, pltpu.roll(wing, 2, 1), pltpu.roll(wing, 6, 1))
        ref[:, cz:] = jnp.where((place >= 2) & (place <= 5), moved, ahead)


def second_kernel(
    even_ref, rest_ref, next_ref, halo1_ref, halo0_ref, store_ref, kinds_ref, cond_ref, two_ref, one_ref,
    newrest_ref, dir_ref, newnext_ref, edge1_ref, edge0_ref,
):
    nf, ca, cz, cr = store_ref.shape
    own = cz // ROWS
    even = even_ref[0] == 1
    cond = cond_ref[...]
    wide = jnp.concatenate([cond] * own, axis=1)
    h1, h0 = halo1_ref[...], halo0_ref[...]
    low = wide * jnp.where(even, h1, h0)
    high = wide * jnp.where(even, h0, h1)
    arrived = {0: low, ca - 1: high}
    dir_ref[...] = next_ref[...]
    dir_ref[:, 0, :cz] += BETA[1] * low
    dir_ref[:, ca - 1, :cz] += BETA[1] * high
    planes = [dir_ref[:, a] for a in range(ca)]
    coef_two, coef_one = two_ref[...], one_ref[...]

    def store(a, t):
        return store_ref[:, a, t * ROWS : (t + 1) * ROWS]

    def kinds(a, t):
        return kinds_ref[a, t * ROWS : (t + 1) * ROWS]

    def emit(a, t, image):
        rows = slice(t * ROWS, (t + 1) * ROWS)
        rest = rest_ref[:, a, rows] - image
        if a in arrived:
            rest = rest + arrived[a][:, rows]
        newrest_ref[:, a, rows] = rest
        newnext_ref[:, a, rows] = ALPHA[2] * planes[a][:, rows] + BETA[2] * rest

    apply_local(planes, store, kinds, cond, coef_two, coef_one, range(own), emit)
    edge1_ref[...] = jnp.where(even, newnext_ref[:, 0], newnext_ref[:, ca - 1])
    edge0_ref[...] = jnp.where(even, newnext_ref[:, ca - 1], newnext_ref[:, 0])


def third_kernel(
    even_ref, live_ref, rest_ref, next_ref, halo1_ref, halo0_ref, dir_ref, first_rest_ref, source_ref, store_ref,
    kinds_ref, wing_ref, wing_kinds_ref, cond_ref, two_ref, one_ref, incoming_ref, emission_ref, reflect_ref,
    out_ref, solution_ref, panel_ref,
):
    nf, ca, cz, cr = source_ref.shape
    own = cz // ROWS
    even = even_ref[0] == 1
    cond = cond_ref[...]
    wide = jnp.concatenate([cond] * own, axis=1)
    h1, h0 = halo1_ref[...], halo0_ref[...]
    halo = {0: jnp.where(even, h1, h0), ca - 1: jnp.where(even, h0, h1)}
    coef_two, coef_one = two_ref[...], one_ref[...]

    place = lax.broadcasted_iota(jnp.int32, (nf, cz, cr), 1)
    rests, dirs = {}, {}
    fix = {}
    side = lax.broadcasted_iota(jnp.int32, (nf, ROWS, cr), 1)
    for a in range(ca):
        if a not in halo:
            dirs[a] = next_ref[:, a]
            continue
        old = halo[a][:, cz:]
        moved = jnp.where(side < 4, pltpu.roll(old, ROWS - 2, 1), pltpu.roll(old, 2, 1))
        fix[a] = cond * jnp.where((side <= 1) | (side >= 6), moved, 0.0)
        turned = pltpu.roll(fix[a], 1, 1)
        back = pltpu.roll(fix[a], ROWS - 1, 1)
        ends = [jnp.where(side == 0, turned, 0.0)]
        ends += [jnp.zeros_like(turned)] * (own - 2)
        ends += [jnp.where(side == ROWS - 1, back, 0.0)]
        added = wide * (halo[a][:, :cz] + BETA[1] * jnp.concatenate(ends, axis=1))
        rests[a] = added
        dirs[a] = next_ref[:, a] + BETA[2] * added

    has_partner = {0: even_ref[1] == 1, ca - 1: even_ref[2] == 1}
    second = [dir_ref[:, a] for a in range(ca)]
    for a in fix:
        second[a] = jnp.concatenate([second[a][:, :cz], second[a][:, cz:] + BETA[1] * fix[a]], axis=1)
    planes = [None] * ca

    def wing_store(a, t):
        return wing_ref[1, :, a]

    def wing_kinds(a, t):
        return wing_kinds_ref[a]

    def wing_emit(a, t, image):
        rest = first_rest_ref[:, a, cz:] - image
        if a in fix:
            beyond = halo[a][:, cz:] + BETA[1] * cond * wing_ref[0, :, a]
            rest = rest + fix[a] + jnp.where(has_partner[a], cond * beyond, 0.0)
        ahead = ALPHA[2] * second[a][:, cz:] + BETA[2] * rest
        planes[a] = jnp.concatenate([dirs[a], ahead], axis=1)

    apply_local(second, wing_store, wing_kinds, cond, coef_two, coef_one, (own,), wing_emit)

    def store(a, t):
        return store_ref[:, a, t * ROWS : (t + 1) * ROWS]

    def kinds(a, t):
        return kinds_ref[a, t * ROWS : (t + 1) * ROWS]

    def emit(a, t, image):
        rows = slice(t * ROWS, (t + 1) * ROWS)
        rest = rest_ref[:, a, rows] - image
        if a in rests:
            rest = rest + rests[a][:, rows]
        out_ref[:, a, rows] = rest
        solution_ref[:, a, rows] = (
            source_ref[:, a, rows] * INV_CENTER + dir_ref[:, a, rows] + planes[a][:, rows]
        )

    apply_local(planes, store, kinds, cond, coef_two, coef_one, range(own), emit)

    slots, values = emission_ref.shape
    wall = solution_ref[0].reshape(ca * cz, cr)[:, cr - 1 : cr]
    wall = jnp.broadcast_to(wall, (ca * cz, values))
    wall = jnp.concatenate([wall] * (-(-slots // (ca * cz))), axis=0)[:slots]
    panel = lax.broadcasted_iota(jnp.int32, (slots, values), 0)
    fresh = emission_ref[...] * wall + reflect_ref[...] * incoming_ref[...]
    panel_ref[...] = jnp.where(panel < live_ref[0], fresh, 0.0)


def last_kernel(even_ref, rest_ref, halo1_ref, halo0_ref, cond_ref, out_ref):
    nf, ca, cz, cr = rest_ref.shape
    even = even_ref[0] == 1
    wide = jnp.concatenate([cond_ref[...]] * (cz // ROWS), axis=1)
    h1, h0 = halo1_ref[...], halo0_ref[...]
    for a in range(1, ca - 1):
        out_ref[:, a] = rest_ref[:, a]
    out_ref[:, 0] = rest_ref[:, 0] + wide * jnp.where(even, h1, h0)
    out_ref[:, ca - 1] = rest_ref[:, ca - 1] + wide * jnp.where(even, h0, h1)


def panel_kernel(chunk, index_ref, block_ref, rows_ref, view_ref, out_ref):
    slots, visible = index_ref.shape
    total, values = rows_ref.shape
    index = index_ref[...]
    block = block_ref[...]
    types = view_ref.shape[0]
    lane = lax.broadcasted_iota(jnp.int32, (slots, chunk), 1)

    def gather(start):
        rows = rows_ref[pl.ds(start, chunk), :]
        return tuple(
            jnp.dot(
                (index[:, k : k + 1] == lane + start).astype(f32).astype(bf16),
                rows,
                preferred_element_type=f32,
            )
            for k in range(visible)
        )

    if total == chunk:
        found = gather(0)
    else:
        zero = tuple(jnp.zeros((slots, values), f32) for _ in range(visible))

        def step(i, sums):
            return tuple(s + g for s, g in zip(sums, gather(pl.multiple_of(i * chunk, chunk))))

        found = lax.fori_loop(0, total // chunk, step, zero)
    out = jnp.zeros((slots, values), f32)
    for b in range(types):
        stack = jnp.concatenate(
            [jnp.where(block[:, k : k + 1] == b, found[k], 0.0) for k in range(visible)], axis=0
        ).astype(bf16)
        moved = lax.dot_general(
            stack, view_ref[b], (((1,), (1,)), ((), ())), preferred_element_type=f32
        )
        for k in range(visible):
            out = out + moved[k * slots : (k + 1) * slots]
    out_ref[...] = out


def pairs(count, first, closed):
    swaps = []
    for i in range(first, count if closed and first else count - 1, 2):
        j = (i + 1) % count
        swaps += [(i, j), (j, i)]
    return swaps


def swap(array, axis, first, closed=False):
    return lax.ppermute(array, axis, pairs(lax.axis_size(axis), first, closed))


def body(
    source, storage, materials, conductance, mixing, counts, vis_owner, vis_slot, vis_block,
    radiosity_old, view_blocks, emission, reflect,
):
    nf, ca, cz, cr = source.shape
    mats = mixing.shape[0]
    owners = lax.axis_size("axial")
    me = lax.axis_index("axial")
    is_even = me % 2 == 0
    even = jnp.stack([is_even, me > 0, me + 1 < owners]).astype(jnp.int32)
    azim_even = lax.axis_index("azim") % 2 == 0
    shape = jax.ShapeDtypeStruct
    call = functools.partial(pl.pallas_call, compiler_params=PARAMS)

    half = ROWS // 2
    bundle = jnp.concatenate(
        [source * INV_CENTER, storage, materials[None].astype(f32)], axis=0
    )
    to_right = bundle[:, :, cz - half :].astype(LINK)
    to_left = bundle[:, :, :half].astype(LINK)
    near = jnp.where(azim_even, to_right, to_left)
    far = jnp.where(azim_even, to_left, to_right)
    far_in = swap(far, "azim", 1, True)
    layer_low, layer_high = source[:, 0] * INV_CENTER, source[:, ca - 1] * INV_CENTER
    halo1 = swap(jnp.where(is_even, layer_low, layer_high).astype(LINK), "axial", 1)
    near_in = swap(near, "azim", 0)
    halo0 = swap(jnp.where(is_even, layer_high, layer_low).astype(LINK), "axial", 0)
    from_right = jnp.where(azim_even, near_in, far_in)
    from_left = jnp.where(azim_even, far_in, near_in)
    wings = jnp.concatenate([from_right, from_left], axis=2).astype(f32)
    wing = wings[: 2 * nf].reshape(2, nf, ca, ROWS, cr)
    wing_kinds = wings[2 * nf].astype(jnp.int32)

    cond = jnp.broadcast_to(conductance[:, None, None], (nf, ROWS, cr))
    mixes = mixing + 6.0 * jnp.diag(conductance)
    mixes = jnp.pad(mixes.reshape(mats * nf, nf), ((0, 0), (0, 128 - nf)))
    full = shape((nf, ca, cz + ROWS, cr), f32)
    plain = shape((nf, ca, cz, cr), f32)
    tall = shape((nf, cz + ROWS, cr), f32)
    layer = shape((nf, cz, cr), f32)
    rest, ahead, edge1, edge0, two, one = call(
        first_kernel,
        out_shape=(
            full, full, tall, tall,
            shape((mats * nf * ROWS, 2 * nf * ROWS), bf16), shape((mats * nf * ROWS, nf * ROWS), bf16),
        ),
        in_specs=[SMEM] + [VMEM] * 7,
        out_specs=(VMEM,) * 6,
    )(even, source, storage, materials, wing, wing_kinds, mixes, cond)

    wide = conductance[:, None, None]

    def grown(edge, halo):
        return (edge + jnp.pad(BETA[1] * wide * halo, ((0, 0), (0, ROWS), (0, 0)))).astype(LINK)

    halo1, halo0 = halo1.astype(f32), halo0.astype(f32)
    second1 = swap(grown(edge1, halo1), "axial", 1).astype(f32)
    second0 = swap(grown(edge0, halo0), "axial", 0).astype(f32)

    slots, visible = vis_owner.shape[2:]
    values = radiosity_old.shape[3]
    tile = -(-slots // 16) * 16
    panels = jnp.pad(radiosity_old[0, 0], ((0, tile - slots), (0, 0)))
    if owners & (owners - 1) == 0:
        step = 1
        while step < owners:
            other = lax.ppermute(panels, "axial", [(i, i ^ step) for i in range(owners)])
            panels = jnp.concatenate([panels, other], axis=0)
            step *= 2
        owner = vis_owner[0, 0] ^ me
    else:
        panels = lax.all_gather(panels, "axial", axis=0, tiled=True)
        owner = vis_owner[0, 0]
    live_count = counts[0]
    index = owner * tile + vis_slot[0, 0]
    chunk = tile * 8 if owners % 8 == 0 else tile * owners
    incoming = call(
        functools.partial(panel_kernel, chunk),
        out_shape=shape((slots, values), f32),
        in_specs=[VMEM] * 4,
        out_specs=VMEM,
    )(index, vis_block[0, 0], panels, view_blocks)

    rest2, dir2, ahead2, edge1, edge0 = call(
        second_kernel,
        out_shape=(plain, full, plain, layer, layer),
        in_specs=[SMEM] + [VMEM] * 9,
        out_specs=(VMEM,) * 5,
    )(even, rest, ahead, halo1, halo0, storage, materials, cond, two, one)

    def grown_again(edge, halo):
        old = BETA[1] * wide * halo[:, cz:]
        zero = jnp.zeros((nf, cz - 2, cr), f32)
        ends = jnp.concatenate([old[:, 5:6], zero, old[:, 2:3]], axis=1)
        return (edge + BETA[2] * wide * (halo[:, :cz] + ends)).astype(LINK)

    third1 = swap(grown_again(edge1, second1), "axial", 1).astype(f32)
    third0 = swap(grown_again(edge0, second0), "axial", 0).astype(f32)

    rest3, solution_out, panel_new = call(
        third_kernel,
        out_shape=(plain, plain, shape((slots, values), f32)),
        in_specs=[SMEM] * 2 + [VMEM] * 17,
        out_specs=(VMEM,) * 3,
    )(
        even, live_count, rest2, ahead2, second1, second0, dir2, rest, source, storage, materials,
        wing, wing_kinds, cond, two, one, incoming, emission[0, 0], reflect[0, 0],
    )
    residual = call(
        last_kernel,
        out_shape=plain,
        in_specs=[SMEM] + [VMEM] * 4,
        out_specs=VMEM,
    )(even, rest3, third1, third0, cond)
    return (solution_out, residual, panel_new[None, None])


def solution(mesh):
    return jax.shard_map(
        body,
        mesh=mesh,
        in_specs=(
            P(None, "axial", "azim", None),
            P(None, "axial", "azim", None),
            P("axial", "azim", None),
            P(),
            P(),
            P("axial", "azim"),
            P("axial", "azim", None, None),
            P("axial", "azim", None, None),
            P("axial", "azim", None, None),
            P("axial", "azim", None, None),
            P(),
            P("axial", "azim", None, None),
            P("axial", "azim", None, None),
        ),
        out_specs=(
            P(None, "axial", "azim", None),
            P(None, "axial", "azim", None),
            P("axial", "azim", None, None),
        ),
        check_vma=False,
    )
```

time: 158 us -> 58.3 us (0.37)
  the two profiles are of different devices: /device:TPU:7 before, /device:TPU:0 now
where the time goes in v1:
time: 58.3 us; the launch traced here: 57.7 us
  starting transfers between devices  20.9 us (36%)
  Pallas kernels  11.2 us (19%)
  local copies, waits for them, and re-layouts  10.7 us (18%)
  other arithmetic  10.7 us (18%)
  waiting for transfers between devices  2.54 us (4%)
  between operations  1.78 us (3%)
    ppermute x8, starting transfers between devices, swap(): return lax.ppermute(array, axis, pairs(lax.axis_size(axis), first, closed))  15.1 us
    unnamed x73, local copies, waits for them, and re-layouts  10.4 us
    ppermute x3, starting transfers between devices, body(): lax.ppermute(panels, 'axial', [(i, i ^ step) for i in range(owners)])  5.73 us
    pallas_call x1, Pallas kernels, body(): call(third_kernel, out_shape=(plain, plain, shape((slots, values), f32)),...  3.77 us
    pallas_call x1, Pallas kernels, body(): call(first_kernel, out_shape=(full, full, tall, tall, shape((mats * nf *...  2.96 us
    ppermute x3, waiting for transfers between devices, body(): lax.ppermute(panels, 'axial', [(i, i ^ step) for i in range(owners)])  2.52 us
    concatenate x3, other arithmetic, body(): panels = jnp.concatenate([panels, other], axis=0)  2.35 us
    pallas_call x1, Pallas kernels, body(): call(second_kernel, out_shape=(plain, full, plain, layer, layer), in_spec...  2.04 us
  transfers between devices with their start and end apart: 11, of which 1 were waited for; matrix products, arithmetic and copies ran while one was open for 20% of the time, Pallas kernels for 17%

profile of v1, /device:TPU:0, one launch (start us, length us, event | category | flops | bytes accessed | tf_op | source)
XLA Modules:
  0.0 57.7 jit_solution(17911716338932608448)
XLA Ops:
  0.7 1.3 %broadcast_multiply_fusion = f32[12,4,16,256]{3,2,1,0:T(8,128)S(1)} fusion(f32[12,4,16,256]{3,2,1,0:T(8,128)} %source_ref.3), kind=kLoop, calls=%fused_computation.5 | loop fusion | flops 196608 | bytes 1572864 | tf_op jit(solution)/shard_map/mul | solution.py:339
  2.0 0.2 broadcast_select_fusion.3
  2.3 0.1 broadcast_select_fusion.2
  2.4 2.5 %collective-permute-start.1 = (f16[25,4,4,256]{3,2,1,0:T(4,128)(2,1)S(1)}, f16[25,4,4,256]{3,2,1,0:T(4,128)(2,1)S(1)}, u32[]{:S(2)}, u32[]{:S(2)}) collective-permute-start(f16[25,4,4,256]{3,2,1,0:T(4,128)(2,1)S(1)} %bitcast.61), channel_id=1, source_target_pairs={{1,2},{2,1},{3,0},{0,3},{5,6},{6,5},{7,4},{4,7},{9,10},{10,9},{11,... | collective-permute-start | bytes 614408 | tf_op jit(solution)/shard_map/ppermute | solution.py:320
  4.9 0.7 %collective-permute-start = (f16[25,4,4,256]{3,2,1,0:T(4,128)(2,1)S(1)}, f16[25,4,4,256]{3,2,1,0:T(4,128)(2,1)S(1)}, u32[]{:S(2)}, u32[]{:S(2)}) collective-permute-start(f16[25,4,4,256]{3,2,1,0:T(4,128)(2,1)S(1)} %get-tuple-element.31), channel_id=1, source_target_pairs={{0,1},{1,0},{2,3},{3,2},{4,5},{5,4},{6,7},{7,6},{8,9},{9,8},{10,11... | collective-permute-start | bytes 614408 | tf_op jit(solution)/shard_map/ppermute | solution.py:320
  5.6 0.7 %collective-permute-start.2 = (f16[12,16,256]{2,1,0:T(8,128)(2,1)S(1)}, f16[12,16,256]{2,1,0:T(8,128)(2,1)S(1)}, u32[]{:S(2)}, u32[]{:S(2)}) collective-permute-start(f16[12,16,256]{2,1,0:T(8,128)(2,1)S(1)} %get-tuple-element.35), channel_id=1, source_target_pairs={{4,8},{8,4},{12,16},{16,12},{20,24},{24,20},{5,9},{9,5},{13,17},{1... | collective-permute-start | bytes 294920 | tf_op jit(solution)/shard_map/ppermute | solution.py:320
  6.3 4.3 %collective-permute-start.3 = (f16[12,16,256]{2,1,0:T(8,128)(2,1)S(1)}, f16[12,16,256]{2,1,0:T(8,128)(2,1)S(1)}, u32[]{:S(2)}, u32[]{:S(2)}) collective-permute-start(f16[12,16,256]{2,1,0:T(8,128)(2,1)S(1)} %get-tuple-element.34), channel_id=1, source_target_pairs={{0,4},{4,0},{8,12},{12,8},{16,20},{20,16},{24,28},{28,24},{1,5},{5... | collective-permute-start | bytes 294920 | tf_op jit(solution)/shard_map/ppermute | solution.py:320
  10.7 0.1 collective-permute-start.6
  11.0 0.7 %copy.33 = s32[1,1,120,4]{3,2,1,0:T(8,128)} copy(s32[1,1,120,4]{2,3,1,0:T(4,128)S(1)} %copy-done.32) | data formatting | bytes 3840 | tf_op args[6]
  11.7 0.7 %copy.35 = s32[1,1,120,4]{3,2,1,0:T(8,128)} copy(s32[1,1,120,4]{2,3,1,0:T(4,128)S(1)} %copy-done.33) | data formatting | bytes 3840 | tf_op args[7]
  12.4 2.5 %collective-permute-done.6 = bf16[128,128]{1,0:T(8,128)(2,1)S(1)} collective-permute-done((bf16[128,128]{1,0:T(8,128)(2,1)S(1)}, bf16[128,128]{1,0:T(8,128)(2,1)S(1)}, u32[]{:S(2)}, u32[]{:S(2)}) %collective-permute-start.6) | collective-permute-done | bytes 32800 | tf_op jit(solution)/shard_map/ppermute | solution.py:389
  15.0 0.6 %pad_maximum_fusion.4 = bf16[256,128]{1,0:T(8,128)(2,1)} fusion(bf16[128,128]{1,0:T(8,128)(2,1)S(1)} %collective-permute-done.6, bf16[128,128]{1,0:T(8,128)(2,1)S(1)} %pad.18), kind=kLoop, calls=%fused_computation.32 | loop fusion | flops 131072 | bytes 131072 | tf_op jit(solution)/shard_map/concatenate | solution.py:390
  15.6 2.6 %collective-permute-start.7 = (bf16[256,128]{1,0:T(8,128)(2,1)}, bf16[256,128]{1,0:T(8,128)(2,1)}, u32[]{:S(2)}, u32[]{:S(2)}) collective-permute-start(bf16[256,128]{1,0:T(8,128)(2,1)} %pad_maximum_fusion.4), channel_id=1, source_target_pairs={{0,8},{4,12},{8,0},{12,4},{16,24},{20,28},{24,16},{28,20},{1,9},{5... | collective-permute-start | bytes 196616 | tf_op jit(solution)/shard_map/ppermute | solution.py:389
  18.2 0.1 broadcast_multiply_fusion.1
  18.3 0.1 broadcast_select_fusion.1
  18.5 0.3 copy-done.23
  18.9 0.2 maximum_convert_fusion.1
  19.2 0.2 copy-done.14
  19.4 0.3 copy-done.8
  19.7 3.0 %shard_map.148 = (f32[12,4,24,256]{3,2,1,0:T(8,128)S(1)}, f32[12,4,24,256]{3,2,1,0:T(8,128)S(1)}, f32[12,24,256]{2,1,0:T(8,128)S(1)}, f32[12,24,256]{2,1,0:T(8,1...) custom-call(s32[3]{0:T(128)S(1)} %add_convert_fusion.2.even_ref, f32[12,4,16,256]{3,2,1,0:T(8,128)S(1)} %copy-done.1, ...), custom_call_target="tpu_custom_call" | custom-call | tf_op jit(solution)/shard_map/pallas_call | solution.py:363
  22.7 1.1 %copy-done.5 = f32[12,4,24,256]{3,2,1,0:T(8,128)} copy-done((f32[12,4,24,256]{3,2,1,0:T(8,128)}, f32[12,4,24,256]{3,2,1,0:T(8,128)S(1)}, u32[]{:S(2)}) %copy-start.5) | copy-done | bytes 1179672
  23.8 0.7 %copy-done.10 = bf16[384,192]{1,0:T(8,128)(2,1)} copy-done((bf16[384,192]{1,0:T(8,128)(2,1)}, bf16[384,192]{1,0:T(8,128)(2,1)S(1)}, u32[]{:S(2)}) %copy-start.10) | copy-done | bytes 147480
  24.4 0.6 %copy-done.12 = bf16[384,96]{1,0:T(8,128)(2,1)} copy-done((bf16[384,96]{1,0:T(8,128)(2,1)}, bf16[384,96]{1,0:T(8,128)(2,1)S(1)}, u32[]{:S(2)}) %copy-start.12) | copy-done | bytes 73752
  25.1 0.7 %add_convert_fusion.1 = f16[12,24,256]{2,1,0:T(8,128)(2,1)} fusion(f32[12,24,256]{2,1,0:T(8,128)S(1)} %get-tuple-element.23, f32[12,16,256]{2,1,0:T(8,128)S(1)} %get-tuple-element.49), kind=kLoop, calls=%fused_computation.7 | loop fusion | flops 147456 | bytes 638976 | tf_op jit(solution)/shard_map/convert_element_type | solution.py:376
  25.8 1.3 %collective-permute-start.4 = (f16[12,24,256]{2,1,0:T(8,128)(2,1)}, f16[12,24,256]{2,1,0:T(8,128)(2,1)}, u32[]{:S(2)}, u32[]{:S(2)}) collective-permute-start(f16[12,24,256]{2,1,0:T(8,128)(2,1)} %add_convert_fusion.1), channel_id=1, source_target_pairs={{4,8},{8,4},{12,16},{16,12},{20,24},{24,20},{5,9},{9,5},{13,17},{1... | collective-permute-start | bytes 442376 | tf_op jit(solution)/shard_map/ppermute | solution.py:320
  27.1 0.7 %add_convert_fusion = f16[12,24,256]{2,1,0:T(8,128)(2,1)} fusion(f32[12,24,256]{2,1,0:T(8,128)S(1)} %get-tuple-element.24, f32[12,16,256]{2,1,0:T(8,128)S(1)} %get-tuple-element.48), kind=kLoop, calls=%fused_computation.6 | loop fusion | flops 147456 | bytes 638976 | tf_op jit(solution)/shard_map/convert_element_type | solution.py:376
  27.8 2.1 %collective-permute-start.5 = (f16[12,24,256]{2,1,0:T(8,128)(2,1)}, f16[12,24,256]{2,1,0:T(8,128)(2,1)}, u32[]{:S(2)}, u32[]{:S(2)}) collective-permute-start(f16[12,24,256]{2,1,0:T(8,128)(2,1)} %add_convert_fusion), channel_id=1, source_target_pairs={{0,4},{4,0},{8,12},{12,8},{16,20},{20,16},{24,28},{28,24},{1,5},{5... | collective-permute-start | bytes 442376 | tf_op jit(solution)/shard_map/ppermute | solution.py:320
  29.9 0.6 %add_bitcast_fusion.index_ref = s32[120,4]{1,0:T(8,128)} fusion(s32[1,1,120,4]{3,2,1,0:T(8,128)S(1)} %copy-done.28, s32[1,1,120,4]{3,2,1,0:T(8,128)S(1)} %copy-done.27, s32[]{:T(128)S(6)} %axis_index.23), kind=kLoop, calls=%fused_computation.34 | loop fusion | flops 1440 | bytes 5764 | tf_op jit(solution)/shard_map/add | solution.py:397
  30.5 0.7 %copy.36 = s32[1,1,120,4]{3,2,1,0:T(8,128)} copy(s32[1,1,120,4]{2,3,1,0:T(4,128)S(1)} %copy-done.34) | data formatting | bytes 3840 | tf_op args[8]
  32.0 0.9 %pad_maximum_fusion.3 = bf16[512,128]{1,0:T(8,128)(2,1)S(1)} fusion(bf16[256,128]{1,0:T(8,128)(2,1)} %collective-permute-done.7, bf16[128,128]{1,0:T(8,128)(2,1)} %copy-done.25, bf16[128,128]{1,0:T(8,128)(2,1)} %copy-done.21), kind=kLoop, calls=%fused_computation.25 | loop fusion | flops 393216 | bytes 262144 | tf_op jit(solution)/shard_map/concatenate | solution.py:390
  32.8 3.1 %collective-permute-start.8 = (bf16[512,128]{1,0:T(8,128)(2,1)S(1)}, bf16[512,128]{1,0:T(8,128)(2,1)S(1)}, u32[]{:S(2)}, u32[]{:S(2)}) collective-permute-start(bf16[512,128]{1,0:T(8,128)(2,1)S(1)} %pad_maximum_fusion.3), channel_id=1, source_target_pairs={{0,16},{4,20},{8,24},{12,28},{16,0},{20,4},{24,8},{28,12},{1,17},{... | collective-permute-start | bytes 393224 | tf_op jit(solution)/shard_map/ppermute | solution.py:389
  35.9 0.9 %convert_element_type.76.halo1_ref = f32[12,16,256]{2,1,0:T(8,128)S(1)} convert(f16[12,16,256]{2,1,0:T(8,128)(2,1)} %copy-done.23) | non-fusion elementwise | flops 49152 | bytes 294912 | tf_op jit(solution)/shard_map/convert_element_type | solution.py:378
  36.8 0.9 %convert_element_type.79.halo0_ref = f32[12,16,256]{2,1,0:T(8,128)S(1)} convert(f16[12,16,256]{2,1,0:T(8,128)(2,1)} %copy-done.24) | non-fusion elementwise | flops 49152 | bytes 294912 | tf_op jit(solution)/shard_map/convert_element_type | solution.py:378
  37.7 0.9 %copy-done.3 = f32[12,8,256]{2,1,0:T(8,128)S(1)} copy-done((f32[12,8,256]{2,1,0:T(8,128)S(1)}, f32[12,8,256]{2,1,0:T(8,128)}, u32[]{:S(2)}) %copy-start.3) | copy-done | bytes 98328
  38.6 1.3 %copy-done.6 = f32[12,4,24,256]{3,2,1,0:T(8,128)S(1)} copy-done((f32[12,4,24,256]{3,2,1,0:T(8,128)S(1)}, f32[12,4,24,256]{3,2,1,0:T(8,128)}, u32[]{:S(2)}) %copy-start.6) | copy-done | bytes 1179672
  39.9 0.8 %copy-done.9 = s32[4,16,256]{2,1,0:T(8,128)S(1)} copy-done((s32[4,16,256]{2,1,0:T(8,128)S(1)}, s32[4,16,256]{2,1,0:T(8,128)}, u32[]{:S(2)}) %copy-start.9) | copy-done | bytes 65560
  40.7 0.9 %copy-done.11 = bf16[384,192]{1,0:T(8,128)(2,1)S(1)} copy-done((bf16[384,192]{1,0:T(8,128)(2,1)S(1)}, bf16[384,192]{1,0:T(8,128)(2,1)}, u32[]{:S(2)}) %copy-start.11) | copy-done | bytes 147480
  41.7 0.9 %copy-done.13 = bf16[384,96]{1,0:T(8,128)(2,1)S(1)} copy-done((bf16[384,96]{1,0:T(8,128)(2,1)S(1)}, bf16[384,96]{1,0:T(8,128)(2,1)}, u32[]{:S(2)}) %copy-start.13) | copy-done | bytes 73752
  42.5 2.0 %shard_map.149 = (f32[12,4,16,256]{3,2,1,0:T(8,128)S(1)}, f32[12,4,24,256]{3,2,1,0:T(8,128)S(1)}, f32[12,4,16,256]{3,2,1,0:T(8,128)S(1)}, f32[12,16,256]{2,1,0:T(8,128)S(1)}, f32[12,16,256]{2,1,0:T(8,128)S(1)}) custom-call(s32[3]{0:T(128)S(1)} %add_convert_fusion.2.even_ref, f32[12,4,24,256]{3,2,1,0:T(8,128)S(1)} %get-tuple-element.17.rest_ref.first_rest_ref, ...), custom_call_target="tpu_custom_call" | custom-call | tf_op jit(solution)/shard_map/pallas_call | solution.py:406
  44.6 0.9 %convert_element_type.81.halo1_ref = f32[12,24,256]{2,1,0:T(8,128)S(1)} convert(f16[12,24,256]{2,1,0:T(8,128)(2,1)} %collective-permute-done.4) | non-fusion elementwise | flops 73728 | bytes 442368 | tf_op jit(solution)/shard_map/convert_element_type | solution.py:379
  45.6 1.0 %convert_element_type.83.halo0_ref = f32[12,24,256]{2,1,0:T(8,128)S(1)} convert(f16[12,24,256]{2,1,0:T(8,128)(2,1)} %collective-permute-done.5) | non-fusion elementwise | flops 73728 | bytes 442368 | tf_op jit(solution)/shard_map/convert_element_type | solution.py:380
  46.8 0.2 fusion.3
  46.9 0.7 %collective-permute-start.9 = (f16[12,16,256]{2,1,0:T(8,128)(2,1)S(1)}, f16[12,16,256]{2,1,0:T(8,128)(2,1)S(1)}, u32[]{:S(2)}, u32[]{:S(2)}) collective-permute-start(f16[12,16,256]{2,1,0:T(8,128)(2,1)S(1)} %get-tuple-element.43), channel_id=1, source_target_pairs={{4,8},{8,4},{12,16},{16,12},{20,24},{24,20},{5,9},{9,5},{13,17},{1... | collective-permute-start | bytes 294920 | tf_op jit(solution)/shard_map/ppermute | solution.py:320
  47.6 2.9 %collective-permute-start.10 = (f16[12,16,256]{2,1,0:T(8,128)(2,1)S(1)}, f16[12,16,256]{2,1,0:T(8,128)(2,1)S(1)}, u32[]{:S(2)}, u32[]{:S(2)}) collective-permute-start(f16[12,16,256]{2,1,0:T(8,128)(2,1)S(1)} %get-tuple-element.42), channel_id=1, source_target_pairs={{0,4},{4,0},{8,12},{12,8},{16,20},{20,16},{24,28},{28,24},{1,5},{5... | collective-permute-start | bytes 294920 | tf_op jit(solution)/shard_map/ppermute | solution.py:320
  50.5 0.9 %pad_maximum_fusion.2.rows_ref = bf16[1024,128]{1,0:T(8,128)(2,1)S(1)} fusion(bf16[512,128]{1,0:T(8,128)(2,1)S(1)} %collective-permute-done.8, bf16[256,128]{1,0:T(8,128)(2,1)} %collective-permute-done.7, bf16[128,128]{1,0:T(8,128)(2,1)S(1)} %copy-done.26, bf16[128,128]{1,0:T(8,128)(2,1)S(1)} %copy-done.22), kind=kLoop, calls=%fused_computation.8 | loop fusion | flops 1048576 | bytes 524288 | tf_op jit(solution)/shard_map/concatenate | solution.py:390
  51.4 0.9 %shard_map.150.incoming_ref = f32[120,128]{1,0:T(8,128)S(1)} custom-call(s32[120,4]{1,0:T(8,128)S(1)} %copy-done.17, s32[120,4]{1,0:T(8,128)S(1)} %bitcast.50, bf16[1024,128]{1,0:T(8,128)(2,1)S(1)} %pad_maximum_fusion.2.rows_ref, bf16[8,128,128]{2,1,0:T(8,128)(2,1)S(1)} %copy-done.16), custom_call_target="tpu_custom_call" | custom-call | tf_op jit(solution)/shard_map/pallas_call | solution.py:399
  52.3 3.8 %shard_map.151 = (f32[12,4,16,256]{3,2,1,0:T(8,128)S(1)}, f32[12,4,16,256]{3,2,1,0:T(8,128)}, f32[120,128]{1,0:T(8,128)}) custom-call(s32[3]{0:T(128)S(1)} %add_convert_fusion.2.even_ref, s32[1]{0:T(128)} %bitcast.47.live_ref, f32[12,4,16,256]{3,2,1,0:T(8,128)S(1)} %get-tuple-element.21.rest_ref, f32[12,4,16,256]{3,2,1,0:T(8,128)S(1)} %get-tuple-element.22.next_ref, ...), custom_call_target="tpu_custom_call" | custom-call | tf_op jit(solution)/shard_map/pallas_call | solution.py:422
  56.2 1.5 %shard_map.152 = f32[12,4,16,256]{3,2,1,0:T(8,128)} custom-call(s32[3]{0:T(128)S(1)} %add_convert_fusion.2.even_ref, f32[12,4,16,256]{3,2,1,0:T(8,128)S(1)} %get-tuple-element.27.rest_ref, f32[12,16,256]{2,1,0:T(8,128)S(1)} %convert_element_type.85.halo1_ref, f32[12,16,256]{2,1,0:T(8,128)S(1)} %convert_element_type.87.halo0_ref, f32[12,8,256]{2,1,0:T(8,128)S(1)} %copy-done.4), custom_call_target="tpu_custom_call" | custom-call | tf_op jit(solution)/shard_map/pallas_call | solution.py:431
  (88 shorter events, 0.9 us)
Async XLA Ops:
  0.6 1.3 %copy-start.7 = (s32[4,16,256]{2,1,0:T(8,128)S(1)}, s32[4,16,256]{2,1,0:T(8,128)}, u32[]{:S(2)}) copy-start(s32[4,16,256]{2,1,0:T(8,128)} %kinds_ref.5) | copy-start | bytes 196612
  0.6 1.4 %copy-start = (f32[12,4,16,256]{3,2,1,0:T(8,128)S(1)}, f32[12,4,16,256]{3,2,1,0:T(8,128)}, u32[]{:S(2)}) copy-start(f32[12,4,16,256]{3,2,1,0:T(8,128)} %store_ref.5) | copy-start | bytes 2359300
  2.0 3.5 %copy-start.1 = (f32[12,4,16,256]{3,2,1,0:T(8,128)S(1)}, f32[12,4,16,256]{3,2,1,0:T(8,128)}, u32[]{:S(2)}) copy-start(f32[12,4,16,256]{3,2,1,0:T(8,128)} %source_ref.3) | copy-start | bytes 2359300
  2.3 8.4 %copy-start.29 = (bf16[1,1,120,128]{3,2,1,0:T(8,128)(2,1)S(1)}, bf16[1,1,120,128]{3,2,1,0:T(8,128)(2,1)}, u32[]{:S(2)}) copy-start(bf16[1,1,120,128]{3,2,1,0:T(8,128)(2,1)} %param.22) | copy-start | bytes 92164
  2.3 8.5 %copy-start.31 = (f32[12]{0:T(128)S(1)}, f32[12]{0:T(128)}, u32[]{:S(2)}) copy-start(f32[12]{0:T(128)} %param.16) | copy-start | bytes 148
  2.3 8.5 %copy-start.30 = (f32[4,12,12]{2,0,1:T(4,128)S(1)}, f32[4,12,12]{2,0,1:T(4,128)}, u32[]{:S(2)}) copy-start(f32[4,12,12]{2,0,1:T(4,128)} %param.17) | copy-start | bytes 6916
  2.3 8.6 %copy-start.32 = (s32[1,1,120,4]{2,3,1,0:T(4,128)S(1)}, s32[1,1,120,4]{2,3,1,0:T(4,128)}, u32[]{:S(2)}) copy-start(s32[1,1,120,4]{2,3,1,0:T(4,128)} %param.19) | copy-start | bytes 5764
  2.3 9.4 %copy-start.33 = (s32[1,1,120,4]{2,3,1,0:T(4,128)S(1)}, s32[1,1,120,4]{2,3,1,0:T(4,128)}, u32[]{:S(2)}) copy-start(s32[1,1,120,4]{2,3,1,0:T(4,128)} %param.20) | copy-start | bytes 5764
  2.4 15.9 %collective-permute-start.1 = (f16[25,4,4,256]{3,2,1,0:T(4,128)(2,1)S(1)}, f16[25,4,4,256]{3,2,1,0:T(4,128)(2,1)S(1)}, u32[]{:S(2)}, u32[]{:S(2)}) collective-permute-start(f16[25,4,4,256]{3,2,1,0:T(4,128)(2,1)S(1)} %bitcast.61), channel_id=1, source_target_pairs={{1,2},{2,1},{3,0},{0,3},{5,6},{6,5},{7,4},{4,7},{9,10},{10,9},{11,... | collective-permute-start | bytes 614408 | tf_op jit(solution)/shard_map/ppermute | solution.py:320
  4.9 13.4 %collective-permute-start = (f16[25,4,4,256]{3,2,1,0:T(4,128)(2,1)S(1)}, f16[25,4,4,256]{3,2,1,0:T(4,128)(2,1)S(1)}, u32[]{:S(2)}, u32[]{:S(2)}) collective-permute-start(f16[25,4,4,256]{3,2,1,0:T(4,128)(2,1)S(1)} %get-tuple-element.31), channel_id=1, source_target_pairs={{0,1},{1,0},{2,3},{3,2},{4,5},{5,4},{6,7},{7,6},{8,9},{9,8},{10,11... | collective-permute-start | bytes 614408 | tf_op jit(solution)/shard_map/ppermute | solution.py:320
  5.6 12.5 %collective-permute-start.2 = (f16[12,16,256]{2,1,0:T(8,128)(2,1)S(1)}, f16[12,16,256]{2,1,0:T(8,128)(2,1)S(1)}, u32[]{:S(2)}, u32[]{:S(2)}) collective-permute-start(f16[12,16,256]{2,1,0:T(8,128)(2,1)S(1)} %get-tuple-element.35), channel_id=1, source_target_pairs={{4,8},{8,4},{12,16},{16,12},{20,24},{24,20},{5,9},{9,5},{13,17},{1... | collective-permute-start | bytes 294920 | tf_op jit(solution)/shard_map/ppermute | solution.py:320
  6.3 11.9 %collective-permute-start.3 = (f16[12,16,256]{2,1,0:T(8,128)(2,1)S(1)}, f16[12,16,256]{2,1,0:T(8,128)(2,1)S(1)}, u32[]{:S(2)}, u32[]{:S(2)}) collective-permute-start(f16[12,16,256]{2,1,0:T(8,128)(2,1)S(1)} %get-tuple-element.34), channel_id=1, source_target_pairs={{0,4},{4,0},{8,12},{12,8},{16,20},{20,16},{24,28},{28,24},{1,5},{5... | collective-permute-start | bytes 294920 | tf_op jit(solution)/shard_map/ppermute | solution.py:320
  10.7 7.8 %copy-start.21 = (bf16[128,128]{1,0:T(8,128)(2,1)}, bf16[128,128]{1,0:T(8,128)(2,1)S(1)}, u32[]{:S(2)}) copy-start(bf16[128,128]{1,0:T(8,128)(2,1)S(1)} %pad.18) | copy-start | bytes 98308
  10.7 4.3 %collective-permute-start.6 = (bf16[128,128]{1,0:T(8,128)(2,1)S(1)}, bf16[128,128]{1,0:T(8,128)(2,1)S(1)}, u32[]{:S(2)}, u32[]{:S(2)}) collective-permute-start(bf16[128,128]{1,0:T(8,128)(2,1)S(1)} %pad.18), channel_id=1, source_target_pairs={{0,4},{4,0},{8,12},{12,8},{16,20},{20,16},{24,28},{28,24},{1,5},{5... | collective-permute-start | bytes 98312 | tf_op jit(solution)/shard_map/ppermute | solution.py:389
  15.0 3.5 %copy-start.25 = (bf16[128,128]{1,0:T(8,128)(2,1)}, bf16[128,128]{1,0:T(8,128)(2,1)S(1)}, u32[]{:S(2)}) copy-start(bf16[128,128]{1,0:T(8,128)(2,1)S(1)} %collective-permute-done.6) | copy-start | bytes 98308
  15.6 16.4 %collective-permute-start.7 = (bf16[256,128]{1,0:T(8,128)(2,1)}, bf16[256,128]{1,0:T(8,128)(2,1)}, u32[]{:S(2)}, u32[]{:S(2)}) collective-permute-start(bf16[256,128]{1,0:T(8,128)(2,1)} %pad_maximum_fusion.4), channel_id=1, source_target_pairs={{0,8},{4,12},{8,0},{12,4},{16,24},{20,28},{24,16},{28,20},{1,9},{5... | collective-permute-start | bytes 196616 | tf_op jit(solution)/shard_map/ppermute | solution.py:389
  18.2 0.6 %copy-start.23 = (f16[12,16,256]{2,1,0:T(8,128)(2,1)}, f16[12,16,256]{2,1,0:T(8,128)(2,1)S(1)}, u32[]{:S(2)}) copy-start(f16[12,16,256]{2,1,0:T(8,128)(2,1)S(1)} %collective-permute-done.2) | copy-start | bytes 294916
  18.2 0.7 %copy-start.24 = (f16[12,16,256]{2,1,0:T(8,128)(2,1)}, f16[12,16,256]{2,1,0:T(8,128)(2,1)S(1)}, u32[]{:S(2)}) copy-start(f16[12,16,256]{2,1,0:T(8,128)(2,1)S(1)} %collective-permute-done.3) | copy-start | bytes 294916
  18.8 0.6 %copy-start.14 = (s32[4,8,256]{2,1,0:T(8,128)}, s32[4,8,256]{2,1,0:T(8,128)S(1)}, u32[]{:S(2)}) copy-start(s32[4,8,256]{2,1,0:T(8,128)S(1)} %fusion.9.wing_kinds_ref) | copy-start | bytes 98308
  18.8 0.9 %copy-start.8 = (s32[4,16,256]{2,1,0:T(8,128)S(1)}, s32[4,16,256]{2,1,0:T(8,128)}, u32[]{:S(2)}) copy-start(s32[4,16,256]{2,1,0:T(8,128)} %kinds_ref.5) | copy-start | bytes 196612
  19.7 3.0 %copy-start.2 = (f32[12,8,256]{2,1,0:T(8,128)}, f32[12,8,256]{2,1,0:T(8,128)S(1)}, u32[]{:S(2)}) copy-start(f32[12,8,256]{2,1,0:T(8,128)S(1)} %broadcast_in_dim.32.cond_ref) | copy-start | bytes 294916
  22.7 1.1 %copy-start.5 = (f32[12,4,24,256]{3,2,1,0:T(8,128)}, f32[12,4,24,256]{3,2,1,0:T(8,128)S(1)}, u32[]{:S(2)}) copy-start(f32[12,4,24,256]{3,2,1,0:T(8,128)S(1)} %get-tuple-element.18.next_ref) | copy-start | bytes 3538948
  23.8 0.7 %copy-start.10 = (bf16[384,192]{1,0:T(8,128)(2,1)}, bf16[384,192]{1,0:T(8,128)(2,1)S(1)}, u32[]{:S(2)}) copy-start(bf16[384,192]{1,0:T(8,128)(2,1)S(1)} %get-tuple-element.19.two_ref) | copy-start | bytes 442372
  24.4 0.6 %copy-start.12 = (bf16[384,96]{1,0:T(8,128)(2,1)}, bf16[384,96]{1,0:T(8,128)(2,1)S(1)}, u32[]{:S(2)}) copy-start(bf16[384,96]{1,0:T(8,128)(2,1)S(1)} %get-tuple-element.20.one_ref) | copy-start | bytes 221188
  25.1 4.8 %copy-start.27 = (s32[1,1,120,4]{3,2,1,0:T(8,128)S(1)}, s32[1,1,120,4]{3,2,1,0:T(8,128)}, u32[]{:S(2)}) copy-start(s32[1,1,120,4]{3,2,1,0:T(8,128)} %copy.33) | copy-start | bytes 5764
  25.1 4.8 %copy-start.28 = (s32[1,1,120,4]{3,2,1,0:T(8,128)S(1)}, s32[1,1,120,4]{3,2,1,0:T(8,128)}, u32[]{:S(2)}) copy-start(s32[1,1,120,4]{3,2,1,0:T(8,128)} %copy.35) | copy-start | bytes 5764
  25.1 5.4 %copy-start.34 = (s32[1,1,120,4]{2,3,1,0:T(4,128)S(1)}, s32[1,1,120,4]{2,3,1,0:T(4,128)}, u32[]{:S(2)}) copy-start(s32[1,1,120,4]{2,3,1,0:T(4,128)} %param.21) | copy-start | bytes 5764
  25.8 18.9 %collective-permute-start.4 = (f16[12,24,256]{2,1,0:T(8,128)(2,1)}, f16[12,24,256]{2,1,0:T(8,128)(2,1)}, u32[]{:S(2)}, u32[]{:S(2)}) collective-permute-start(f16[12,24,256]{2,1,0:T(8,128)(2,1)} %add_convert_fusion.1), channel_id=1, source_target_pairs={{4,8},{8,4},{12,16},{16,12},{20,24},{24,20},{5,9},{9,5},{13,17},{1... | collective-permute-start | bytes 442376 | tf_op jit(solution)/shard_map/ppermute | solution.py:320
  27.8 17.8 %collective-permute-start.5 = (f16[12,24,256]{2,1,0:T(8,128)(2,1)}, f16[12,24,256]{2,1,0:T(8,128)(2,1)}, u32[]{:S(2)}, u32[]{:S(2)}) collective-permute-start(f16[12,24,256]{2,1,0:T(8,128)(2,1)} %add_convert_fusion), channel_id=1, source_target_pairs={{0,4},{4,0},{8,12},{12,8},{16,20},{20,16},{24,28},{28,24},{1,5},{5... | collective-permute-start | bytes 442376 | tf_op jit(solution)/shard_map/ppermute | solution.py:320
  32.8 17.7 %collective-permute-start.8 = (bf16[512,128]{1,0:T(8,128)(2,1)S(1)}, bf16[512,128]{1,0:T(8,128)(2,1)S(1)}, u32[]{:S(2)}, u32[]{:S(2)}) collective-permute-start(bf16[512,128]{1,0:T(8,128)(2,1)S(1)} %pad_maximum_fusion.3), channel_id=1, source_target_pairs={{0,16},{4,20},{8,24},{12,28},{16,0},{20,4},{24,8},{28,12},{1,17},{... | collective-permute-start | bytes 393224 | tf_op jit(solution)/shard_map/ppermute | solution.py:389
  37.7 0.9 %copy-start.3 = (f32[12,8,256]{2,1,0:T(8,128)S(1)}, f32[12,8,256]{2,1,0:T(8,128)}, u32[]{:S(2)}) copy-start(f32[12,8,256]{2,1,0:T(8,128)} %copy-done.2) | copy-start | bytes 294916
  38.6 1.3 %copy-start.6 = (f32[12,4,24,256]{3,2,1,0:T(8,128)S(1)}, f32[12,4,24,256]{3,2,1,0:T(8,128)}, u32[]{:S(2)}) copy-start(f32[12,4,24,256]{3,2,1,0:T(8,128)} %copy-done.5) | copy-start | bytes 3538948
  39.9 0.8 %copy-start.9 = (s32[4,16,256]{2,1,0:T(8,128)S(1)}, s32[4,16,256]{2,1,0:T(8,128)}, u32[]{:S(2)}) copy-start(s32[4,16,256]{2,1,0:T(8,128)} %kinds_ref.5) | copy-start | bytes 196612
  40.7 0.9 %copy-start.11 = (bf16[384,192]{1,0:T(8,128)(2,1)S(1)}, bf16[384,192]{1,0:T(8,128)(2,1)}, u32[]{:S(2)}) copy-start(bf16[384,192]{1,0:T(8,128)(2,1)} %copy-done.10) | copy-start | bytes 442372
  41.7 0.9 %copy-start.13 = (bf16[384,96]{1,0:T(8,128)(2,1)S(1)}, bf16[384,96]{1,0:T(8,128)(2,1)}, u32[]{:S(2)}) copy-start(bf16[384,96]{1,0:T(8,128)(2,1)} %copy-done.12) | copy-start | bytes 221188
  44.6 5.9 %copy-start.22 = (bf16[128,128]{1,0:T(8,128)(2,1)S(1)}, bf16[128,128]{1,0:T(8,128)(2,1)}, u32[]{:S(2)}) copy-start(bf16[128,128]{1,0:T(8,128)(2,1)} %copy-done.21) | copy-start | bytes 98308
  44.6 5.9 %copy-start.26 = (bf16[128,128]{1,0:T(8,128)(2,1)S(1)}, bf16[128,128]{1,0:T(8,128)(2,1)}, u32[]{:S(2)}) copy-start(bf16[128,128]{1,0:T(8,128)(2,1)} %copy-done.25) | copy-start | bytes 98308
  45.6 5.8 %copy-start.16 = (bf16[8,128,128]{2,1,0:T(8,128)(2,1)S(1)}, bf16[8,128,128]{2,1,0:T(8,128)(2,1)}, u32[]{:S(2)}) copy-start(bf16[8,128,128]{2,1,0:T(8,128)(2,1)} %view_ref.1) | copy-start | bytes 786436
  45.6 5.8 %copy-start.17 = (s32[120,4]{1,0:T(8,128)S(1)}, s32[120,4]{1,0:T(8,128)}, u32[]{:S(2)}) copy-start(s32[120,4]{1,0:T(8,128)} %add_bitcast_fusion.index_ref) | copy-start | bytes 5764
  45.6 5.8 %copy-start.18 = (s32[1,1,120,4]{3,2,1,0:T(8,128)S(1)}, s32[1,1,120,4]{3,2,1,0:T(8,128)}, u32[]{:S(2)}) copy-start(s32[1,1,120,4]{3,2,1,0:T(8,128)} %copy.36) | copy-start | bytes 5764
  46.7 5.6 %copy-start.4 = (f32[12,8,256]{2,1,0:T(8,128)S(1)}, f32[12,8,256]{2,1,0:T(8,128)}, u32[]{:S(2)}) copy-start(f32[12,8,256]{2,1,0:T(8,128)} %copy-done.2) | copy-start | bytes 294916
  46.7 5.6 %copy-start.15 = (s32[4,8,256]{2,1,0:T(8,128)S(1)}, s32[4,8,256]{2,1,0:T(8,128)}, u32[]{:S(2)}) copy-start(s32[4,8,256]{2,1,0:T(8,128)} %copy-done.14) | copy-start | bytes 98308
  46.7 5.6 %copy-start.19 = (f32[1,1,120,128]{3,2,1,0:T(8,128)S(1)}, f32[1,1,120,128]{3,2,1,0:T(8,128)}, u32[]{:S(2)}) copy-start(f32[1,1,120,128]{3,2,1,0:T(8,128)} %param.24) | copy-start | bytes 184324
  46.7 5.6 %copy-start.20 = (f32[1,1,120,128]{3,2,1,0:T(8,128)S(1)}, f32[1,1,120,128]{3,2,1,0:T(8,128)}, u32[]{:S(2)}) copy-start(f32[1,1,120,128]{3,2,1,0:T(8,128)} %param.25) | copy-start | bytes 184324
  46.9 9.2 %collective-permute-start.9 = (f16[12,16,256]{2,1,0:T(8,128)(2,1)S(1)}, f16[12,16,256]{2,1,0:T(8,128)(2,1)S(1)}, u32[]{:S(2)}, u32[]{:S(2)}) collective-permute-start(f16[12,16,256]{2,1,0:T(8,128)(2,1)S(1)} %get-tuple-element.43), channel_id=1, source_target_pairs={{4,8},{8,4},{12,16},{16,12},{20,24},{24,20},{5,9},{9,5},{13,17},{1... | collective-permute-start | bytes 294920 | tf_op jit(solution)/shard_map/ppermute | solution.py:320
  47.6 8.5 %collective-permute-start.10 = (f16[12,16,256]{2,1,0:T(8,128)(2,1)S(1)}, f16[12,16,256]{2,1,0:T(8,128)(2,1)S(1)}, u32[]{:S(2)}, u32[]{:S(2)}) collective-permute-start(f16[12,16,256]{2,1,0:T(8,128)(2,1)S(1)} %get-tuple-element.42), channel_id=1, source_target_pairs={{0,4},{4,0},{8,12},{12,8},{16,20},{20,16},{24,28},{28,24},{1,5},{5... | collective-permute-start | bytes 294920 | tf_op jit(solution)/shard_map/ppermute | solution.py:320

commit v2 on v1

--- a/solution.py
+++ b/solution.py
@@ -18,11 +18,12 @@
 
 ROWS = 8
 LINK = jnp.float16
+RAD_SCALE = 8192.0
 f32, bf16 = jnp.float32, jnp.bfloat16
 
 VMEM = pl.BlockSpec(memory_space=pltpu.VMEM)
 SMEM = pl.BlockSpec(memory_space=pltpu.SMEM)
-PARAMS = pltpu.CompilerParams(vmem_limit_bytes=24 * 1024 * 1024)
+PARAMS = pltpu.CompilerParams(vmem_limit_bytes=16 * 1024 * 1024)
 
 
 def mixed_part(cells, kinds, coef_two, coef_one):
@@ -71,7 +72,7 @@
 
 def first_kernel(
     even_ref, source_ref, store_ref, kinds_ref, wing_ref, wing_kinds_ref, mix_ref, cond_ref,
-    rest_ref, next_ref, edge1_ref, edge0_ref, two_ref, one_ref,
+    rest_ref, edge_ref, two_ref, one_ref,
 ):
     nf, ca, cz, cr = source_ref.shape
     own = cz // ROWS
@@ -112,6 +113,9 @@
     def kinds(a, t):
         return kinds_ref[a, t * ROWS : (t + 1) * ROWS] if t < own else wing_kinds_ref[a]
 
+    slot = {0: 1 - even_ref[0], ca - 1: even_ref[0]}
+    place = lax.broadcasted_iota(jnp.int32, (nf, ROWS, cr), 1)
+
     def emit(a, t, image):
         rows = slice(t * ROWS, (t + 1) * ROWS)
         direction = planes[a][:, rows]
@@ -120,24 +124,19 @@
         else:
             rest = center_value * direction - image
         rest_ref[:, a, rows] = rest
-        next_ref[:, a, rows] = ALPHA[1] * direction + BETA[1] * rest
+        if a in slot:
+            ahead = ALPHA[1] * direction + BETA[1] * rest
+            if t == own:
+                moved = jnp.where(place < 4, pltpu.roll(direction, 2, 1), pltpu.roll(direction, 6, 1))
+                ahead = jnp.where((place >= 2) & (place <= 5), moved, ahead)
+            edge_ref[slot[a], :, rows] = ahead
 
     apply_local(planes, store, kinds, cond, coef_two, coef_one, range(own + 1), emit)
 
-    even = even_ref[0] == 1
-    for ref, first in ((edge1_ref, True), (edge0_ref, False)):
-        below, above = (0, ca - 1) if first else (ca - 1, 0)
-        ref[:, :cz] = jnp.where(even, next_ref[:, below, :cz], next_ref[:, above, :cz])
-        ahead = jnp.where(even, next_ref[:, below, cz:], next_ref[:, above, cz:])
-        wing = jnp.where(even, wing_ref[0, :, below], wing_ref[0, :, above])
-        place = lax.broadcasted_iota(jnp.int32, wing.shape, 1)
-        moved = jnp.where(place < 4, pltpu.roll(wing, 2, 1), pltpu.roll(wing, 6, 1))
-        ref[:, cz:] = jnp.where((place >= 2) & (place <= 5), moved, ahead)
-
 
 def second_kernel(
-    even_ref, rest_ref, next_ref, halo1_ref, halo0_ref, store_ref, kinds_ref, cond_ref, two_ref, one_ref,
-    newrest_ref, dir_ref, newnext_ref, edge1_ref, edge0_ref,
+    even_ref, rest_ref, halo1_ref, halo0_ref, source_ref, store_ref, kinds_ref, wing_ref, cond_ref, two_ref, one_ref,
+    newrest_ref, dir_ref, edge_ref,
 ):
     nf, ca, cz, cr = store_ref.shape
     own = cz // ROWS
@@ -145,14 +144,16 @@
     cond = cond_ref[...]
     wide = jnp.concatenate([cond] * own, axis=1)
     h1, h0 = halo1_ref[...], halo0_ref[...]
-    low = wide * jnp.where(even, h1, h0)
-    high = wide * jnp.where(even, h0, h1)
-    arrived = {0: low, ca - 1: high}
-    dir_ref[...] = next_ref[...]
-    dir_ref[:, 0, :cz] += BETA[1] * low
-    dir_ref[:, ca - 1, :cz] += BETA[1] * high
+    arrived = {0: wide * jnp.where(even, h1, h0), ca - 1: wide * jnp.where(even, h0, h1)}
+    for a in range(ca):
+        rest = rest_ref[:, a, :cz]
+        if a in arrived:
+            rest = rest + arrived[a]
+        dir_ref[:, a, :cz] = (ALPHA[1] * INV_CENTER) * source_ref[:, a] + BETA[1] * rest
+        dir_ref[:, a, cz:] = ALPHA[1] * wing_ref[0, :, a] + BETA[1] * rest_ref[:, a, cz:]
     planes = [dir_ref[:, a] for a in range(ca)]
     coef_two, coef_one = two_ref[...], one_ref[...]
+    slot = {0: 1 - even_ref[0], ca - 1: even_ref[0]}
 
     def store(a, t):
         return store_ref[:, a, t * ROWS : (t + 1) * ROWS]
@@ -166,15 +167,14 @@
         if a in arrived:
             rest = rest + arrived[a][:, rows]
         newrest_ref[:, a, rows] = rest
-        newnext_ref[:, a, rows] = ALPHA[2] * planes[a][:, rows] + BETA[2] * rest
+        if a in slot:
+            edge_ref[slot[a], :, rows] = ALPHA[2] * planes[a][:, rows] + BETA[2] * rest
 
     apply_local(planes, store, kinds, cond, coef_two, coef_one, range(own), emit)
-    edge1_ref[...] = jnp.where(even, newnext_ref[:, 0], newnext_ref[:, ca - 1])
-    edge0_ref[...] = jnp.where(even, newnext_ref[:, ca - 1], newnext_ref[:, 0])
 
 
 def third_kernel(
-    even_ref, live_ref, rest_ref, next_ref, halo1_ref, halo0_ref, dir_ref, first_rest_ref, source_ref, store_ref,
+    even_ref, live_ref, rest_ref, halo1_ref, halo0_ref, dir_ref, first_rest_ref, source_ref, store_ref,
     kinds_ref, wing_ref, wing_kinds_ref, cond_ref, two_ref, one_ref, incoming_ref, emission_ref, reflect_ref,
     out_ref, solution_ref, panel_ref,
 ):
@@ -192,8 +192,9 @@
     fix = {}
     side = lax.broadcasted_iota(jnp.int32, (nf, ROWS, cr), 1)
     for a in range(ca):
+        ahead = ALPHA[2] * dir_ref[:, a, :cz] + BETA[2] * rest_ref[:, a]
         if a not in halo:
-            dirs[a] = next_ref[:, a]
+            dirs[a] = ahead
             continue
         old = halo[a][:, cz:]
         moved = jnp.where(side < 4, pltpu.roll(old, ROWS - 2, 1), pltpu.roll(old, 2, 1))
@@ -205,7 +206,7 @@
         ends += [jnp.where(side == ROWS - 1, back, 0.0)]
         added = wide * (halo[a][:, :cz] + BETA[1] * jnp.concatenate(ends, axis=1))
         rests[a] = added
-        dirs[a] = next_ref[:, a] + BETA[2] * added
+        dirs[a] = ahead + BETA[2] * added
 
     has_partner = {0: even_ref[1] == 1, ca - 1: even_ref[2] == 1}
     second = [dir_ref[:, a] for a in range(ca)]
@@ -224,8 +225,8 @@
         if a in fix:
             beyond = halo[a][:, cz:] + BETA[1] * cond * wing_ref[0, :, a]
             rest = rest + fix[a] + jnp.where(has_partner[a], cond * beyond, 0.0)
-        ahead = ALPHA[2] * second[a][:, cz:] + BETA[2] * rest
-        planes[a] = jnp.concatenate([dirs[a], ahead], axis=1)
+        beside = ALPHA[2] * second[a][:, cz:] + BETA[2] * rest
+        planes[a] = jnp.concatenate([dirs[a], beside], axis=1)
 
     apply_local(second, wing_store, wing_kinds, cond, coef_two, coef_one, (own,), wing_emit)
 
@@ -252,7 +253,7 @@
     wall = jnp.broadcast_to(wall, (ca * cz, values))
     wall = jnp.concatenate([wall] * (-(-slots // (ca * cz))), axis=0)[:slots]
     panel = lax.broadcasted_iota(jnp.int32, (slots, values), 0)
-    fresh = emission_ref[...] * wall + reflect_ref[...] * incoming_ref[...]
+    fresh = emission_ref[...] * wall + reflect_ref[...] * incoming_ref[:slots]
     panel_ref[...] = jnp.where(panel < live_ref[0], fresh, 0.0)
 
 
@@ -267,11 +268,11 @@
     out_ref[:, ca - 1] = rest_ref[:, ca - 1] + wide * jnp.where(even, h0, h1)
 
 
-def panel_kernel(chunk, index_ref, block_ref, rows_ref, view_ref, out_ref):
-    slots, visible = index_ref.shape
+def panel_kernel(chunk, visible, index_ref, block_ref, rows_ref, view_ref, out_ref):
+    slots = index_ref.shape[1]
     total, values = rows_ref.shape
-    index = index_ref[...]
-    block = block_ref[...]
+    index = index_ref[...].T
+    block = block_ref[...].T
     types = view_ref.shape[0]
     lane = lax.broadcasted_iota(jnp.int32, (slots, chunk), 1)
 
@@ -331,22 +332,36 @@
     is_even = me % 2 == 0
     even = jnp.stack([is_even, me > 0, me + 1 < owners]).astype(jnp.int32)
     azim_even = lax.axis_index("azim") % 2 == 0
-    shape = jax.ShapeDtypeStruct
+    near_memory = functools.partial(pltpu.with_memory_space_constraint, memory_space=pltpu.VMEM)
     call = functools.partial(pl.pallas_call, compiler_params=PARAMS)
 
     half = ROWS // 2
-    bundle = jnp.concatenate(
-        [source * INV_CENTER, storage, materials[None].astype(f32)], axis=0
-    )
-    to_right = bundle[:, :, cz - half :].astype(LINK)
-    to_left = bundle[:, :, :half].astype(LINK)
-    near = jnp.where(azim_even, to_right, to_left)
-    far = jnp.where(azim_even, to_left, to_right)
-    far_in = swap(far, "azim", 1, True)
+
+    def columns(right):
+        def cut(array):
+            return jnp.where(right, array[..., cz - half :, :], array[..., :half, :])
+
+        kinds = cut(materials)[None].astype(f32)
+        return jnp.concatenate([cut(source) * INV_CENTER, cut(storage), kinds], axis=0).astype(LINK)
+
+    far_in = swap(columns(~azim_even), "azim", 1, True)
     layer_low, layer_high = source[:, 0] * INV_CENTER, source[:, ca - 1] * INV_CENTER
     halo1 = swap(jnp.where(is_even, layer_low, layer_high).astype(LINK), "axial", 1)
-    near_in = swap(near, "azim", 0)
-    halo0 = swap(jnp.where(is_even, layer_high, layer_low).astype(LINK), "axial", 0)
+    near_in = swap(columns(azim_even), "azim", 0)
+
+    slots, visible = vis_owner.shape[2:]
+    values = radiosity_old.shape[3]
+    tile = -(-slots // 16) * 16
+    panels = jnp.pad(radiosity_old[0, 0], ((0, tile - slots), (0, 0)))
+    fold = cr // values
+    folded = panels.astype(f32) * RAD_SCALE
+    folded = jnp.concatenate(jnp.split(folded, fold, axis=0), axis=1)
+    layer0 = jnp.where(is_even, layer_high, layer_low).reshape(nf * cz, cr)
+    message = swap(jnp.concatenate([layer0, folded], axis=0).astype(LINK), "axial", 0)
+    halo0 = message[: nf * cz].reshape(nf, cz, cr)
+    partner = message[nf * cz :].astype(f32) * (1.0 / RAD_SCALE)
+    partner = jnp.concatenate(jnp.split(partner, fold, axis=1), axis=0).astype(bf16)
+
     from_right = jnp.where(azim_even, near_in, far_in)
     from_left = jnp.where(azim_even, far_in, near_in)
     wings = jnp.concatenate([from_right, from_left], axis=2).astype(f32)
@@ -356,18 +371,15 @@
     cond = jnp.broadcast_to(conductance[:, None, None], (nf, ROWS, cr))
     mixes = mixing + 6.0 * jnp.diag(conductance)
     mixes = jnp.pad(mixes.reshape(mats * nf, nf), ((0, 0), (0, 128 - nf)))
-    full = shape((nf, ca, cz + ROWS, cr), f32)
-    plain = shape((nf, ca, cz, cr), f32)
-    tall = shape((nf, cz + ROWS, cr), f32)
-    layer = shape((nf, cz, cr), f32)
-    rest, ahead, edge1, edge0, two, one = call(
+    here = pltpu.VMEM
+    rest, edges, two, one = call(
         first_kernel,
         out_shape=(
-            full, full, tall, tall,
-            shape((mats * nf * ROWS, 2 * nf * ROWS), bf16), shape((mats * nf * ROWS, nf * ROWS), bf16),
+            here((nf, ca, cz + ROWS, cr), f32), here((2, nf, cz + ROWS, cr), f32),
+            here((mats * nf * ROWS, 2 * nf * ROWS), bf16), here((mats * nf * ROWS, nf * ROWS), bf16),
         ),
         in_specs=[SMEM] + [VMEM] * 7,
-        out_specs=(VMEM,) * 6,
+        out_specs=(VMEM,) * 4,
     )(even, source, storage, materials, wing, wing_kinds, mixes, cond)
 
     wide = conductance[:, None, None]
@@ -376,39 +388,43 @@
         return (edge + jnp.pad(BETA[1] * wide * halo, ((0, 0), (0, ROWS), (0, 0)))).astype(LINK)
 
     halo1, halo0 = halo1.astype(f32), halo0.astype(f32)
-    second1 = swap(grown(edge1, halo1), "axial", 1).astype(f32)
-    second0 = swap(grown(edge0, halo0), "axial", 0).astype(f32)
-
-    slots, visible = vis_owner.shape[2:]
-    values = radiosity_old.shape[3]
-    tile = -(-slots // 16) * 16
-    panels = jnp.pad(radiosity_old[0, 0], ((0, tile - slots), (0, 0)))
+    second1 = swap(grown(edges[0], halo1), "axial", 1).astype(f32)
+    second0 = swap(grown(edges[1], halo0), "axial", 0).astype(f32)
+
     if owners & (owners - 1) == 0:
-        step = 1
+        panels = jnp.concatenate([panels, partner], axis=0)
+        step = 2
         while step < owners:
             other = lax.ppermute(panels, "axial", [(i, i ^ step) for i in range(owners)])
             panels = jnp.concatenate([panels, other], axis=0)
             step *= 2
-        owner = vis_owner[0, 0] ^ me
+        owner = vis_owner[0, 0].T ^ me
     else:
-        panels = lax.all_gather(panels, "axial", axis=0, tiled=True)
-        owner = vis_owner[0, 0]
+        pair = jnp.stack([panels, partner])
+        panels = jnp.where(is_even, pair, pair[::-1]).reshape(2 * tile, values)
+        groups = [list(range(k, owners, 2)) for k in range(2)]
+        panels = lax.all_gather(panels, "axial", axis=0, tiled=True, axis_index_groups=groups)
+        owner = vis_owner[0, 0].T
     live_count = counts[0]
-    index = owner * tile + vis_slot[0, 0]
+    pad = ((0, -visible % ROWS), (0, -slots % 128))
+    index = jnp.pad(owner * tile + vis_slot[0, 0].T, pad, constant_values=-1)
+    block = jnp.pad(vis_block[0, 0].T, pad)
     chunk = tile * 8 if owners % 8 == 0 else tile * owners
     incoming = call(
-        functools.partial(panel_kernel, chunk),
-        out_shape=shape((slots, values), f32),
+        functools.partial(panel_kernel, chunk, visible),
+        out_shape=here((index.shape[1], values), f32),
         in_specs=[VMEM] * 4,
         out_specs=VMEM,
-    )(index, vis_block[0, 0], panels, view_blocks)
-
-    rest2, dir2, ahead2, edge1, edge0 = call(
+    )(index, block, panels, view_blocks)
+
+    rest2, dir2, edges = call(
         second_kernel,
-        out_shape=(plain, full, plain, layer, layer),
-        in_specs=[SMEM] + [VMEM] * 9,
-        out_specs=(VMEM,) * 5,
-    )(even, rest, ahead, halo1, halo0, storage, materials, cond, two, one)
+        out_shape=(
+            here((nf, ca, cz, cr), f32), here((nf, ca, cz + ROWS, cr), f32), here((2, nf, cz, cr), f32),
+        ),
+        in_specs=[SMEM] + [VMEM] * 10,
+        out_specs=(VMEM,) * 3,
+    )(even, rest, halo1, halo0, source, storage, materials, wing, cond, two, one)
 
     def grown_again(edge, halo):
         old = BETA[1] * wide * halo[:, cz:]
@@ -416,16 +432,17 @@
         ends = jnp.concatenate([old[:, 5:6], zero, old[:, 2:3]], axis=1)
         return (edge + BETA[2] * wide * (halo[:, :cz] + ends)).astype(LINK)
 
-    third1 = swap(grown_again(edge1, second1), "axial", 1).astype(f32)
-    third0 = swap(grown_again(edge0, second0), "axial", 0).astype(f32)
-
+    third1 = swap(grown_again(edges[0], second1), "axial", 1).astype(f32)
+    third0 = swap(grown_again(edges[1], second0), "axial", 0).astype(f32)
+
+    plain = jax.ShapeDtypeStruct((nf, ca, cz, cr), f32)
     rest3, solution_out, panel_new = call(
         third_kernel,
-        out_shape=(plain, plain, shape((slots, values), f32)),
-        in_specs=[SMEM] * 2 + [VMEM] * 17,
+        out_shape=(here(plain.shape, f32), plain, jax.ShapeDtypeStruct((slots, values), f32)),
+        in_specs=[SMEM] * 2 + [VMEM] * 16,
         out_specs=(VMEM,) * 3,
     )(
-        even, live_count, rest2, ahead2, second1, second0, dir2, rest, source, storage, materials,
+        even, live_count, rest2, second1, second0, dir2, rest, source, storage, materials,
         wing, wing_kinds, cond, two, one, incoming, emission[0, 0], reflect[0, 0],
     )
     residual = call(

time: 58.3 us -> 42.9 us (0.74)
  the two profiles are of different devices: /device:TPU:0 before, /device:TPU:24 now
where the time goes in v2:
time: 42.9 us; the launch traced here: 42.7 us
  starting transfers between devices  19.7 us (46%)
  Pallas kernels  11.4 us (27%)
  waiting for transfers between devices  4.64 us (11%)
  other arithmetic  3.91 us (9%)
  between operations  1.84 us (4%)
  local copies, waits for them, and re-layouts  1.22 us (3%)
    ppermute x8, starting transfers between devices, swap(): return lax.ppermute(array, axis, pairs(lax.axis_size(axis), first, closed))  14.7 us
    ppermute x2, starting transfers between devices, body(): lax.ppermute(panels, 'axial', [(i, i ^ step) for i in range(owners)])  5 us
    ppermute x8, waiting for transfers between devices, swap(): return lax.ppermute(array, axis, pairs(lax.axis_size(axis), first, closed))  4.63 us
    pallas_call x1, Pallas kernels, body(): call(third_kernel, out_shape=(here(plain.shape, f32), plain, jax.ShapeDty...  3.83 us
    pallas_call x1, Pallas kernels, body(): call(first_kernel, out_shape=(here((nf, ca, cz + ROWS, cr), f32), here((2...  2.98 us
    pallas_call x1, Pallas kernels, body(): call(second_kernel, out_shape=(here((nf, ca, cz, cr), f32), here((nf, ca,...  2.05 us
    another operation x4, other arithmetic  1.67 us
    pallas_call x1, Pallas kernels, body(): call(last_kernel, out_shape=plain, in_specs=[SMEM] + [VMEM] * 4, out_spec...  1.51 us
  transfers between devices with their start and end apart: 10, of which 2 were waited for; matrix products, arithmetic and copies ran while one was open for 4% of the time, Pallas kernels for 23%

profile of v2, /device:TPU:24, one launch (start us, length us, event | category | flops | bytes accessed | tf_op | source)
XLA Modules:
  0.0 42.7 jit_solution(12668199634993598269)
XLA Ops:
  0.6 0.0 copy-start
  0.7 0.9 %fusion.10 = (f16[1,4,4,256]{3,2,1,0:T(4,128)(2,1)S(1)}, f16[1,4,4,256]{3,2,1,0:T(4,128)(2,1)S(1)}) fusion(s32[4,16,256]{2,1,0:T(8,128)} %kinds_ref.5, pred[]{:T(512)S(6)} %eq.18, pred[]{:T(512)S(6)} %not.3), kind=kLoop, calls=%fused_computation.45 | loop fusion | flops 24576 | bytes 49154 | tf_op jit(solution)/shard_map/convert_element_type | solution.py:344
  1.5 0.0 copy-start.6
  1.5 1.6 %select_convert_fusion.3 = (f16[12,4,4,256]{3,2,1,0:T(4,128)(2,1)S(1)}, f16[12,4,4,256]{3,2,1,0:T(4,128)(2,1)S(1)}, f16[12,4,4,256]{3,2,1,0:T(4,128)(2,1)S(1)}, f16[12,4,4,256]{3,2,1,0:T(4,128)(2,1)S(1)}) fusion(f32[12,4,16,256]{3,2,1,0:T(8,128)} %store_ref.5, pred[]{:T(512)S(6)} %eq.18, pred[]{:T(512)S(6)} %not.3, f32[12,4,16,256]{3,2,1,0:T(8,128)} %source_ref.5), kind=kLoop, calls=%fused_computation.23 | loop fusion | flops 491520 | bytes 1179650 | tf_op jit(solution)/shard_map/convert.17
  3.1 0.0 copy-start.8
  3.1 0.0 copy-start.7
  3.2 0.0 copy-start.9
  3.2 0.0 copy-start.10
  3.2 0.0 copy-start.11
  3.2 0.2 pad_maximum_fusion.1
  3.4 1.0 %collective-permute-start.1 = (f16[25,4,4,256]{3,2,1,0:T(4,128)(2,1)S(1)}, f16[25,4,4,256]{3,2,1,0:T(4,128)(2,1)S(1)}, u32[]{:S(2)}, u32[]{:S(2)}) collective-permute-start(f16[25,4,4,256]{3,2,1,0:T(4,128)(2,1)S(1)} %pad_maximum_fusion.1), channel_id=1, source_target_pairs={{1,2},{2,1},{3,0},{0,3},{5,6},{6,5},{7,4},{4,7},{9,10},{10,9},{11,... | collective-permute-start | bytes 614408 | tf_op jit(solution)/shard_map/ppermute | solution.py:321
  4.4 0.2 pad_maximum_fusion
  4.6 0.7 %collective-permute-start = (f16[25,4,4,256]{3,2,1,0:T(4,128)(2,1)S(1)}, f16[25,4,4,256]{3,2,1,0:T(4,128)(2,1)S(1)}, u32[]{:S(2)}, u32[]{:S(2)}) collective-permute-start(f16[25,4,4,256]{3,2,1,0:T(4,128)(2,1)S(1)} %pad_maximum_fusion), channel_id=1, source_target_pairs={{0,1},{1,0},{2,3},{3,2},{4,5},{5,4},{6,7},{7,6},{8,9},{9,8},{10,11... | collective-permute-start | bytes 614408 | tf_op jit(solution)/shard_map/ppermute | solution.py:321
  5.4 1.6 %collective-permute-start.3 = (f16[256,256]{1,0:T(8,128)(2,1)S(1)}, f16[256,256]{1,0:T(8,128)(2,1)S(1)}, u32[]{:S(2)}, u32[]{:S(2)}) collective-permute-start(f16[256,256]{1,0:T(8,128)(2,1)S(1)} %maximum_maximum_fusion), channel_id=1, source_target_pairs={{0,4},{4,0},{8,12},{12,8},{16,20},{20,16},{24,28},{28,24},{1,5},{5... | collective-permute-start | bytes 393224 | tf_op jit(solution)/shard_map/ppermute | solution.py:321
  7.0 2.3 %collective-permute-start.2 = (f16[12,16,256]{2,1,0:T(8,128)(2,1)S(1)}, f16[12,16,256]{2,1,0:T(8,128)(2,1)S(1)}, u32[]{:S(2)}, u32[]{:S(2)}) collective-permute-start(f16[12,16,256]{2,1,0:T(8,128)(2,1)S(1)} %get-tuple-element.24), channel_id=1, source_target_pairs={{4,8},{8,4},{12,16},{16,12},{20,24},{24,20},{5,9},{9,5},{13,17},{1... | collective-permute-start | bytes 294920 | tf_op jit(solution)/shard_map/ppermute | solution.py:321
  9.3 0.1 select_multiply_fusion
  10.2 0.1 pad.32.clone
  10.3 0.1 add_convert_fusion.even_ref
  10.4 4.0 %collective-permute-done.2 = f16[12,16,256]{2,1,0:T(8,128)(2,1)S(1)} collective-permute-done((f16[12,16,256]{2,1,0:T(8,128)(2,1)S(1)}, f16[12,16,256]{2,1,0:T(8,128)(2,1)S(1)}, u32[]{:S(2)}, u32[]{:S(2)}) %collective-permute-start.2) | collective-permute-done | bytes 98336 | tf_op jit(solution)/shard_map/ppermute | solution.py:321
  14.4 0.0 collective-permute-done.3
  14.5 0.5 %collective-permute-start.6 = (bf16[256,128]{1,0:T(8,128)(2,1)S(1)}, bf16[256,128]{1,0:T(8,128)(2,1)S(1)}, u32[]{:S(2)}, u32[]{:S(2)}) collective-permute-start(bf16[256,128]{1,0:T(8,128)(2,1)S(1)} %pad_maximum_fusion.3), channel_id=1, source_target_pairs={{0,8},{4,12},{8,0},{12,4},{16,24},{20,28},{24,16},{28,20},{1,9},{5... | collective-permute-start | bytes 196616 | tf_op jit(solution)/shard_map/ppermute | solution.py:398
  15.1 0.1 broadcast_multiply_fusion
  15.2 0.0 collective-permute-done.1
  15.2 0.0 collective-permute-done
  15.2 0.1 broadcast_select_fusion.1
  15.3 0.0 copy-start.1
  15.3 0.0 copy-start.2
  15.3 0.2 maximum_convert_fusion
  15.5 0.1 slice.102
  15.6 0.1 broadcast_in_dim.33.cond_ref
  15.7 0.8 %copy-done.1 = f32[12,4,16,256]{3,2,1,0:T(8,128)S(1)} copy-done((f32[12,4,16,256]{3,2,1,0:T(8,128)S(1)}, f32[12,4,16,256]{3,2,1,0:T(8,128)}, u32[]{:S(2)}) %copy-start.1) | copy-done | bytes 786456
  16.5 3.0 %shard_map.148 = (f32[12,4,24,256]{3,2,1,0:T(8,128)S(1)}, f32[2,12,24,256]{3,2,1,0:T(8,128)S(1)}, bf16[384,192]{1,0:T(8,128)(2,1)S(1)}, bf16[384,96]{1,0:T(8,128)(2,1)S(1)}) custom-call(s32[3]{0:T(128)S(1)} %add_convert_fusion.even_ref, f32[12,4,16,256]{3,2,1,0:T(8,128)S(1)} %copy-done, f32[12,4,16,256]{3,2,1,0:T(8,128)S(1)} %copy-done.1, ...), custom_call_target="tpu_custom_call" | custom-call | tf_op jit(solution)/shard_map/pallas_call | solution.py:375
  19.4 0.1 fusion
  19.5 1.9 %collective-permute-start.4 = (f16[12,24,256]{2,1,0:T(8,128)(2,1)S(1)}, f16[12,24,256]{2,1,0:T(8,128)(2,1)S(1)}, u32[]{:S(2)}, u32[]{:S(2)}) collective-permute-start(f16[12,24,256]{2,1,0:T(8,128)(2,1)S(1)} %get-tuple-element.30), channel_id=1, source_target_pairs={{4,8},{8,4},{12,16},{16,12},{20,24},{24,20},{5,9},{9,5},{13,17},{1... | collective-permute-start | bytes 442376 | tf_op jit(solution)/shard_map/ppermute | solution.py:321
  21.5 0.1 collective-permute-start.5
  21.6 4.5 %collective-permute-start.7 = (bf16[512,128]{1,0:T(8,128)(2,1)S(1)}, bf16[512,128]{1,0:T(8,128)(2,1)S(1)}, u32[]{:S(2)}, u32[]{:S(2)}) collective-permute-start(bf16[512,128]{1,0:T(8,128)(2,1)S(1)} %pad_maximum_fusion.2), channel_id=1, source_target_pairs={{0,16},{4,20},{8,24},{12,28},{16,0},{20,4},{24,8},{28,12},{1,17},{... | collective-permute-start | bytes 393224 | tf_op jit(solution)/shard_map/ppermute | solution.py:398
  26.1 2.0 %shard_map.149 = (f32[12,4,16,256]{3,2,1,0:T(8,128)S(1)}, f32[12,4,24,256]{3,2,1,0:T(8,128)S(1)}, f32[2,12,16,256]{3,2,1,0:T(8,128)S(1)}) custom-call(s32[3]{0:T(128)S(1)} %add_convert_fusion.even_ref, f32[12,4,24,256]{3,2,1,0:T(8,128)S(1)} %get-tuple-element.13.rest_ref.first_rest_ref, f32[12,16,256]{2,1,0:T(8,128)S(1)} %convert_element_type.88.halo1_ref, ...), custom_call_target="tpu_custom_call" | custom-call | tf_op jit(solution)/shard_map/pallas_call | solution.py:420
  28.2 0.0 copy-start.3
  28.2 0.6 %collective-permute-done.5 = f16[12,24,256]{2,1,0:T(8,128)(2,1)S(1)} collective-permute-done((f16[12,24,256]{2,1,0:T(8,128)(2,1)S(1)}, f16[12,24,256]{2,1,0:T(8,128)(2,1)S(1)}, u32[]{:S(2)}, u32[]{:S(2)}) %collective-permute-start.5) | collective-permute-done | bytes 147488 | tf_op jit(solution)/shard_map/ppermute | solution.py:321
  28.8 0.0 copy-start.4
  28.8 0.0 copy-start.5
  28.8 0.1 slice_multiply_fusion
  29.0 0.2 fusion.4
  29.1 0.1 collective-permute-start.9
  29.2 7.0 %collective-permute-start.8 = (f16[12,16,256]{2,1,0:T(8,128)(2,1)S(1)}, f16[12,16,256]{2,1,0:T(8,128)(2,1)S(1)}, u32[]{:S(2)}, u32[]{:S(2)}) collective-permute-start(f16[12,16,256]{2,1,0:T(8,128)(2,1)S(1)} %get-tuple-element.34), channel_id=1, source_target_pairs={{4,8},{8,4},{12,16},{16,12},{20,24},{24,20},{5,9},{9,5},{13,17},{1... | collective-permute-start | bytes 294920 | tf_op jit(solution)/shard_map/ppermute | solution.py:321
  36.2 1.0 %shard_map.150.incoming_ref = f32[128,128]{1,0:T(8,128)S(1)} custom-call(s32[8,128]{1,0:T(8,128)S(1)} %pad.26.index_ref, s32[8,128]{1,0:T(8,128)S(1)} %pad.27.block_ref, bf16[1024,128]{1,0:T(8,128)(2,1)S(1)} %constant_dynamic-update-slice_fusion.rows_ref, bf16[8,128,128]{2,1,0:T(8,128)(2,1)S(1)} %copy-done.3), custom_call_target="tpu_custom_call" | custom-call | tf_op jit(solution)/shard_map/pallas_call | solution.py:413
  37.3 3.8 %shard_map.151 = (f32[12,4,16,256]{3,2,1,0:T(8,128)S(1)}, f32[12,4,16,256]{3,2,1,0:T(8,128)}, f32[120,128]{1,0:T(8,128)}) custom-call(s32[3]{0:T(128)S(1)} %add_convert_fusion.even_ref, s32[1]{0:T(128)} %bitcast.59.live_ref, f32[12,4,16,256]{3,2,1,0:T(8,128)S(1)} %get-tuple-element.16.rest_ref, f32[12,24,256]{2,1,0:T(8,128)S(1)} %convert_element_type.93.halo1_ref, ...), custom_call_target="tpu_custom_call" | custom-call | tf_op jit(solution)/shard_map/pallas_call | solution.py:439
  41.2 1.5 %shard_map.152 = f32[12,4,16,256]{3,2,1,0:T(8,128)} custom-call(s32[3]{0:T(128)S(1)} %add_convert_fusion.even_ref, f32[12,4,16,256]{3,2,1,0:T(8,128)S(1)} %get-tuple-element.20.rest_ref, f32[12,16,256]{2,1,0:T(8,128)S(1)} %convert_element_type.98.halo1_ref, f32[12,16,256]{2,1,0:T(8,128)S(1)} %convert_element_type.100.halo0_ref, ...), custom_call_target="tpu_custom_call" | custom-call | tf_op jit(solution)/shard_map/pallas_call | solution.py:448
  (47 shorter events, 0.5 us)
Async XLA Ops:
  0.6 4.7 %copy-start = (f32[12,4,16,256]{3,2,1,0:T(8,128)S(1)}, f32[12,4,16,256]{3,2,1,0:T(8,128)}, u32[]{:S(2)}) copy-start(f32[12,4,16,256]{3,2,1,0:T(8,128)} %source_ref.5) | copy-start | bytes 2359300
  1.5 3.8 %copy-start.6 = (bf16[1,1,120,128]{3,2,1,0:T(8,128)(2,1)S(1)}, bf16[1,1,120,128]{3,2,1,0:T(8,128)(2,1)}, u32[]{:S(2)}) copy-start(bf16[1,1,120,128]{3,2,1,0:T(8,128)(2,1)} %param.22) | copy-start | bytes 92164
  3.1 6.2 %copy-start.8 = (f32[12]{0:T(128)S(1)}, f32[12]{0:T(128)}, u32[]{:S(2)}) copy-start(f32[12]{0:T(128)} %param.16) | copy-start | bytes 148
  3.1 6.3 %copy-start.7 = (f32[4,12,12]{2,0,1:T(4,128)S(1)}, f32[4,12,12]{2,0,1:T(4,128)}, u32[]{:S(2)}) copy-start(f32[4,12,12]{2,0,1:T(4,128)} %param.17) | copy-start | bytes 6916
  3.2 6.3 %copy-start.9 = (s32[1,1,120,4]{2,3,1,0:T(4,128)S(1)}, s32[1,1,120,4]{2,3,1,0:T(4,128)}, u32[]{:S(2)}) copy-start(s32[1,1,120,4]{2,3,1,0:T(4,128)} %param.20) | copy-start | bytes 5764
  3.2 6.3 %copy-start.10 = (s32[1,1,120,4]{2,3,1,0:T(4,128)S(1)}, s32[1,1,120,4]{2,3,1,0:T(4,128)}, u32[]{:S(2)}) copy-start(s32[1,1,120,4]{2,3,1,0:T(4,128)} %param.19) | copy-start | bytes 5764
  3.2 6.3 %copy-start.11 = (s32[1,1,120,4]{2,3,1,0:T(4,128)S(1)}, s32[1,1,120,4]{2,3,1,0:T(4,128)}, u32[]{:S(2)}) copy-start(s32[1,1,120,4]{2,3,1,0:T(4,128)} %param.21) | copy-start | bytes 5764
  3.4 11.8 %collective-permute-start.1 = (f16[25,4,4,256]{3,2,1,0:T(4,128)(2,1)S(1)}, f16[25,4,4,256]{3,2,1,0:T(4,128)(2,1)S(1)}, u32[]{:S(2)}, u32[]{:S(2)}) collective-permute-start(f16[25,4,4,256]{3,2,1,0:T(4,128)(2,1)S(1)} %pad_maximum_fusion.1), channel_id=1, source_target_pairs={{1,2},{2,1},{3,0},{0,3},{5,6},{6,5},{7,4},{4,7},{9,10},{10,9},{11,... | collective-permute-start | bytes 614408 | tf_op jit(solution)/shard_map/ppermute | solution.py:321
  4.6 10.6 %collective-permute-start = (f16[25,4,4,256]{3,2,1,0:T(4,128)(2,1)S(1)}, f16[25,4,4,256]{3,2,1,0:T(4,128)(2,1)S(1)}, u32[]{:S(2)}, u32[]{:S(2)}) collective-permute-start(f16[25,4,4,256]{3,2,1,0:T(4,128)(2,1)S(1)} %pad_maximum_fusion), channel_id=1, source_target_pairs={{0,1},{1,0},{2,3},{3,2},{4,5},{5,4},{6,7},{7,6},{8,9},{9,8},{10,11... | collective-permute-start | bytes 614408 | tf_op jit(solution)/shard_map/ppermute | solution.py:321
  5.4 9.0 %collective-permute-start.3 = (f16[256,256]{1,0:T(8,128)(2,1)S(1)}, f16[256,256]{1,0:T(8,128)(2,1)S(1)}, u32[]{:S(2)}, u32[]{:S(2)}) collective-permute-start(f16[256,256]{1,0:T(8,128)(2,1)S(1)} %maximum_maximum_fusion), channel_id=1, source_target_pairs={{0,4},{4,0},{8,12},{12,8},{16,20},{20,16},{24,28},{28,24},{1,5},{5... | collective-permute-start | bytes 393224 | tf_op jit(solution)/shard_map/ppermute | solution.py:321
  7.0 7.4 %collective-permute-start.2 = (f16[12,16,256]{2,1,0:T(8,128)(2,1)S(1)}, f16[12,16,256]{2,1,0:T(8,128)(2,1)S(1)}, u32[]{:S(2)}, u32[]{:S(2)}) collective-permute-start(f16[12,16,256]{2,1,0:T(8,128)(2,1)S(1)} %get-tuple-element.24), channel_id=1, source_target_pairs={{4,8},{8,4},{12,16},{16,12},{20,24},{24,20},{5,9},{9,5},{13,17},{1... | collective-permute-start | bytes 294920 | tf_op jit(solution)/shard_map/ppermute | solution.py:321
  14.5 7.0 %collective-permute-start.6 = (bf16[256,128]{1,0:T(8,128)(2,1)S(1)}, bf16[256,128]{1,0:T(8,128)(2,1)S(1)}, u32[]{:S(2)}, u32[]{:S(2)}) collective-permute-start(bf16[256,128]{1,0:T(8,128)(2,1)S(1)} %pad_maximum_fusion.3), channel_id=1, source_target_pairs={{0,8},{4,12},{8,0},{12,4},{16,24},{20,28},{24,16},{28,20},{1,9},{5... | collective-permute-start | bytes 196616 | tf_op jit(solution)/shard_map/ppermute | solution.py:398
  15.3 1.1 %copy-start.1 = (f32[12,4,16,256]{3,2,1,0:T(8,128)S(1)}, f32[12,4,16,256]{3,2,1,0:T(8,128)}, u32[]{:S(2)}) copy-start(f32[12,4,16,256]{3,2,1,0:T(8,128)} %store_ref.5) | copy-start | bytes 2359300
  15.3 1.1 %copy-start.2 = (s32[4,16,256]{2,1,0:T(8,128)S(1)}, s32[4,16,256]{2,1,0:T(8,128)}, u32[]{:S(2)}) copy-start(s32[4,16,256]{2,1,0:T(8,128)} %kinds_ref.5) | copy-start | bytes 196612
  19.5 8.6 %collective-permute-start.4 = (f16[12,24,256]{2,1,0:T(8,128)(2,1)S(1)}, f16[12,24,256]{2,1,0:T(8,128)(2,1)S(1)}, u32[]{:S(2)}, u32[]{:S(2)}) collective-permute-start(f16[12,24,256]{2,1,0:T(8,128)(2,1)S(1)} %get-tuple-element.30), channel_id=1, source_target_pairs={{4,8},{8,4},{12,16},{16,12},{20,24},{24,20},{5,9},{9,5},{13,17},{1... | collective-permute-start | bytes 442376 | tf_op jit(solution)/shard_map/ppermute | solution.py:321
  21.5 7.3 %collective-permute-start.5 = (f16[12,24,256]{2,1,0:T(8,128)(2,1)S(1)}, f16[12,24,256]{2,1,0:T(8,128)(2,1)S(1)}, u32[]{:S(2)}, u32[]{:S(2)}) collective-permute-start(f16[12,24,256]{2,1,0:T(8,128)(2,1)S(1)} %get-tuple-element.29), channel_id=1, source_target_pairs={{0,4},{4,0},{8,12},{12,8},{16,20},{20,16},{24,28},{28,24},{1,5},{5... | collective-permute-start | bytes 442376 | tf_op jit(solution)/shard_map/ppermute | solution.py:321
  21.6 14.6 %collective-permute-start.7 = (bf16[512,128]{1,0:T(8,128)(2,1)S(1)}, bf16[512,128]{1,0:T(8,128)(2,1)S(1)}, u32[]{:S(2)}, u32[]{:S(2)}) collective-permute-start(bf16[512,128]{1,0:T(8,128)(2,1)S(1)} %pad_maximum_fusion.2), channel_id=1, source_target_pairs={{0,16},{4,20},{8,24},{12,28},{16,0},{20,4},{24,8},{28,12},{1,17},{... | collective-permute-start | bytes 393224 | tf_op jit(solution)/shard_map/ppermute | solution.py:398
  28.2 8.1 %copy-start.3 = (bf16[8,128,128]{2,1,0:T(8,128)(2,1)S(1)}, bf16[8,128,128]{2,1,0:T(8,128)(2,1)}, u32[]{:S(2)}) copy-start(bf16[8,128,128]{2,1,0:T(8,128)(2,1)} %view_ref.1) | copy-start | bytes 786436
  28.8 8.5 %copy-start.4 = (f32[1,1,120,128]{3,2,1,0:T(8,128)S(1)}, f32[1,1,120,128]{3,2,1,0:T(8,128)}, u32[]{:S(2)}) copy-start(f32[1,1,120,128]{3,2,1,0:T(8,128)} %param.24) | copy-start | bytes 184324
  28.8 8.5 %copy-start.5 = (f32[1,1,120,128]{3,2,1,0:T(8,128)S(1)}, f32[1,1,120,128]{3,2,1,0:T(8,128)}, u32[]{:S(2)}) copy-start(f32[1,1,120,128]{3,2,1,0:T(8,128)} %param.25) | copy-start | bytes 184324
  29.1 12.0 %collective-permute-start.9 = (f16[12,16,256]{2,1,0:T(8,128)(2,1)S(1)}, f16[12,16,256]{2,1,0:T(8,128)(2,1)S(1)}, u32[]{:S(2)}, u32[]{:S(2)}) collective-permute-start(f16[12,16,256]{2,1,0:T(8,128)(2,1)S(1)} %get-tuple-element.33), channel_id=1, source_target_pairs={{0,4},{4,0},{8,12},{12,8},{16,20},{20,16},{24,28},{28,24},{1,5},{5... | collective-permute-start | bytes 294920 | tf_op jit(solution)/shard_map/ppermute | solution.py:321
  29.2 11.9 %collective-permute-start.8 = (f16[12,16,256]{2,1,0:T(8,128)(2,1)S(1)}, f16[12,16,256]{2,1,0:T(8,128)(2,1)S(1)}, u32[]{:S(2)}, u32[]{:S(2)}) collective-permute-start(f16[12,16,256]{2,1,0:T(8,128)(2,1)S(1)} %get-tuple-element.34), channel_id=1, source_target_pairs={{4,8},{8,4},{12,16},{16,12},{20,24},{24,20},{5,9},{9,5},{13,17},{1... | collective-permute-start | bytes 294920 | tf_op jit(solution)/shard_map/ppermute | solution.py:321

commit v3 on v2

v3 whole, which is shorter than its diff:
```python
import functools
import jax
import jax.numpy as jnp
from jax import lax
from jax.experimental import pallas as pl
from jax.experimental.pallas import tpu as pltpu
from jax.sharding import PartitionSpec as P

center_value = 14.2
half_width = 13.8
sigma = center_value / half_width
ratio_0 = 1.0 / sigma
ratio_1 = 1.0 / (2.0 * sigma - ratio_0)
ratio_2 = 1.0 / (2.0 * sigma - ratio_1)
ALPHA = (None, ratio_1 * ratio_0, ratio_2 * ratio_1)
BETA = (None, 2.0 * ratio_1 / half_width, 2.0 * ratio_2 / half_width)
INV_CENTER = 1.0 / center_value

COPIES = 4
ROWS = 8
LINK = jnp.float16
RAD_SCALE = 8192.0
f32, bf16 = jnp.float32, jnp.bfloat16

VMEM = pl.BlockSpec(memory_space=pltpu.VMEM)
HBM = pl.BlockSpec(memory_space=pl.ANY)
PARAMS = pltpu.CompilerParams(vmem_limit_bytes=16 * 1024 * 1024)
CHEAP = pl.CostEstimate(flops=0, bytes_accessed=0, transcendentals=0)


def each_field(count, step):
    for f in range(count):
        step(f)


def tall(tile, height):
    return jnp.concatenate([tile] * (height // ROWS), axis=0)


def mixed_part(cells, kinds, coef, out_ref, a, rows):
    nf, height, cr = cells.shape
    flat = cells.reshape(nf * height, cr)
    high = flat.astype(bf16)
    low = (flat - high.astype(f32)).astype(bf16)
    out = jnp.dot(coef, jnp.concatenate([high, high, low], axis=0), preferred_element_type=f32)
    mats = out.shape[0] // (nf * height)
    out = out.reshape(mats, nf, height, cr)
    is_kind = [kinds == m for m in range(mats - 1)]
    for f in range(nf):
        picked = out[mats - 1, f]
        for m in range(mats - 1):
            picked = jnp.where(is_kind[m], out[m, f], picked)
        out_ref[f, a, rows] = picked


def radial_sum(cells):
    cr = cells.shape[-1]
    lane = lax.broadcasted_iota(jnp.int32, cells.shape, cells.ndim - 1)
    inner = jnp.where(lane == 0, 0.0, pltpu.roll(cells, 1, cells.ndim - 1))
    outer = jnp.where(lane == cr - 1, 0.0, pltpu.roll(cells, cr - 1, cells.ndim - 1))
    return inner + outer


def azim_sum(cells):
    rows = cells.shape[0]
    return pltpu.roll(cells, 1, 0) + pltpu.roll(cells, rows - 1, 0)


def apply_local(dir_ref, store, kinds, cond_ref, coef, mix_ref, span, emit):
    nf, ca = dir_ref.shape[:2]
    start, stop = span
    for a in range(ca):
        for t in range(start // ROWS, stop // ROWS):
            rows = slice(t * ROWS, (t + 1) * ROWS)
            mixed_part(dir_ref[:, a, rows], kinds(a, t), coef, mix_ref, a, rows)

    def step(f):
        cond = tall(cond_ref[f], stop - start)
        planes = [dir_ref[f, a] for a in range(ca)]
        for a in range(ca):
            cells = planes[a][start:stop]
            around = azim_sum(planes[a])[start:stop] + radial_sum(cells)
            if a > 0:
                around = around + planes[a - 1][start:stop]
            if a + 1 < ca:
                around = around + planes[a + 1][start:stop]
            emit(f, a, store(f, a) * cells + mix_ref[f, a, start:stop] - cond * around)

    each_field(nf, step)


def swapped(tile):
    place = lax.broadcasted_iota(jnp.int32, tile.shape, 0)
    return jnp.where((place // 2) % 2 == 0, pltpu.roll(tile, ROWS - 2, 0), pltpu.roll(tile, 2, 0))


def ends_kernel(
    flags_ref, source_hbm, store_hbm, kinds_hbm, source_ref, store_ref, kinds_ref, edge_ref, side_ref, sems
):
    nf, ca, cz, cr = source_ref.shape
    part = nf // COPIES
    pairs_of = [
        (far.at[pl.ds(i * part, part)], near.at[pl.ds(i * part, part)])
        for far, near in ((source_hbm, source_ref), (store_hbm, store_ref))
        for i in range(COPIES)
    ] + [(kinds_hbm, kinds_ref)]
    copies = [pltpu.make_async_copy(far, near, sems.at[i]) for i, (far, near) in enumerate(pairs_of)]
    for copy in copies:
        copy.start()
    even = tall(flags_ref[0], cz) > 0.5
    place = lax.broadcasted_iota(jnp.int32, (ROWS, cr), 0)

    def both(ref, *lead):
        return jnp.where(place < ROWS // 2, ref[(*lead, slice(0, ROWS))], ref[(*lead, slice(cz - ROWS, cz))])

    for copy in copies[:COPIES]:
        copy.wait()
    for f in range(nf):
        low, high = source_ref[f, 0] * INV_CENTER, source_ref[f, ca - 1] * INV_CENTER
        edge_ref[0, f] = jnp.where(even, low, high)
        edge_ref[1, f] = jnp.where(even, high, low)
        for a in range(ca):
            side_ref[f, a] = both(source_ref, f, a) * INV_CENTER
    for copy in copies[COPIES : 2 * COPIES]:
        copy.wait()
    outer = (place < 2) | (place >= ROWS - 2)
    for f in range(nf // 2):
        for a in range(ca):
            side_ref[nf + f, a] = jnp.where(
                outer, both(store_ref, f, a), swapped(both(store_ref, nf // 2 + f, a))
            )
    copies[2 * COPIES].wait()
    for a in range(ca):
        side_ref[nf + nf // 2, a] = both(kinds_ref, a).astype(f32)


def wing_store(wing_ref, f, a):
    nf = wing_ref.shape[0] // 3 * 2
    if f < nf // 2:
        return wing_ref[nf + f, a]
    return swapped(wing_ref[nf // 2 + f, a])


def coef_kernel(mix_ref, coef_ref):
    mixes = mix_ref[...]
    high = mixes.astype(bf16)
    low = (mixes - high.astype(f32)).astype(bf16)
    wide, inner = coef_ref.shape[0], coef_ref.shape[1] // 3
    row = lax.broadcasted_iota(jnp.int32, (wide, mixes.shape[0]), 0)
    col = lax.broadcasted_iota(jnp.int32, (wide, mixes.shape[0]), 1)
    down = (row // ROWS == col).astype(bf16)
    row = lax.broadcasted_iota(jnp.int32, (mixes.shape[1], inner), 0)
    col = lax.broadcasted_iota(jnp.int32, (mixes.shape[1], inner), 1)
    across = (col // ROWS == row).astype(bf16)
    row = lax.broadcasted_iota(jnp.int32, (wide, inner), 0)
    col = lax.broadcasted_iota(jnp.int32, (wide, inner), 1)
    same = row % ROWS == col % ROWS

    def spread(part):
        part = jnp.dot(down, part, preferred_element_type=f32).astype(bf16)
        full = jnp.dot(part, across, preferred_element_type=f32)
        return jnp.where(same, full, 0.0).astype(bf16)

    high = spread(high)
    coef_ref[:, :inner] = high
    coef_ref[:, inner : 2 * inner] = spread(low)
    coef_ref[:, 2 * inner :] = high


def first_kernel(
    source_ref, store_ref, kinds_ref, wing_ref, cond_ref, coef_ref,
    rest_ref, dir_ref, mix_ref,
):
    nf, ca, cz, cr = source_ref.shape
    own = cz // ROWS
    for f in range(nf):
        for a in range(ca):
            dir_ref[f, a, :cz] = source_ref[f, a] * INV_CENTER
            dir_ref[f, a, cz:] = wing_ref[f, a]

    def store(f, a):
        return jnp.concatenate([store_ref[f, a], wing_store(wing_ref, f, a)], axis=0)

    def kinds(a, t):
        return kinds_ref[a, t * ROWS : (t + 1) * ROWS].astype(f32) if t < own else wing_ref[nf + nf // 2, a]

    def emit(f, a, image):
        origin = jnp.concatenate([source_ref[f, a], center_value * wing_ref[f, a]], axis=0)
        rest_ref[f, a] = origin - image

    apply_local(dir_ref, store, kinds, cond_ref, coef_ref[...], mix_ref, (0, cz + ROWS), emit)


def side_kernel(
    first, flags_ref, rest_ref, halo_ref, source_ref, store_ref, kinds_ref, wing_ref, cond_ref, coef_ref,
    message_ref, dir_ref, next_ref, mix_ref,
):
    nf, ca, cz, cr = source_ref.shape
    even = flags_ref[0] > 0.5

    def choose(low, high):
        mask = tall(even, low.shape[0])
        return jnp.where(mask, low, high) if first else jnp.where(mask, high, low)

    place = lax.broadcasted_iota(jnp.int32, (ROWS, cr), 0)
    for f in range(nf):
        rest = choose(rest_ref[f, 0], rest_ref[f, ca - 1])
        wing = choose(wing_ref[f, 0], wing_ref[f, ca - 1])
        own = rest[:cz] + tall(cond_ref[f], cz) * halo_ref[f]
        direction = (ALPHA[1] * INV_CENTER) * choose(source_ref[f, 0], source_ref[f, ca - 1]) + BETA[1] * own
        beside = ALPHA[1] * wing + BETA[1] * rest[cz:]
        next_ref[f] = (ALPHA[1] * INV_CENTER) * choose(source_ref[f, 1], source_ref[f, ca - 2]) + BETA[1] * choose(
            rest_ref[f, 1, :cz], rest_ref[f, ca - 2, :cz]
        )
        dir_ref[f, 0, :cz] = direction
        dir_ref[f, 0, cz:] = beside
        message_ref[f, :cz] = direction
        message_ref[f, cz : 2 * cz] = own
        moved = jnp.where(place < 4, pltpu.roll(wing, 2, 0), pltpu.roll(wing, 6, 0))
        message_ref[f, 2 * cz :] = jnp.where((place >= 2) & (place <= 5), moved, beside)

    def kinds(a, t):
        rows = slice(t * ROWS, (t + 1) * ROWS)
        return choose(kinds_ref[0, rows].astype(f32), kinds_ref[ca - 1, rows].astype(f32))

    def emit(f, a, image):
        rest = message_ref[f, cz : 2 * cz] - image + tall(cond_ref[f], cz) * next_ref[f]
        message_ref[f, cz : 2 * cz] = ALPHA[2] * dir_ref[f, 0, :cz] + BETA[2] * rest

    apply_local(
        dir_ref, lambda f, a: choose(store_ref[f, 0], store_ref[f, ca - 1]), kinds,
        cond_ref, coef_ref[...], mix_ref, (0, cz), emit,
    )


def second_kernel(
    flags_ref, rest_ref, halo1_ref, halo0_ref, source_ref, store_ref, kinds_ref, wing_ref, cond_ref, coef_ref,
    newrest_ref, dir_ref, mix_ref,
):
    nf, ca, cz, cr = store_ref.shape
    even = tall(flags_ref[0], cz) > 0.5
    for f in range(nf):
        cond = tall(cond_ref[f], cz)
        arrived = {
            0: cond * jnp.where(even, halo1_ref[f], halo0_ref[f]),
            ca - 1: cond * jnp.where(even, halo0_ref[f], halo1_ref[f]),
        }
        for a in range(ca):
            rest = rest_ref[f, a, :cz]
            if a in arrived:
                rest = rest + arrived[a]
            newrest_ref[f, a] = rest
            dir_ref[f, a, :cz] = (ALPHA[1] * INV_CENTER) * source_ref[f, a] + BETA[1] * rest
            dir_ref[f, a, cz:] = ALPHA[1] * wing_ref[f, a] + BETA[1] * rest_ref[f, a, cz:]

    def emit(f, a, image):
        newrest_ref[f, a] = newrest_ref[f, a] - image

    apply_local(
        dir_ref, lambda f, a: store_ref[f, a], lambda a, t: kinds_ref[a, t * ROWS : (t + 1) * ROWS].astype(f32),
        cond_ref, coef_ref[...], mix_ref, (0, cz), emit,
    )


def third_kernel(
    flags_ref, rest_ref, halo1_ref, halo0_ref, second_ref, first_rest_ref, source_ref, store_ref,
    kinds_ref, wing_ref, cond_ref, coef_ref, live_ref, incoming_ref, emission_ref, reflect_ref,
    panel_ref, solution_ref, residual_ref,
    total_ref, out_ref, fixed_ref, dir_ref, beside_ref, mix_ref, sems,
):
    nf, ca, cz, cr = source_ref.shape
    own = cz // ROWS
    even = tall(flags_ref[0], 2 * cz + ROWS) > 0.5
    partner = {0: flags_ref[1] > 0.5, ca - 1: flags_ref[2] > 0.5}
    place = lax.broadcasted_iota(jnp.int32, (ROWS, cr), 0)
    outer = (place <= 1) | (place >= 6)

    def inward(beside):
        ends = [jnp.where(place == 0, pltpu.roll(beside, 1, 0), 0.0)]
        ends += [jnp.zeros_like(beside)] * (own - 2)
        ends += [jnp.where(place == ROWS - 1, pltpu.roll(beside, ROWS - 1, 0), 0.0)]
        return jnp.concatenate(ends, axis=0)

    for f in range(nf):
        cond = cond_ref[f]
        wide = tall(cond, cz)
        halo = {
            0: jnp.where(even, halo1_ref[f], halo0_ref[f]),
            ca - 1: jnp.where(even, halo0_ref[f], halo1_ref[f]),
        }
        for a in range(ca):
            rest = rest_ref[f, a]
            wing = second_ref[f, a, cz:]
            beside = first_rest_ref[f, a, cz:]
            direction = second_ref[f, a, :cz]
            if a in halo:
                old = halo[a][2 * cz :]
                moved = jnp.where(place < 4, pltpu.roll(old, ROWS - 2, 0), pltpu.roll(old, 2, 0))
                fix = cond * jnp.where(outer, moved, 0.0)
                rest = rest + wide * (halo[a][:cz] + BETA[1] * inward(fix))
                wing = wing + BETA[1] * fix
                mine = cond * wing_ref[f, a]
                beyond = cond * (old + BETA[1] * mine)
                beside = beside + fix + jnp.where(partner[a], beyond, 0.0)
            ahead = ALPHA[2] * direction + BETA[2] * rest
            if a in halo:
                third = halo[a][cz : 2 * cz] + BETA[2] * wide * (direction + BETA[1] * inward(mine))
                rest = rest + jnp.where(tall(partner[a], cz), wide * third, 0.0)
            out_ref[f, a] = rest
            fixed_ref[f, a, :cz] = direction
            fixed_ref[f, a, cz:] = wing
            beside_ref[f, a] = beside
            dir_ref[f, a, :cz] = ahead
            total_ref[f, a] = source_ref[f, a] * INV_CENTER + direction + ahead
    done_solution = pltpu.make_async_copy(total_ref, solution_ref, sems.at[0])
    done_solution.start()

    slots, values = panel_ref.shape
    wall = total_ref[0].reshape(ca * cz, cr)[:, cr - 1 : cr]
    wall = jnp.broadcast_to(wall, (ca * cz, values))
    wall = jnp.concatenate([wall] * (-(-slots // (ca * cz))), axis=0)[:slots]
    panel = lax.broadcasted_iota(jnp.int32, (slots, values), 0)
    fresh = emission_ref[...] * wall + reflect_ref[...] * incoming_ref[:slots]
    panel_ref[...] = jnp.where(panel < live_ref[:1], fresh, 0.0)

    def wing_emit(f, a, image):
        dir_ref[f, a, cz:] = ALPHA[2] * fixed_ref[f, a, cz:] + BETA[2] * (beside_ref[f, a] - image)

    apply_local(
        fixed_ref, lambda f, a: wing_store(wing_ref, f, a), lambda a, t: wing_ref[nf + nf // 2, a],
        cond_ref, coef_ref[...], mix_ref, (cz, cz + ROWS), wing_emit,
    )

    def emit(f, a, image):
        out_ref[f, a] = out_ref[f, a] - image

    apply_local(
        dir_ref, lambda f, a: store_ref[f, a], lambda a, t: kinds_ref[a, t * ROWS : (t + 1) * ROWS].astype(f32),
        cond_ref, coef_ref[...], mix_ref, (0, cz), emit,
    )
    done_residual = pltpu.make_async_copy(out_ref, residual_ref, sems.at[1])
    done_residual.start()
    done_solution.wait()
    done_residual.wait()


def panel_kernel(
    chunk, visible, index_ref, block_ref, rows_ref, view_ref, out_ref
):
    slots = index_ref.shape[1]
    total, values = rows_ref.shape
    index = index_ref[...].T
    block = block_ref[...].T
    types = view_ref.shape[0]
    lane = lax.broadcasted_iota(jnp.int32, (slots, chunk), 1)

    def gather(start):
        rows = rows_ref[pl.ds(start, chunk), :]
        return tuple(
            jnp.dot(
                (index[:, k : k + 1] == lane + start).astype(f32).astype(bf16),
                rows,
                preferred_element_type=f32,
            )
            for k in range(visible)
        )

    if total == chunk:
        found = gather(0)
    else:
        zero = tuple(jnp.zeros((slots, values), f32) for _ in range(visible))

        def step(i, sums):
            return tuple(s + g for s, g in zip(sums, gather(pl.multiple_of(i * chunk, chunk))))

        found = lax.fori_loop(0, total // chunk, step, zero)
    out = jnp.zeros((slots, values), f32)
    for b in range(types):
        stack = jnp.concatenate(
            [jnp.where(block[:, k : k + 1] == b, found[k], 0.0) for k in range(visible)], axis=0
        ).astype(bf16)
        moved = lax.dot_general(
            stack, view_ref[b], (((1,), (1,)), ((), ())), preferred_element_type=f32
        )
        for k in range(visible):
            out = out + moved[k * slots : (k + 1) * slots]
    out_ref[...] = out


def pairs(count, first, closed):
    swaps = []
    for i in range(first, count if closed and first else count - 1, 2):
        j = (i + 1) % count
        swaps += [(i, j), (j, i)]
    return swaps


def swap(array, axis, first, closed=False):
    return lax.ppermute(array, axis, pairs(lax.axis_size(axis), first, closed))


def body(
    source, storage, materials, conductance, mixing, counts, vis_owner, vis_slot, vis_block,
    radiosity_old, view_blocks, emission, reflect,
):
    nf, ca, cz, cr = source.shape
    mats = mixing.shape[0]
    owners = lax.axis_size("axial")
    me = lax.axis_index("axial")
    is_even = me % 2 == 0
    flags = jnp.stack([is_even, me > 0, me + 1 < owners]).astype(f32)
    flags = jnp.broadcast_to(flags[:, None, None], (3, ROWS, cr))
    azim_even = lax.axis_index("azim") % 2 == 0
    here = pltpu.VMEM

    def call(kernel, outs, args, scratch=(), far_out=False, plain_args=False):
        specs = [VMEM] * len(outs)
        if far_out:
            specs[-1] = HBM
        if not plain_args:
            args = [pltpu.with_memory_space_constraint(x, pltpu.VMEM) for x in args]
        single = len(outs) == 1
        return pl.pallas_call(
            kernel,
            out_shape=outs[0] if single else tuple(outs),
            in_specs=[VMEM] * len(args),
            out_specs=specs[0] if single else tuple(specs),
            scratch_shapes=list(scratch),
            compiler_params=PARAMS, cost_estimate=CHEAP,
        )(*args)

    def after(value, *others):
        return lax.optimization_barrier((value, *others))[0]

    plain = here((nf, ca, cz, cr), f32)
    layers = here((2, nf, cz, cr), f32)
    source, storage, materials, edges, sides = pl.pallas_call(
        ends_kernel,
        out_shape=(
            plain, plain, here((ca, cz, cr), jnp.int32), layers, here((nf + nf // 2 + 1, ca, ROWS, cr), f32)
        ),
        in_specs=[VMEM] + [HBM] * 3,
        out_specs=(VMEM,) * 5,
        scratch_shapes=[pltpu.SemaphoreType.DMA((2 * COPIES + 1,))],
        compiler_params=PARAMS, cost_estimate=CHEAP,
    )(flags, *(pltpu.with_memory_space_constraint(x, pltpu.HBM) for x in (source, storage, materials)))
    half = ROWS // 2
    to_right, to_left = sides[:, :, half:], sides[:, :, :half]
    far = jnp.where(azim_even, to_left, to_right).astype(LINK)
    near = jnp.where(azim_even, to_right, to_left).astype(LINK)
    far_in = swap(far, "azim", 1, True)
    message1 = after(edges, far)[0].astype(LINK)
    halo1 = swap(message1, "axial", 1)
    near_in = swap(after(near, message1), "azim", 0)

    slots, visible = vis_owner.shape[2:]
    values = radiosity_old.shape[3]
    tile = -(-slots // 16) * 16
    panels = jnp.pad(radiosity_old[0, 0], ((0, tile - slots), (0, 0)))
    fold = cr // values
    folded = panels.astype(f32) * RAD_SCALE
    folded = jnp.concatenate(jnp.split(folded, fold, axis=0), axis=1)
    layer0 = after(edges, message1)[1].reshape(nf * cz, cr)
    message = swap(jnp.concatenate([layer0, folded], axis=0).astype(LINK), "axial", 0)

    from_right = jnp.where(azim_even, near_in, far_in)
    from_left = jnp.where(azim_even, far_in, near_in)
    wings = jnp.concatenate([from_right, from_left], axis=2).astype(f32)

    cond = jnp.broadcast_to(conductance[:, None, None], (nf, ROWS, cr))
    mixes = mixing + 6.0 * jnp.diag(conductance)
    mixes = jnp.pad(mixes.reshape(mats * nf, nf), ((0, 0), (0, 128 - nf)))
    coef = call(coef_kernel, (here((mats * nf * ROWS, 3 * nf * ROWS), bf16),), (mixes,))
    full = here((nf, ca, cz + ROWS, cr), f32)
    rest = call(first_kernel, (full,), (source, storage, materials, wings, cond, coef), (full, full))

    def side(first, halo):
        return call(
            functools.partial(side_kernel, first),
            (here((nf, 2 * cz + ROWS, cr), f32),),
            (flags, rest, halo, source, storage, materials, wings, cond, coef),
            (here((nf, 1, cz + ROWS, cr), f32), here((nf, cz, cr), f32), here((nf, 1, cz + ROWS, cr), f32)),
        ).astype(LINK)

    halo1 = after(halo1, rest).astype(f32)
    message1 = side(True, halo1)
    second1 = swap(message1, "axial", 1).astype(f32)
    message = after(message, message1)
    halo0 = message[: nf * cz].reshape(nf, cz, cr).astype(f32)
    message0 = side(False, halo0)
    second0 = swap(message0, "axial", 0).astype(f32)

    rest2, dir2 = call(
        second_kernel,
        (plain, full),
        (flags, after(rest, message0), halo1, halo0, source, storage, materials, wings, cond, coef),
        (full,),
    )

    partner = after(message, rest2)[nf * cz :].astype(f32) * (1.0 / RAD_SCALE)
    partner = jnp.concatenate(jnp.split(partner, fold, axis=1), axis=0).astype(bf16)
    if owners <= 8 and owners & (owners - 1) == 0:
        pair = jnp.concatenate([panels, partner], axis=0)
        others = [
            lax.ppermute(pair, "axial", [(i, i ^ step) for i in range(owners)]) for step in range(2, owners, 2)
        ]
        panels = jnp.concatenate([pair, *others], axis=0)
        owner = vis_owner[0, 0].T ^ me
    else:
        pair = jnp.stack([panels, partner])
        panels = jnp.where(is_even, pair, pair[::-1]).reshape(2 * tile, values)
        groups = [list(range(k, owners, 2)) for k in range(2)]
        panels = lax.all_gather(panels, "axial", axis=0, tiled=True, axis_index_groups=groups)
        panels = panels.reshape(owners // 2, 2 * tile, values).reshape(owners * tile, values)
        owner = vis_owner[0, 0].T
    pad = ((0, -visible % ROWS), (0, -slots % 128))
    index = jnp.pad(owner * tile + vis_slot[0, 0].T, pad, constant_values=-1)
    block = jnp.pad(vis_block[0, 0].T, pad)
    chunk = tile * 8 if owners % 8 == 0 else tile * owners
    incoming = call(
        functools.partial(panel_kernel, chunk, visible),
        (here((index.shape[1], values), f32),),
        (index, block, panels, view_blocks),
        plain_args=True,
    )

    live = jnp.broadcast_to(counts, (ROWS, values))
    shape = jax.ShapeDtypeStruct
    panel_new, solution_out, residual = pl.pallas_call(
        third_kernel,
        out_shape=(shape((slots, values), f32), shape(source.shape, f32), shape(source.shape, f32)),
        in_specs=[VMEM] * 16,
        out_specs=(VMEM, HBM, HBM),
        scratch_shapes=[
            plain, plain, full, full, here((nf, ca, ROWS, cr), f32), full, pltpu.SemaphoreType.DMA((2,))
        ],
        compiler_params=PARAMS, cost_estimate=CHEAP,
    )(
        flags, rest2, second1, second0, dir2, rest, source, storage, materials, wings, cond, coef,
        live, incoming, emission[0, 0], reflect[0, 0],
    )
    return (solution_out, residual, panel_new[None, None])


def solution(mesh):
    return jax.shard_map(
        body,
        mesh=mesh,
        in_specs=(
            P(None, "axial", "azim", None),
            P(None, "axial", "azim", None),
            P("axial", "azim", None),
            P(),
            P(),
            P("axial", "azim"),
            P("axial", "azim", None, None),
            P("axial", "azim", None, None),
            P("axial", "azim", None, None),
            P("axial", "azim", None, None),
            P(),
            P("axial", "azim", None, None),
            P("axial", "azim", None, None),
        ),
        out_specs=(
            P(None, "axial", "azim", None),
            P(None, "axial", "azim", None),
            P("axial", "azim", None, None),
        ),
        check_vma=False,
    )
```

time: 42.9 us -> 36.8 us (0.86)
  the two profiles are of different devices: /device:TPU:24 before, /device:TPU:0 now
where the time goes in v3:
time: 36.8 us; the launch traced here: 36.6 us
  starting transfers between devices  17.1 us (46%)
  Pallas kernels  11.8 us (32%)
  waiting for transfers between devices  4.78 us (13%)
  between operations  1.74 us (5%)
  other arithmetic  0.87 us (2%)
    ppermute x6, starting transfers between devices, swap(): return lax.ppermute(array, axis, pairs(lax.axis_size(axis), first, closed))  12.7 us
    pallas_call x6, Pallas kernels, call(): pl.pallas_call(kernel, out_shape=outs[0] if single else tuple(outs), in_s...  6.26 us
    ppermute x3, waiting for transfers between devices, body(): lax.ppermute(pair, 'axial', [(i, i ^ step) for i in range(owners)])  4.76 us
    ppermute x3, starting transfers between devices, body(): lax.ppermute(pair, 'axial', [(i, i ^ step) for i in range(owners)])  4.45 us
    pallas_call x1, Pallas kernels, body(): pl.pallas_call(third_kernel, out_shape=(shape((slots, values), f32), shap...  3.92 us
    pallas_call x1, Pallas kernels, body(): pl.pallas_call(ends_kernel, out_shape=(plain, plain, here((ca, cz, cr), j...  1.59 us
  transfers between devices with their start and end apart: 9, of which 2 were waited for; matrix products, arithmetic and copies ran while one was open for 2% of the time, Pallas kernels for 17%

profile of v3, /device:TPU:0, one launch (start us, length us, event | category | flops | bytes accessed | tf_op | source)
XLA Modules:
  0.0 36.6 jit_solution(1132626112593769295)
XLA Ops:
  0.7 0.1 add_convert_fusion
  0.7 0.1 broadcast_in_dim.41.flags_ref
  0.8 1.6 %shard_map.148 = (f32[12,4,16,256]{3,2,1,0:T(8,128)S(1)}, f32[12,4,16,256]{3,2,1,0:T(8,128)S(1)}, s32[4,16,256]{2,1,0:T(8,128)S(1)}, f32[2,12,16,256]{3,2,1,0:T(8,128)S(1)}, f32[19,4,8,256]{3,2,1,0:T(8,128)S(1)}) custom-call(f32[3,8,256]{2,1,0:T(8,128)S(1)} %broadcast_in_dim.41.flags_ref, f32[12,4,16,256]{3,2,1,0:T(8,128)} %source_hbm.1, ...), custom_call_target="tpu_custom_call" | custom-call | tf_op jit(solution)/shard_map/pallas_call | solution.py:437
  2.4 0.0 copy-start.5
  2.4 0.0 copy-start.4
  2.4 0.0 copy-start.6
  2.4 0.0 copy-start.7
  2.5 0.0 copy-start.8
  2.5 0.2 select_convert_fusion.1
  2.6 2.5 %collective-permute-start.1 = (f16[19,4,4,256]{3,2,1,0:T(4,128)(2,1)S(1)}, f16[19,4,4,256]{3,2,1,0:T(4,128)(2,1)S(1)}, u32[]{:S(2)}, u32[]{:S(2)}) collective-permute-start(f16[19,4,4,256]{3,2,1,0:T(4,128)(2,1)S(1)} %get-tuple-element.38), channel_id=1, source_target_pairs={{1,2},{2,1},{3,0},{0,3},{5,6},{6,5},{7,4},{4,7},{9,10},{10,9},{11,... | collective-permute-start | bytes 466952 | tf_op jit(solution)/shard_map/ppermute | solution.py:399
  5.1 0.7 %collective-permute-start.3 = (f16[12,16,256]{2,1,0:T(8,128)(2,1)S(1)}, f16[12,16,256]{2,1,0:T(8,128)(2,1)S(1)}, u32[]{:S(2)}, u32[]{:S(2)}) collective-permute-start(f16[12,16,256]{2,1,0:T(8,128)(2,1)S(1)} %fusion), channel_id=1, source_target_pairs={{4,8},{8,4},{12,16},{16,12},{20,24},{24,20},{5,9},{9,5},{13,17},{1... | collective-permute-start | bytes 294920 | tf_op jit(solution)/shard_map/ppermute | solution.py:399
  5.8 0.0 copy-done.3
  5.9 4.3 %collective-permute-start.2 = (f16[256,256]{1,0:T(8,128)(2,1)S(1)}, f16[256,256]{1,0:T(8,128)(2,1)S(1)}, u32[]{:S(2)}, u32[]{:S(2)}) collective-permute-start(f16[256,256]{1,0:T(8,128)(2,1)S(1)} %maximum_maximum_fusion), channel_id=1, source_target_pairs={{0,4},{4,0},{8,12},{12,8},{16,20},{20,16},{24,28},{28,24},{1,5},{5... | collective-permute-start | bytes 393224 | tf_op jit(solution)/shard_map/ppermute | solution.py:399
  10.3 0.1 collective-permute-start
  10.4 0.0 copy-done.5
  10.4 0.1 select_multiply_fusion
  10.5 0.0 copy-done.4
  10.5 0.0 copy-done.6
  10.5 0.0 copy-done.7
  11.2 0.0 copy-done.8
  11.3 0.4 %shard_map.149.coef_ref = bf16[384,288]{1,0:T(8,128)(2,1)S(1)} custom-call(f32[48,128]{1,0:T(8,128)S(1)} %pad.15.mix_ref), custom_call_target="tpu_custom_call" | custom-call | tf_op jit(solution)/shard_map/pallas_call | solution.py:423
  11.7 0.0 collective-permute-done
  11.7 0.0 collective-permute-done.1
  11.7 0.1 broadcast_select_fusion.1
  11.8 0.2 maximum_convert_fusion.wing_ref
  12.0 0.1 broadcast_in_dim.42.cond_ref
  12.1 2.1 %shard_map.150.rest_ref.first_rest_ref = f32[12,4,24,256]{3,2,1,0:T(8,128)S(1)} custom-call(f32[12,4,16,256]{3,2,1,0:T(8,128)S(1)} %get-tuple-element.20.source_ref, f32[12,4,16,256]{3,2,1,0:T(8,128)S(1)} %get-tuple-element.21.store_ref, s32[4,16,256]{2,1,0:T(8,128)S(1)} %get-tuple-element.22.kinds_ref, f32[19,4,8,256]{3,2,1,0:T(8,128)S(1)} %maximum_convert_fusion.wing_ref, ...), custom_call_target="tpu_custom_call" | custom-call | tf_op jit(solution)/shard_map/pallas_call | solution.py:423
  14.2 0.0 collective-permute-done.3
  14.2 0.6 %shard_map.151 = f32[12,40,256]{2,1,0:T(8,128)S(1)} custom-call(f32[3,8,256]{2,1,0:T(8,128)S(1)} %broadcast_in_dim.41.flags_ref, f32[12,4,24,256]{3,2,1,0:T(8,128)S(1)} %shard_map.150.rest_ref.first_rest_ref, f32[12,16,256]{2,1,0:T(8,128)S(1)} %convert_element_type.58.halo_ref.halo1_ref, f32[12,4,16,256]{3,2,1,0:T(8,128)S(1)} %get-tuple-element.20.source_ref, ...), custom_call_target="tpu_custom_call" | custom-call | tf_op jit(solution)/shard_map/pallas_call | solution.py:423
  14.8 0.7 %collective-permute-start.4 = (f16[12,40,256]{2,1,0:T(8,128)(2,1)S(1)}, f16[12,40,256]{2,1,0:T(8,128)(2,1)S(1)}, u32[]{:S(2)}, u32[]{:S(2)}) collective-permute-start(f16[12,40,256]{2,1,0:T(8,128)(2,1)S(1)} %convert_element_type.59), channel_id=1, source_target_pairs={{4,8},{8,4},{12,16},{16,12},{20,24},{24,20},{5,9},{9,5},{13,17},{1... | collective-permute-start | bytes 737288 | tf_op jit(solution)/shard_map/ppermute | solution.py:399
  15.5 0.0 collective-permute-done.2
  15.6 0.6 %shard_map.152 = f32[12,40,256]{2,1,0:T(8,128)S(1)} custom-call(f32[3,8,256]{2,1,0:T(8,128)S(1)} %broadcast_in_dim.41.flags_ref, f32[12,4,24,256]{3,2,1,0:T(8,128)S(1)} %shard_map.150.rest_ref.first_rest_ref, f32[12,16,256]{2,1,0:T(8,128)S(1)} %convert.26.halo_ref.halo0_ref, f32[12,4,16,256]{3,2,1,0:T(8,128)S(1)} %get-tuple-element.20.source_ref, ...), custom_call_target="tpu_custom_call" | custom-call | tf_op jit(solution)/shard_map/pallas_call | solution.py:423
  16.2 0.0 copy-start
  16.2 4.4 %collective-permute-start.5 = (f16[12,40,256]{2,1,0:T(8,128)(2,1)S(1)}, f16[12,40,256]{2,1,0:T(8,128)(2,1)S(1)}, u32[]{:S(2)}, u32[]{:S(2)}) collective-permute-start(f16[12,40,256]{2,1,0:T(8,128)(2,1)S(1)} %convert_element_type.62), channel_id=1, source_target_pairs={{0,4},{4,0},{8,12},{12,8},{16,20},{20,16},{24,28},{28,24},{1,5},{5... | collective-permute-start | bytes 737288 | tf_op jit(solution)/shard_map/ppermute | solution.py:399
  20.6 1.6 %shard_map.153 = (f32[12,4,16,256]{3,2,1,0:T(8,128)S(1)}, f32[12,4,24,256]{3,2,1,0:T(8,128)S(1)}) custom-call(f32[3,8,256]{2,1,0:T(8,128)S(1)} %broadcast_in_dim.41.flags_ref, f32[12,4,24,256]{3,2,1,0:T(8,128)S(1)} %shard_map.150.rest_ref.first_rest_ref, f32[12,16,256]{2,1,0:T(8,128)S(1)} %convert_element_type.58.halo_ref.halo1_ref, ...), custom_call_target="tpu_custom_call" | custom-call | tf_op jit(solution)/shard_map/pallas_call | solution.py:423
  22.2 1.2 %collective-permute-start.8 = (bf16[256,128]{1,0:T(8,128)(2,1)S(1)}, bf16[256,128]{1,0:T(8,128)(2,1)S(1)}, u32[]{:S(2)}, u32[]{:S(2)}) collective-permute-start(bf16[256,128]{1,0:T(8,128)(2,1)S(1)} %pad_maximum_fusion), channel_id=1, source_target_pairs={{0,24},{4,28},{8,16},{12,20},{16,8},{20,12},{24,0},{28,4},{1,25},{... | collective-permute-start | bytes 196616 | tf_op jit(solution)/shard_map/ppermute | solution.py:505
  23.4 1.9 %collective-permute-start.7 = (bf16[256,128]{1,0:T(8,128)(2,1)S(1)}, bf16[256,128]{1,0:T(8,128)(2,1)S(1)}, u32[]{:S(2)}, u32[]{:S(2)}) collective-permute-start(bf16[256,128]{1,0:T(8,128)(2,1)S(1)} %pad_maximum_fusion), channel_id=1, source_target_pairs={{0,16},{4,20},{8,24},{12,28},{16,0},{20,4},{24,8},{28,12},{1,17},{... | collective-permute-start | bytes 196616 | tf_op jit(solution)/shard_map/ppermute | solution.py:505
  25.3 1.4 %collective-permute-start.6 = (bf16[256,128]{1,0:T(8,128)(2,1)S(1)}, bf16[256,128]{1,0:T(8,128)(2,1)S(1)}, u32[]{:S(2)}, u32[]{:S(2)}) collective-permute-start(bf16[256,128]{1,0:T(8,128)(2,1)S(1)} %pad_maximum_fusion), channel_id=1, source_target_pairs={{0,8},{4,12},{8,0},{12,4},{16,24},{20,28},{24,16},{28,20},{1,9},{5... | collective-permute-start | bytes 196616 | tf_op jit(solution)/shard_map/ppermute | solution.py:505
  26.7 3.3 %collective-permute-done.6 = bf16[256,128]{1,0:T(8,128)(2,1)S(1)} collective-permute-done((bf16[256,128]{1,0:T(8,128)(2,1)S(1)}, bf16[256,128]{1,0:T(8,128)(2,1)S(1)}, u32[]{:S(2)}, u32[]{:S(2)}) %collective-permute-start.6) | collective-permute-done | bytes 65568 | tf_op jit(solution)/shard_map/ppermute | solution.py:505
  30.0 0.0 copy-start.1
  30.0 0.0 copy-start.2
  30.0 1.5 %collective-permute-done.7 = bf16[256,128]{1,0:T(8,128)(2,1)S(1)} collective-permute-done((bf16[256,128]{1,0:T(8,128)(2,1)S(1)}, bf16[256,128]{1,0:T(8,128)(2,1)S(1)}, u32[]{:S(2)}, u32[]{:S(2)}) %collective-permute-start.7) | collective-permute-done | bytes 65568 | tf_op jit(solution)/shard_map/ppermute | solution.py:505
  31.5 0.0 collective-permute-done.8
  31.5 0.0 copy-done
  31.5 1.0 %shard_map.154.incoming_ref = f32[128,128]{1,0:T(8,128)S(1)} custom-call(s32[8,128]{1,0:T(8,128)S(1)} %pad.17.index_ref, s32[8,128]{1,0:T(8,128)S(1)} %pad.18.block_ref, bf16[1024,128]{1,0:T(8,128)(2,1)S(1)} %constant_dynamic-update-slice_fusion.rows_ref, bf16[8,128,128]{2,1,0:T(8,128)(2,1)S(1)} %copy-done), custom_call_target="tpu_custom_call" | custom-call | tf_op jit(solution)/shard_map/pallas_call | solution.py:423
  32.6 0.0 collective-permute-done.4
  32.6 0.0 collective-permute-done.5
  32.7 3.9 %shard_map.155 = (f32[120,128]{1,0:T(8,128)}, f32[12,4,16,256]{3,2,1,0:T(8,128)}, f32[12,4,16,256]{3,2,1,0:T(8,128)}) custom-call(f32[3,8,256]{2,1,0:T(8,128)S(1)} %broadcast_in_dim.41.flags_ref, f32[12,4,16,256]{3,2,1,0:T(8,128)S(1)} %get-tuple-element.31.rest_ref, f32[12,40,256]{2,1,0:T(8,128)S(1)} %convert_element_type.63.halo1_ref, ...), custom_call_target="tpu_custom_call" | custom-call | tf_op jit(solution)/shard_map/pallas_call | solution.py:529
  (31 shorter events, 0.4 us)
Async XLA Ops:
  0.8 5.0 %copy-start.3 = (bf16[1,1,120,128]{3,2,1,0:T(8,128)(2,1)S(1)}, bf16[1,1,120,128]{3,2,1,0:T(8,128)(2,1)}, u32[]{:S(2)}) copy-start(bf16[1,1,120,128]{3,2,1,0:T(8,128)(2,1)} %param.22) | copy-start | bytes 92164
  2.4 8.0 %copy-start.5 = (f32[12]{0:T(128)S(1)}, f32[12]{0:T(128)}, u32[]{:S(2)}) copy-start(f32[12]{0:T(128)} %param.16) | copy-start | bytes 148
  2.4 8.1 %copy-start.4 = (f32[4,12,12]{2,0,1:T(4,128)S(1)}, f32[4,12,12]{2,0,1:T(4,128)}, u32[]{:S(2)}) copy-start(f32[4,12,12]{2,0,1:T(4,128)} %param.17) | copy-start | bytes 6916
  2.4 8.1 %copy-start.6 = (s32[1,1,120,4]{2,3,1,0:T(4,128)S(1)}, s32[1,1,120,4]{2,3,1,0:T(4,128)}, u32[]{:S(2)}) copy-start(s32[1,1,120,4]{2,3,1,0:T(4,128)} %param.20) | copy-start | bytes 5764
  2.4 8.1 %copy-start.7 = (s32[1,1,120,4]{2,3,1,0:T(4,128)S(1)}, s32[1,1,120,4]{2,3,1,0:T(4,128)}, u32[]{:S(2)}) copy-start(s32[1,1,120,4]{2,3,1,0:T(4,128)} %param.19) | copy-start | bytes 5764
  2.5 8.7 %copy-start.8 = (s32[1,1,120,4]{2,3,1,0:T(4,128)S(1)}, s32[1,1,120,4]{2,3,1,0:T(4,128)}, u32[]{:S(2)}) copy-start(s32[1,1,120,4]{2,3,1,0:T(4,128)} %param.21) | copy-start | bytes 5764
  2.6 9.1 %collective-permute-start.1 = (f16[19,4,4,256]{3,2,1,0:T(4,128)(2,1)S(1)}, f16[19,4,4,256]{3,2,1,0:T(4,128)(2,1)S(1)}, u32[]{:S(2)}, u32[]{:S(2)}) collective-permute-start(f16[19,4,4,256]{3,2,1,0:T(4,128)(2,1)S(1)} %get-tuple-element.38), channel_id=1, source_target_pairs={{1,2},{2,1},{3,0},{0,3},{5,6},{6,5},{7,4},{4,7},{9,10},{10,9},{11,... | collective-permute-start | bytes 466952 | tf_op jit(solution)/shard_map/ppermute | solution.py:399
  5.1 9.0 %collective-permute-start.3 = (f16[12,16,256]{2,1,0:T(8,128)(2,1)S(1)}, f16[12,16,256]{2,1,0:T(8,128)(2,1)S(1)}, u32[]{:S(2)}, u32[]{:S(2)}) collective-permute-start(f16[12,16,256]{2,1,0:T(8,128)(2,1)S(1)} %fusion), channel_id=1, source_target_pairs={{4,8},{8,4},{12,16},{16,12},{20,24},{24,20},{5,9},{9,5},{13,17},{1... | collective-permute-start | bytes 294920 | tf_op jit(solution)/shard_map/ppermute | solution.py:399
  5.9 9.6 %collective-permute-start.2 = (f16[256,256]{1,0:T(8,128)(2,1)S(1)}, f16[256,256]{1,0:T(8,128)(2,1)S(1)}, u32[]{:S(2)}, u32[]{:S(2)}) collective-permute-start(f16[256,256]{1,0:T(8,128)(2,1)S(1)} %maximum_maximum_fusion), channel_id=1, source_target_pairs={{0,4},{4,0},{8,12},{12,8},{16,20},{20,16},{24,28},{28,24},{1,5},{5... | collective-permute-start | bytes 393224 | tf_op jit(solution)/shard_map/ppermute | solution.py:399
  10.3 1.4 %collective-permute-start = (f16[19,4,4,256]{3,2,1,0:T(4,128)(2,1)S(1)}, f16[19,4,4,256]{3,2,1,0:T(4,128)(2,1)S(1)}, u32[]{:S(2)}, u32[]{:S(2)}) collective-permute-start(f16[19,4,4,256]{3,2,1,0:T(4,128)(2,1)S(1)} %get-tuple-element.26), channel_id=1, source_target_pairs={{0,1},{1,0},{2,3},{3,2},{4,5},{5,4},{6,7},{7,6},{8,9},{9,8},{10,11... | collective-permute-start | bytes 466952 | tf_op jit(solution)/shard_map/ppermute | solution.py:399
  14.8 17.7 %collective-permute-start.4 = (f16[12,40,256]{2,1,0:T(8,128)(2,1)S(1)}, f16[12,40,256]{2,1,0:T(8,128)(2,1)S(1)}, u32[]{:S(2)}, u32[]{:S(2)}) collective-permute-start(f16[12,40,256]{2,1,0:T(8,128)(2,1)S(1)} %convert_element_type.59), channel_id=1, source_target_pairs={{4,8},{8,4},{12,16},{16,12},{20,24},{24,20},{5,9},{9,5},{13,17},{1... | collective-permute-start | bytes 737288 | tf_op jit(solution)/shard_map/ppermute | solution.py:399
  16.2 15.3 %copy-start = (bf16[8,128,128]{2,1,0:T(8,128)(2,1)S(1)}, bf16[8,128,128]{2,1,0:T(8,128)(2,1)}, u32[]{:S(2)}) copy-start(bf16[8,128,128]{2,1,0:T(8,128)(2,1)} %view_ref.1) | copy-start | bytes 786436
  16.2 16.4 %collective-permute-start.5 = (f16[12,40,256]{2,1,0:T(8,128)(2,1)S(1)}, f16[12,40,256]{2,1,0:T(8,128)(2,1)S(1)}, u32[]{:S(2)}, u32[]{:S(2)}) collective-permute-start(f16[12,40,256]{2,1,0:T(8,128)(2,1)S(1)} %convert_element_type.62), channel_id=1, source_target_pairs={{0,4},{4,0},{8,12},{12,8},{16,20},{20,16},{24,28},{28,24},{1,5},{5... | collective-permute-start | bytes 737288 | tf_op jit(solution)/shard_map/ppermute | solution.py:399
  22.2 9.3 %collective-permute-start.8 = (bf16[256,128]{1,0:T(8,128)(2,1)S(1)}, bf16[256,128]{1,0:T(8,128)(2,1)S(1)}, u32[]{:S(2)}, u32[]{:S(2)}) collective-permute-start(bf16[256,128]{1,0:T(8,128)(2,1)S(1)} %pad_maximum_fusion), channel_id=1, source_target_pairs={{0,24},{4,28},{8,16},{12,20},{16,8},{20,12},{24,0},{28,4},{1,25},{... | collective-permute-start | bytes 196616 | tf_op jit(solution)/shard_map/ppermute | solution.py:505
  23.4 8.1 %collective-permute-start.7 = (bf16[256,128]{1,0:T(8,128)(2,1)S(1)}, bf16[256,128]{1,0:T(8,128)(2,1)S(1)}, u32[]{:S(2)}, u32[]{:S(2)}) collective-permute-start(bf16[256,128]{1,0:T(8,128)(2,1)S(1)} %pad_maximum_fusion), channel_id=1, source_target_pairs={{0,16},{4,20},{8,24},{12,28},{16,0},{20,4},{24,8},{28,12},{1,17},{... | collective-permute-start | bytes 196616 | tf_op jit(solution)/shard_map/ppermute | solution.py:505
  25.3 4.7 %collective-permute-start.6 = (bf16[256,128]{1,0:T(8,128)(2,1)S(1)}, bf16[256,128]{1,0:T(8,128)(2,1)S(1)}, u32[]{:S(2)}, u32[]{:S(2)}) collective-permute-start(bf16[256,128]{1,0:T(8,128)(2,1)S(1)} %pad_maximum_fusion), channel_id=1, source_target_pairs={{0,8},{4,12},{8,0},{12,4},{16,24},{20,28},{24,16},{28,20},{1,9},{5... | collective-permute-start | bytes 196616 | tf_op jit(solution)/shard_map/ppermute | solution.py:505
  30.0 2.7 %copy-start.1 = (f32[1,1,120,128]{3,2,1,0:T(8,128)S(1)}, f32[1,1,120,128]{3,2,1,0:T(8,128)}, u32[]{:S(2)}) copy-start(f32[1,1,120,128]{3,2,1,0:T(8,128)} %param.24) | copy-start | bytes 184324
  30.0 2.7 %copy-start.2 = (f32[1,1,120,128]{3,2,1,0:T(8,128)S(1)}, f32[1,1,120,128]{3,2,1,0:T(8,128)}, u32[]{:S(2)}) copy-start(f32[1,1,120,128]{3,2,1,0:T(8,128)} %param.25) | copy-start | bytes 184324

commit v4 on v3

--- a/solution.py
+++ b/solution.py
@@ -16,6 +16,7 @@
 BETA = (None, 2.0 * ratio_1 / half_width, 2.0 * ratio_2 / half_width)
 INV_CENTER = 1.0 / center_value
 
+GROUP = 4
 COPIES = 4
 ROWS = 8
 LINK = jnp.float16
@@ -44,12 +45,12 @@
     low = (flat - high.astype(f32)).astype(bf16)
     out = jnp.dot(coef, jnp.concatenate([high, high, low], axis=0), preferred_element_type=f32)
     mats = out.shape[0] // (nf * height)
-    out = out.reshape(mats, nf, height, cr)
+    out = out.reshape(nf, mats, height, cr)
     is_kind = [kinds == m for m in range(mats - 1)]
     for f in range(nf):
-        picked = out[mats - 1, f]
+        picked = out[f, mats - 1]
         for m in range(mats - 1):
-            picked = jnp.where(is_kind[m], out[m, f], picked)
+            picked = jnp.where(is_kind[m], out[f, m], picked)
         out_ref[f, a, rows] = picked
 
 
@@ -66,7 +67,7 @@
     return pltpu.roll(cells, 1, 0) + pltpu.roll(cells, rows - 1, 0)
 
 
-def apply_local(dir_ref, store, kinds, cond_ref, coef, mix_ref, span, emit):
+def apply_local(dir_ref, store, kinds, cond_ref, coef, mix_ref, span, emit, linked=True):
     nf, ca = dir_ref.shape[:2]
     start, stop = span
     for a in range(ca):
@@ -80,9 +81,9 @@
         for a in range(ca):
             cells = planes[a][start:stop]
             around = azim_sum(planes[a])[start:stop] + radial_sum(cells)
-            if a > 0:
+            if linked and a > 0:
                 around = around + planes[a - 1][start:stop]
-            if a + 1 < ca:
+            if linked and a + 1 < ca:
                 around = around + planes[a + 1][start:stop]
             emit(f, a, store(f, a) * cells + mix_ref[f, a, start:stop] - cond * around)
 
@@ -94,12 +95,38 @@
     return jnp.where((place // 2) % 2 == 0, pltpu.roll(tile, ROWS - 2, 0), pltpu.roll(tile, 2, 0))
 
 
+def coef_rows(mixes):
+    tall_rows, nf = mixes.shape
+    wide, inner = tall_rows * ROWS, nf * ROWS
+    high = mixes.astype(bf16)
+    low = (mixes - high.astype(f32)).astype(bf16)
+    row = lax.broadcasted_iota(jnp.int32, (wide, tall_rows), 0)
+    col = lax.broadcasted_iota(jnp.int32, (wide, tall_rows), 1)
+    down = (row // ROWS == col).astype(bf16)
+    row = lax.broadcasted_iota(jnp.int32, (nf, inner), 0)
+    col = lax.broadcasted_iota(jnp.int32, (nf, inner), 1)
+    across = (col // ROWS == row).astype(bf16)
+    row = lax.broadcasted_iota(jnp.int32, (wide, inner), 0)
+    col = lax.broadcasted_iota(jnp.int32, (wide, inner), 1)
+    same = row % ROWS == col % ROWS
+
+    def spread(part):
+        part = jnp.dot(down, part, preferred_element_type=f32).astype(bf16)
+        full = jnp.dot(part, across, preferred_element_type=f32)
+        return jnp.where(same, full, 0.0).astype(bf16)
+
+    high = spread(high)
+    return high, spread(low), high
+
+
 def ends_kernel(
-    flags_ref, source_hbm, store_hbm, kinds_hbm, source_ref, store_ref, kinds_ref, edge_ref, side_ref, sems
+    flags_ref, source_hbm, store_hbm, kinds_hbm, cond_hbm, mix_hbm,
+    source_ref, store_ref, kinds_ref, edge_ref, side_ref, cond_ref, coef_ref,
+    cond_row, mix_rows, sems,
 ):
     nf, ca, cz, cr = source_ref.shape
     part = nf // COPIES
-    pairs_of = [
+    pairs_of = [(cond_hbm, cond_row), (mix_hbm, mix_rows)] + [
         (far.at[pl.ds(i * part, part)], near.at[pl.ds(i * part, part)])
         for far, near in ((source_hbm, source_ref), (store_hbm, store_ref))
         for i in range(COPIES)
@@ -110,18 +137,31 @@
     even = tall(flags_ref[0], cz) > 0.5
     place = lax.broadcasted_iota(jnp.int32, (ROWS, cr), 0)
 
+    copies[0].wait()
+    copies[1].wait()
+    for f in range(nf):
+        cond_ref[f] = jnp.broadcast_to(cond_row[:, f : f + 1], (ROWS, cr))
+    mats = mix_rows.shape[1]
+    mixes = jnp.concatenate([mix_rows[f] for f in range(nf)], axis=0)
+    row = lax.broadcasted_iota(jnp.int32, mixes.shape, 0)
+    col = lax.broadcasted_iota(jnp.int32, mixes.shape, 1)
+    mixes = mixes + jnp.where(row // mats == col, 6.0 * cond_row[...], 0.0)
+    inner = nf * ROWS
+    for i, rows in enumerate(coef_rows(mixes)):
+        coef_ref[:, i * inner : (i + 1) * inner] = rows
+
     def both(ref, *lead):
         return jnp.where(place < ROWS // 2, ref[(*lead, slice(0, ROWS))], ref[(*lead, slice(cz - ROWS, cz))])
 
-    for copy in copies[:COPIES]:
-        copy.wait()
-    for f in range(nf):
+    for f in range(nf):
+        if f % part == 0:
+            copies[2 + f // part].wait()
         low, high = source_ref[f, 0] * INV_CENTER, source_ref[f, ca - 1] * INV_CENTER
         edge_ref[0, f] = jnp.where(even, low, high)
         edge_ref[1, f] = jnp.where(even, high, low)
         for a in range(ca):
             side_ref[f, a] = both(source_ref, f, a) * INV_CENTER
-    for copy in copies[COPIES : 2 * COPIES]:
+    for copy in copies[2 + COPIES :]:
         copy.wait()
     outer = (place < 2) | (place >= ROWS - 2)
     for f in range(nf // 2):
@@ -129,7 +169,6 @@
             side_ref[nf + f, a] = jnp.where(
                 outer, both(store_ref, f, a), swapped(both(store_ref, nf // 2 + f, a))
             )
-    copies[2 * COPIES].wait()
     for a in range(ca):
         side_ref[nf + nf // 2, a] = both(kinds_ref, a).astype(f32)
 
@@ -141,32 +180,6 @@
     return swapped(wing_ref[nf // 2 + f, a])
 
 
-def coef_kernel(mix_ref, coef_ref):
-    mixes = mix_ref[...]
-    high = mixes.astype(bf16)
-    low = (mixes - high.astype(f32)).astype(bf16)
-    wide, inner = coef_ref.shape[0], coef_ref.shape[1] // 3
-    row = lax.broadcasted_iota(jnp.int32, (wide, mixes.shape[0]), 0)
-    col = lax.broadcasted_iota(jnp.int32, (wide, mixes.shape[0]), 1)
-    down = (row // ROWS == col).astype(bf16)
-    row = lax.broadcasted_iota(jnp.int32, (mixes.shape[1], inner), 0)
-    col = lax.broadcasted_iota(jnp.int32, (mixes.shape[1], inner), 1)
-    across = (col // ROWS == row).astype(bf16)
-    row = lax.broadcasted_iota(jnp.int32, (wide, inner), 0)
-    col = lax.broadcasted_iota(jnp.int32, (wide, inner), 1)
-    same = row % ROWS == col % ROWS
-
-    def spread(part):
-        part = jnp.dot(down, part, preferred_element_type=f32).astype(bf16)
-        full = jnp.dot(part, across, preferred_element_type=f32)
-        return jnp.where(same, full, 0.0).astype(bf16)
-
-    high = spread(high)
-    coef_ref[:, :inner] = high
-    coef_ref[:, inner : 2 * inner] = spread(low)
-    coef_ref[:, 2 * inner :] = high
-
-
 def first_kernel(
     source_ref, store_ref, kinds_ref, wing_ref, cond_ref, coef_ref,
     rest_ref, dir_ref, mix_ref,
@@ -191,6 +204,12 @@
     apply_local(dir_ref, store, kinds, cond_ref, coef_ref[...], mix_ref, (0, cz + ROWS), emit)
 
 
+def beside_rows(wing, beside):
+    place = lax.broadcasted_iota(jnp.int32, wing.shape, 0)
+    moved = jnp.where(place < 4, pltpu.roll(wing, 2, 0), pltpu.roll(wing, 6, 0))
+    return jnp.where((place >= 2) & (place <= 5), moved, beside)
+
+
 def side_kernel(
     first, flags_ref, rest_ref, halo_ref, source_ref, store_ref, kinds_ref, wing_ref, cond_ref, coef_ref,
     message_ref, dir_ref, next_ref, mix_ref,
@@ -202,7 +221,6 @@
         mask = tall(even, low.shape[0])
         return jnp.where(mask, low, high) if first else jnp.where(mask, high, low)
 
-    place = lax.broadcasted_iota(jnp.int32, (ROWS, cr), 0)
     for f in range(nf):
         rest = choose(rest_ref[f, 0], rest_ref[f, ca - 1])
         wing = choose(wing_ref[f, 0], wing_ref[f, ca - 1])
@@ -216,8 +234,7 @@
         dir_ref[f, 0, cz:] = beside
         message_ref[f, :cz] = direction
         message_ref[f, cz : 2 * cz] = own
-        moved = jnp.where(place < 4, pltpu.roll(wing, 2, 0), pltpu.roll(wing, 6, 0))
-        message_ref[f, 2 * cz :] = jnp.where((place >= 2) & (place <= 5), moved, beside)
+        message_ref[f, 2 * cz :] = beside_rows(wing, beside)
 
     def kinds(a, t):
         rows = slice(t * ROWS, (t + 1) * ROWS)
@@ -233,7 +250,7 @@
     )
 
 
-def second_kernel(
+def second_part(
     flags_ref, rest_ref, halo1_ref, halo0_ref, source_ref, store_ref, kinds_ref, wing_ref, cond_ref, coef_ref,
     newrest_ref, dir_ref, mix_ref,
 ):
@@ -262,86 +279,143 @@
     )
 
 
-def third_kernel(
-    flags_ref, rest_ref, halo1_ref, halo0_ref, second_ref, first_rest_ref, source_ref, store_ref,
-    kinds_ref, wing_ref, cond_ref, coef_ref, live_ref, incoming_ref, emission_ref, reflect_ref,
+def inward(beside, cz):
+    place = lax.broadcasted_iota(jnp.int32, beside.shape, 0)
+    ends = [jnp.where(place == 0, pltpu.roll(beside, 1, 0), 0.0)]
+    ends += [jnp.zeros_like(beside)] * (cz // ROWS - 2)
+    ends += [jnp.where(place == ROWS - 1, pltpu.roll(beside, ROWS - 1, 0), 0.0)]
+    return jnp.concatenate(ends, axis=0)
+
+
+def third_part(
+    flags_ref, rest_ref, second_ref, first_rest_ref, source_ref, store_ref, kinds_ref, wing_ref, cond_ref, coef_ref,
+    out_ref, total_ref, dir_ref, mix_ref,
+):
+    nf, ca, cz, cr = source_ref.shape
+    partner = {0: flags_ref[1] > 0.5, ca - 1: flags_ref[2] > 0.5}
+    for f in range(nf):
+        cond = cond_ref[f]
+        wide = tall(cond, cz)
+        for a in range(ca):
+            rest = rest_ref[f, a]
+            direction = second_ref[f, a, :cz]
+            ahead = ALPHA[2] * direction + BETA[2] * rest
+            if a in partner:
+                mine = inward(cond * wing_ref[f, a], cz)
+                third = BETA[2] * wide * (direction + BETA[1] * mine)
+                rest = rest + jnp.where(tall(partner[a], cz), wide * third, 0.0)
+            out_ref[f, a] = rest
+            dir_ref[f, a, :cz] = ahead
+            total_ref[f, a] = source_ref[f, a] * INV_CENTER + direction + ahead
+
+    def wing_emit(f, a, image):
+        rest = first_rest_ref[f, a, cz:] - image
+        if a in partner:
+            cond = cond_ref[f]
+            rest = rest + jnp.where(partner[a], BETA[1] * cond * cond * wing_ref[f, a], 0.0)
+        dir_ref[f, a, cz:] = ALPHA[2] * second_ref[f, a, cz:] + BETA[2] * rest
+
+    apply_local(
+        second_ref, lambda f, a: wing_store(wing_ref, f, a), lambda a, t: wing_ref[nf + nf // 2, a],
+        cond_ref, coef_ref[...], mix_ref, (cz, cz + ROWS), wing_emit,
+    )
+
+    def emit(f, a, image):
+        out_ref[f, a] = out_ref[f, a] - image
+
+    apply_local(
+        dir_ref, lambda f, a: store_ref[f, a], lambda a, t: kinds_ref[a, t * ROWS : (t + 1) * ROWS].astype(f32),
+        cond_ref, coef_ref[...], mix_ref, (0, cz), emit,
+    )
+
+
+def later_kernel(
+    flags_ref, rest_ref, halo1_ref, halo0_ref, source_ref, store_ref, kinds_ref, wing_ref, cond_ref, coef_ref,
+    out_ref, total_ref, second_rest_ref, second_ref, dir_ref, mix_ref,
+):
+    second_part(
+        flags_ref, rest_ref, halo1_ref, halo0_ref, source_ref, store_ref, kinds_ref, wing_ref, cond_ref, coef_ref,
+        second_rest_ref, second_ref, mix_ref,
+    )
+    third_part(
+        flags_ref, second_rest_ref, second_ref, rest_ref, source_ref, store_ref, kinds_ref, wing_ref, cond_ref,
+        coef_ref, out_ref, total_ref, dir_ref, mix_ref,
+    )
+
+
+def last_kernel(
+    flags_ref, rest_ref, total_ref, halo1_ref, halo0_ref, store_ref, kinds_ref, wing_ref, cond_ref, coef_ref,
+    live_ref, incoming_ref, emission_ref, reflect_ref,
     panel_ref, solution_ref, residual_ref,
-    total_ref, out_ref, fixed_ref, dir_ref, beside_ref, mix_ref, sems,
-):
-    nf, ca, cz, cr = source_ref.shape
-    own = cz // ROWS
+    end_ref, out_ref, base_ref, fixed_ref, add_ref, beside_ref, mix_ref, sems,
+):
+    nf, ca, cz, cr = store_ref.shape
+    ends = (0, ca - 1)
+    beside_ends = (1, ca - 2)
+    copies = []
+
+    def send(near, far):
+        copies.append(pltpu.make_async_copy(near, far, sems.at[len(copies)]))
+        copies[-1].start()
+
+    send(total_ref.at[:, 1 : ca - 1], solution_ref.at[:, 1 : ca - 1])
     even = tall(flags_ref[0], 2 * cz + ROWS) > 0.5
-    partner = {0: flags_ref[1] > 0.5, ca - 1: flags_ref[2] > 0.5}
     place = lax.broadcasted_iota(jnp.int32, (ROWS, cr), 0)
     outer = (place <= 1) | (place >= 6)
-
-    def inward(beside):
-        ends = [jnp.where(place == 0, pltpu.roll(beside, 1, 0), 0.0)]
-        ends += [jnp.zeros_like(beside)] * (own - 2)
-        ends += [jnp.where(place == ROWS - 1, pltpu.roll(beside, ROWS - 1, 0), 0.0)]
-        return jnp.concatenate(ends, axis=0)
-
     for f in range(nf):
         cond = cond_ref[f]
         wide = tall(cond, cz)
-        halo = {
-            0: jnp.where(even, halo1_ref[f], halo0_ref[f]),
-            ca - 1: jnp.where(even, halo0_ref[f], halo1_ref[f]),
-        }
-        for a in range(ca):
-            rest = rest_ref[f, a]
-            wing = second_ref[f, a, cz:]
-            beside = first_rest_ref[f, a, cz:]
-            direction = second_ref[f, a, :cz]
-            if a in halo:
-                old = halo[a][2 * cz :]
-                moved = jnp.where(place < 4, pltpu.roll(old, ROWS - 2, 0), pltpu.roll(old, 2, 0))
-                fix = cond * jnp.where(outer, moved, 0.0)
-                rest = rest + wide * (halo[a][:cz] + BETA[1] * inward(fix))
-                wing = wing + BETA[1] * fix
-                mine = cond * wing_ref[f, a]
-                beyond = cond * (old + BETA[1] * mine)
-                beside = beside + fix + jnp.where(partner[a], beyond, 0.0)
-            ahead = ALPHA[2] * direction + BETA[2] * rest
-            if a in halo:
-                third = halo[a][cz : 2 * cz] + BETA[2] * wide * (direction + BETA[1] * inward(mine))
-                rest = rest + jnp.where(tall(partner[a], cz), wide * third, 0.0)
-            out_ref[f, a] = rest
-            fixed_ref[f, a, :cz] = direction
-            fixed_ref[f, a, cz:] = wing
-            beside_ref[f, a] = beside
-            dir_ref[f, a, :cz] = ahead
-            total_ref[f, a] = source_ref[f, a] * INV_CENTER + direction + ahead
-    done_solution = pltpu.make_async_copy(total_ref, solution_ref, sems.at[0])
-    done_solution.start()
+        h1, h0 = halo1_ref[f], halo0_ref[f]
+        for e, halo in enumerate((jnp.where(even, h1, h0), jnp.where(even, h0, h1))):
+            old = halo[2 * cz :]
+            moved = jnp.where(place < 4, pltpu.roll(old, ROWS - 2, 0), pltpu.roll(old, 2, 0))
+            fix = cond * jnp.where(outer, moved, 0.0)
+            rest = wide * (halo[:cz] + BETA[1] * inward(fix, cz))
+            base_ref[f, e] = rest + wide * halo[cz : 2 * cz]
+            fixed_ref[f, e, :cz] = jnp.zeros_like(rest)
+            fixed_ref[f, e, cz:] = BETA[1] * fix
+            beside_ref[f, e] = fix + cond * old
+            add_ref[f, e, :cz] = BETA[2] * rest
+            end_ref[e, f] = total_ref[f, ends[e]] + BETA[2] * rest
+    for e in range(2):
+        send(end_ref.at[e], solution_ref.at[:, ends[e]])
 
     slots, values = panel_ref.shape
-    wall = total_ref[0].reshape(ca * cz, cr)[:, cr - 1 : cr]
+    wall = [end_ref[0, 0]] + [total_ref[0, a] for a in range(1, ca - 1)] + [end_ref[1, 0]]
+    wall = jnp.concatenate(wall, axis=0)[:, cr - 1 : cr]
     wall = jnp.broadcast_to(wall, (ca * cz, values))
     wall = jnp.concatenate([wall] * (-(-slots // (ca * cz))), axis=0)[:slots]
     panel = lax.broadcasted_iota(jnp.int32, (slots, values), 0)
     fresh = emission_ref[...] * wall + reflect_ref[...] * incoming_ref[:slots]
     panel_ref[...] = jnp.where(panel < live_ref[:1], fresh, 0.0)
 
-    def wing_emit(f, a, image):
-        dir_ref[f, a, cz:] = ALPHA[2] * fixed_ref[f, a, cz:] + BETA[2] * (beside_ref[f, a] - image)
+    def wing_emit(f, e, image):
+        add_ref[f, e, cz:] = ALPHA[2] * fixed_ref[f, e, cz:] + BETA[2] * (beside_ref[f, e] - image)
 
     apply_local(
-        fixed_ref, lambda f, a: wing_store(wing_ref, f, a), lambda a, t: wing_ref[nf + nf // 2, a],
-        cond_ref, coef_ref[...], mix_ref, (cz, cz + ROWS), wing_emit,
-    )
-
-    def emit(f, a, image):
-        out_ref[f, a] = out_ref[f, a] - image
+        fixed_ref, lambda f, e: wing_store(wing_ref, f, ends[e]), lambda e, t: wing_ref[nf + nf // 2, ends[e]],
+        cond_ref, coef_ref[...], mix_ref, (cz, cz + ROWS), wing_emit, linked=False,
+    )
+
+    def emit(f, e, image):
+        cond = cond_ref[f]
+        out_ref[f, ends[e]] = rest_ref[f, ends[e]] + base_ref[f, e] - image
+        inner = add_ref[f, e, :cz] + inward(BETA[2] * cond * fixed_ref[f, e, cz:], cz)
+        out_ref[f, beside_ends[e]] = rest_ref[f, beside_ends[e]] + tall(cond, cz) * inner
+        if e == 1:
+            for a in range(2, ca - 2):
+                out_ref[f, a] = rest_ref[f, a]
+            if f % GROUP == GROUP - 1:
+                some = pl.ds(f + 1 - GROUP, GROUP)
+                send(out_ref.at[some], residual_ref.at[some])
 
     apply_local(
-        dir_ref, lambda f, a: store_ref[f, a], lambda a, t: kinds_ref[a, t * ROWS : (t + 1) * ROWS].astype(f32),
-        cond_ref, coef_ref[...], mix_ref, (0, cz), emit,
-    )
-    done_residual = pltpu.make_async_copy(out_ref, residual_ref, sems.at[1])
-    done_residual.start()
-    done_solution.wait()
-    done_residual.wait()
+        add_ref, lambda f, e: store_ref[f, ends[e]],
+        lambda e, t: kinds_ref[ends[e], t * ROWS : (t + 1) * ROWS].astype(f32),
+        cond_ref, coef_ref[...], mix_ref, (0, cz), emit, linked=False,
+    )
+    for copy in copies:
+        copy.wait()
 
 
 def panel_kernel(
@@ -385,6 +459,10 @@
         for k in range(visible):
             out = out + moved[k * slots : (k + 1) * slots]
     out_ref[...] = out
+
+
+def relay_kernel(flags_ref, out_ref):
+    out_ref[...] = flags_ref[...]
 
 
 def pairs(count, first, closed):
@@ -434,16 +512,19 @@
 
     plain = here((nf, ca, cz, cr), f32)
     layers = here((2, nf, cz, cr), f32)
-    source, storage, materials, edges, sides = pl.pallas_call(
+    small = (conductance[None], mixing.transpose(1, 0, 2))
+    values = radiosity_old.shape[3]
+    source, storage, materials, edges, sides, cond, coef = pl.pallas_call(
         ends_kernel,
         out_shape=(
-            plain, plain, here((ca, cz, cr), jnp.int32), layers, here((nf + nf // 2 + 1, ca, ROWS, cr), f32)
+            plain, plain, here((ca, cz, cr), jnp.int32), layers, here((nf + nf // 2 + 1, ca, ROWS, cr), f32),
+            here((nf, ROWS, cr), f32), here((mats * nf * ROWS, 3 * nf * ROWS), bf16),
         ),
-        in_specs=[VMEM] + [HBM] * 3,
-        out_specs=(VMEM,) * 5,
-        scratch_shapes=[pltpu.SemaphoreType.DMA((2 * COPIES + 1,))],
+        in_specs=[VMEM] + [HBM] * 5,
+        out_specs=(VMEM,) * 7,
+        scratch_shapes=[here(x.shape, x.dtype) for x in small] + [pltpu.SemaphoreType.DMA((2 * COPIES + 3,))],
         compiler_params=PARAMS, cost_estimate=CHEAP,
-    )(flags, *(pltpu.with_memory_space_constraint(x, pltpu.HBM) for x in (source, storage, materials)))
+    )(flags, *(pltpu.with_memory_space_constraint(x, pltpu.HBM) for x in (source, storage, materials, *small)))
     half = ROWS // 2
     to_right, to_left = sides[:, :, half:], sides[:, :, :half]
     far = jnp.where(azim_even, to_left, to_right).astype(LINK)
@@ -454,7 +535,6 @@
     near_in = swap(after(near, message1), "azim", 0)
 
     slots, visible = vis_owner.shape[2:]
-    values = radiosity_old.shape[3]
     tile = -(-slots // 16) * 16
     panels = jnp.pad(radiosity_old[0, 0], ((0, tile - slots), (0, 0)))
     fold = cr // values
@@ -467,19 +547,16 @@
     from_left = jnp.where(azim_even, far_in, near_in)
     wings = jnp.concatenate([from_right, from_left], axis=2).astype(f32)
 
-    cond = jnp.broadcast_to(conductance[:, None, None], (nf, ROWS, cr))
-    mixes = mixing + 6.0 * jnp.diag(conductance)
-    mixes = jnp.pad(mixes.reshape(mats * nf, nf), ((0, 0), (0, 128 - nf)))
-    coef = call(coef_kernel, (here((mats * nf * ROWS, 3 * nf * ROWS), bf16),), (mixes,))
     full = here((nf, ca, cz + ROWS, cr), f32)
     rest = call(first_kernel, (full,), (source, storage, materials, wings, cond, coef), (full, full))
 
     def side(first, halo):
+        one = here((nf, 1, cz + ROWS, cr), f32)
         return call(
             functools.partial(side_kernel, first),
             (here((nf, 2 * cz + ROWS, cr), f32),),
             (flags, rest, halo, source, storage, materials, wings, cond, coef),
-            (here((nf, 1, cz + ROWS, cr), f32), here((nf, cz, cr), f32), here((nf, 1, cz + ROWS, cr), f32)),
+            (one, here((nf, cz, cr), f32), one),
         ).astype(LINK)
 
     halo1 = after(halo1, rest).astype(f32)
@@ -489,22 +566,21 @@
     halo0 = message[: nf * cz].reshape(nf, cz, cr).astype(f32)
     message0 = side(False, halo0)
     second0 = swap(message0, "axial", 0).astype(f32)
-
-    rest2, dir2 = call(
-        second_kernel,
-        (plain, full),
+    rest3, total = call(
+        later_kernel,
+        (plain, plain),
         (flags, after(rest, message0), halo1, halo0, source, storage, materials, wings, cond, coef),
-        (full,),
-    )
-
-    partner = after(message, rest2)[nf * cz :].astype(f32) * (1.0 / RAD_SCALE)
+        (plain, full, full, full),
+    )
+
+    partner = after(message, message0)[nf * cz :].astype(f32) * (1.0 / RAD_SCALE)
     partner = jnp.concatenate(jnp.split(partner, fold, axis=1), axis=0).astype(bf16)
     if owners <= 8 and owners & (owners - 1) == 0:
         pair = jnp.concatenate([panels, partner], axis=0)
         others = [
             lax.ppermute(pair, "axial", [(i, i ^ step) for i in range(owners)]) for step in range(2, owners, 2)
         ]
-        panels = jnp.concatenate([pair, *others], axis=0)
+        panels = jnp.concatenate([after(pair, second1), *others], axis=0)
         owner = vis_owner[0, 0].T ^ me
     else:
         pair = jnp.stack([panels, partner])
@@ -524,19 +600,22 @@
         plain_args=True,
     )
 
-    live = jnp.broadcast_to(counts, (ROWS, values))
+    live = jnp.broadcast_to(after(counts, rest3), (ROWS, values))
+    checked = call(relay_kernel, (here(flags.shape, f32),), (after(flags, second0),))
     shape = jax.ShapeDtypeStruct
+    pair_full = here((nf, 2, cz + ROWS, cr), f32)
     panel_new, solution_out, residual = pl.pallas_call(
-        third_kernel,
-        out_shape=(shape((slots, values), f32), shape(source.shape, f32), shape(source.shape, f32)),
-        in_specs=[VMEM] * 16,
+        last_kernel,
+        out_shape=(shape((slots, values), f32), shape(plain.shape, f32), shape(plain.shape, f32)),
+        in_specs=[VMEM] * 14,
         out_specs=(VMEM, HBM, HBM),
         scratch_shapes=[
-            plain, plain, full, full, here((nf, ca, ROWS, cr), f32), full, pltpu.SemaphoreType.DMA((2,))
+            layers, plain, here((nf, 2, cz, cr), f32), pair_full, pair_full, here((nf, 2, ROWS, cr), f32), pair_full,
+            pltpu.SemaphoreType.DMA((3 + nf // GROUP,)),
         ],
         compiler_params=PARAMS, cost_estimate=CHEAP,
     )(
-        flags, rest2, second1, second0, dir2, rest, source, storage, materials, wings, cond, coef,
+        checked, rest3, total, second1, second0, storage, materials, wings, cond, coef,
         live, incoming, emission[0, 0], reflect[0, 0],
     )
     return (solution_out, residual, panel_new[None, None])

time: 36.8 us -> 34.7 us (0.943)
  waiting for transfers between devices: 4.78 us -> 3.51 us
  Pallas kernels: 11.8 us -> 11.4 us
    ppermute x3, waiting for transfers between devices: 4.76 us -> 2.07 us  [body(): lax.ppermute(pair, 'axial', [(i, i ^ step) for i in range(owners)])]
    ppermute x6, waiting for transfers between devices: 0.02 us -> 1.43 us  [swap(): return lax.ppermute(array, axis, pairs(lax.axis_size(axis), first, closed))]
    pallas_call x1, Pallas kernels: 3.92 us -> 2.66 us  [body(): pl.pallas_call(last_kernel, out_shape=(shape((slots, values), f32), shape...]
    pallas_call x6, Pallas kernels: 6.26 us -> 7.16 us  [call(): pl.pallas_call(kernel, out_shape=outs[0] if single else tuple(outs), in_s...]
  transfers between devices with their start and end apart: 9 -> 9, of which waited for: 2 -> 3; matrix products, arithmetic and copies ran while one was open for 2% -> 2% of each run, Pallas kernels for 17% -> 18%
where the time goes in v4:
time: 34.7 us; the launch traced here: 34.5 us
  starting transfers between devices  17 us (49%)
  Pallas kernels  11.4 us (33%)
  waiting for transfers between devices  3.51 us (10%)
  between operations  1.65 us (5%)
  other arithmetic  0.76 us (2%)
    ppermute x6, starting transfers between devices, swap(): return lax.ppermute(array, axis, pairs(lax.axis_size(axis), first, closed))  12.5 us
    pallas_call x6, Pallas kernels, call(): pl.pallas_call(kernel, out_shape=outs[0] if single else tuple(outs), in_s...  7.16 us
    ppermute x3, starting transfers between devices, body(): lax.ppermute(pair, 'axial', [(i, i ^ step) for i in range(owners)])  4.45 us
    pallas_call x1, Pallas kernels, body(): pl.pallas_call(last_kernel, out_shape=(shape((slots, values), f32), shape...  2.66 us
    ppermute x3, waiting for transfers between devices, body(): lax.ppermute(pair, 'axial', [(i, i ^ step) for i in range(owners)])  2.07 us
    pallas_call x1, Pallas kernels, body(): pl.pallas_call(ends_kernel, out_shape=(plain, plain, here((ca, cz, cr), j...  1.63 us
    ppermute x6, waiting for transfers between devices, swap(): return lax.ppermute(array, axis, pairs(lax.axis_size(axis), first, closed))  1.43 us
  transfers between devices with their start and end apart: 9, of which 3 were waited for; matrix products, arithmetic and copies ran while one was open for 2% of the time, Pallas kernels for 18%

profile of v4, /device:TPU:0, one launch (start us, length us, event | category | flops | bytes accessed | tf_op | source)
XLA Modules:
  0.0 34.5 jit_solution(6675786657227375612)
XLA Ops:
  0.7 0.1 add_convert_fusion
  0.7 0.1 broadcast_in_dim.19.flags_ref
  0.8 1.6 %shard_map.148 = (f32[12,4,16,256]{3,2,1,0:T(8,128)S(1)}, f32[12,4,16,256]{3,2,1,0:T(8,128)S(1)}, s32[4,16,256]{2,1,0:T(8,128)S(1)}, f32[2,12,16,256]{3,2,1,0:T(...) custom-call(f32[3,8,256]{2,1,0:T(8,128)S(1)} %broadcast_in_dim.19.flags_ref, ...), custom_call_target="tpu_custom_call" | custom-call | tf_op jit(solution)/shard_map/pallas_call | solution.py:517
  2.4 0.0 copy-start.3
  2.5 0.2 select_convert_fusion.1
  2.6 2.5 %collective-permute-start.1 = (f16[19,4,4,256]{3,2,1,0:T(4,128)(2,1)S(1)}, f16[19,4,4,256]{3,2,1,0:T(4,128)(2,1)S(1)}, u32[]{:S(2)}, u32[]{:S(2)}) collective-permute-start(f16[19,4,4,256]{3,2,1,0:T(4,128)(2,1)S(1)} %get-tuple-element.48), channel_id=1, source_target_pairs={{1,2},{2,1},{3,0},{0,3},{5,6},{6,5},{7,4},{4,7},{9,10},{10,9},{11,... | collective-permute-start | bytes 466952 | tf_op jit(solution)/shard_map/ppermute | solution.py:477
  5.1 0.7 %collective-permute-start.3 = (f16[12,16,256]{2,1,0:T(8,128)(2,1)S(1)}, f16[12,16,256]{2,1,0:T(8,128)(2,1)S(1)}, u32[]{:S(2)}, u32[]{:S(2)}) collective-permute-start(f16[12,16,256]{2,1,0:T(8,128)(2,1)S(1)} %fusion), channel_id=1, source_target_pairs={{4,8},{8,4},{12,16},{16,12},{20,24},{24,20},{5,9},{9,5},{13,17},{1... | collective-permute-start | bytes 294920 | tf_op jit(solution)/shard_map/ppermute | solution.py:477
  5.8 0.7 %collective-permute-start = (f16[19,4,4,256]{3,2,1,0:T(4,128)(2,1)S(1)}, f16[19,4,4,256]{3,2,1,0:T(4,128)(2,1)S(1)}, u32[]{:S(2)}, u32[]{:S(2)}) collective-permute-start(f16[19,4,4,256]{3,2,1,0:T(4,128)(2,1)S(1)} %get-tuple-element.31), channel_id=1, source_target_pairs={{0,1},{1,0},{2,3},{3,2},{4,5},{5,4},{6,7},{7,6},{8,9},{9,8},{10,11... | collective-permute-start | bytes 466952 | tf_op jit(solution)/shard_map/ppermute | solution.py:477
  6.6 0.0 copy-done.3
  6.6 4.1 %collective-permute-start.2 = (f16[256,256]{1,0:T(8,128)(2,1)S(1)}, f16[256,256]{1,0:T(8,128)(2,1)S(1)}, u32[]{:S(2)}, u32[]{:S(2)}) collective-permute-start(f16[256,256]{1,0:T(8,128)(2,1)S(1)} %maximum_maximum_fusion), channel_id=1, source_target_pairs={{0,4},{4,0},{8,12},{12,8},{16,20},{20,16},{24,28},{28,24},{1,5},{5... | collective-permute-start | bytes 393224 | tf_op jit(solution)/shard_map/ppermute | solution.py:477
  10.7 0.0 collective-permute-done
  10.7 0.0 collective-permute-done.1
  10.7 0.1 broadcast_select_fusion.1
  10.8 0.1 maximum_convert_fusion.wing_ref
  11.0 1.8 %shard_map.149.rest_ref = f32[12,4,24,256]{3,2,1,0:T(8,128)S(1)} custom-call(f32[12,4,16,256]{3,2,1,0:T(8,128)S(1)} %get-tuple-element.25.source_ref, f32[12,4,16,256]{3,2,1,0:T(8,128)S(1)} %get-tuple-element.26.store_ref, s32[4,16,256]{2,1,0:T(8,128)S(1)} %get-tuple-element.27.kinds_ref, f32[19,4,8,256]{3,2,1,0:T(8,128)S(1)} %maximum_convert_fusion.wing_ref, ...), custom_call_target="tpu_custom_call" | custom-call | tf_op jit(solution)/shard_map/pallas_call | solution.py:501
  12.8 0.0 collective-permute-done.3
  12.8 0.5 %shard_map.150 = f32[12,40,256]{2,1,0:T(8,128)S(1)} custom-call(f32[3,8,256]{2,1,0:T(8,128)S(1)} %broadcast_in_dim.19.flags_ref, f32[12,4,24,256]{3,2,1,0:T(8,128)S(1)} %shard_map.149.rest_ref, f32[12,16,256]{2,1,0:T(8,128)S(1)} %convert_element_type.56.halo_ref.halo1_ref, f32[12,4,16,256]{3,2,1,0:T(8,128)S(1)} %get-tuple-element.25.source_ref, ...), custom_call_target="tpu_custom_call" | custom-call | tf_op jit(solution)/shard_map/pallas_call | solution.py:501
  13.4 0.7 %collective-permute-start.5 = (f16[12,40,256]{2,1,0:T(8,128)(2,1)S(1)}, f16[12,40,256]{2,1,0:T(8,128)(2,1)S(1)}, u32[]{:S(2)}, u32[]{:S(2)}) collective-permute-start(f16[12,40,256]{2,1,0:T(8,128)(2,1)S(1)} %convert_element_type.57), channel_id=1, source_target_pairs={{4,8},{8,4},{12,16},{16,12},{20,24},{24,20},{5,9},{9,5},{13,17},{1... | collective-permute-start | bytes 737288 | tf_op jit(solution)/shard_map/ppermute | solution.py:477
  14.1 1.0 %collective-permute-done.2 = f16[256,256]{1,0:T(8,128)(2,1)S(1)} collective-permute-done((f16[256,256]{1,0:T(8,128)(2,1)S(1)}, f16[256,256]{1,0:T(8,128)(2,1)S(1)}, u32[]{:S(2)}, u32[]{:S(2)}) %collective-permute-start.2) | collective-permute-done | bytes 131104 | tf_op jit(solution)/shard_map/ppermute | solution.py:477
  15.2 0.0 copy-start.4
  15.2 0.0 copy-start.5
  15.2 0.0 copy-start.6
  15.2 0.5 %shard_map.151 = f32[12,40,256]{2,1,0:T(8,128)S(1)} custom-call(f32[3,8,256]{2,1,0:T(8,128)S(1)} %broadcast_in_dim.19.flags_ref, f32[12,4,24,256]{3,2,1,0:T(8,128)S(1)} %shard_map.149.rest_ref, f32[12,16,256]{2,1,0:T(8,128)S(1)} %convert.26.halo_ref.halo0_ref, f32[12,4,16,256]{3,2,1,0:T(8,128)S(1)} %get-tuple-element.25.source_ref, ...), custom_call_target="tpu_custom_call" | custom-call | tf_op jit(solution)/shard_map/pallas_call | solution.py:501
  15.7 3.9 %collective-permute-start.4 = (f16[12,40,256]{2,1,0:T(8,128)(2,1)S(1)}, f16[12,40,256]{2,1,0:T(8,128)(2,1)S(1)}, u32[]{:S(2)}, u32[]{:S(2)}) collective-permute-start(f16[12,40,256]{2,1,0:T(8,128)(2,1)S(1)} %convert_element_type.60), channel_id=1, source_target_pairs={{0,4},{4,0},{8,12},{12,8},{16,20},{20,16},{24,28},{28,24},{1,5},{5... | collective-permute-start | bytes 737288 | tf_op jit(solution)/shard_map/ppermute | solution.py:477
  19.7 1.6 %collective-permute-start.6 = (bf16[256,128]{1,0:T(8,128)(2,1)S(1)}, bf16[256,128]{1,0:T(8,128)(2,1)S(1)}, u32[]{:S(2)}, u32[]{:S(2)}) collective-permute-start(bf16[256,128]{1,0:T(8,128)(2,1)S(1)} %pad_maximum_fusion.1), channel_id=1, source_target_pairs={{0,8},{4,12},{8,0},{12,4},{16,24},{20,28},{24,16},{28,20},{1,9},{5... | collective-permute-start | bytes 196616 | tf_op jit(solution)/shard_map/ppermute | solution.py:581
  21.3 1.1 %collective-permute-start.7 = (bf16[256,128]{1,0:T(8,128)(2,1)S(1)}, bf16[256,128]{1,0:T(8,128)(2,1)S(1)}, u32[]{:S(2)}, u32[]{:S(2)}) collective-permute-start(bf16[256,128]{1,0:T(8,128)(2,1)S(1)} %pad_maximum_fusion.1), channel_id=1, source_target_pairs={{0,16},{4,20},{8,24},{12,28},{16,0},{20,4},{24,8},{28,12},{1,17},{... | collective-permute-start | bytes 196616 | tf_op jit(solution)/shard_map/ppermute | solution.py:581
  22.4 1.7 %collective-permute-start.8 = (bf16[256,128]{1,0:T(8,128)(2,1)S(1)}, bf16[256,128]{1,0:T(8,128)(2,1)S(1)}, u32[]{:S(2)}, u32[]{:S(2)}) collective-permute-start(bf16[256,128]{1,0:T(8,128)(2,1)S(1)} %pad_maximum_fusion.1), channel_id=1, source_target_pairs={{0,24},{4,28},{8,16},{12,20},{16,8},{20,12},{24,0},{28,4},{1,25},{... | collective-permute-start | bytes 196616 | tf_op jit(solution)/shard_map/ppermute | solution.py:581
  24.1 0.0 copy-done.4
  24.1 0.0 copy-done.5
  24.2 0.0 copy-done.6
  24.8 3.3 %shard_map.153 = (f32[12,4,16,256]{3,2,1,0:T(8,128)S(1)}, f32[12,4,16,256]{3,2,1,0:T(8,128)S(1)}) custom-call(f32[3,8,256]{2,1,0:T(8,128)S(1)} %broadcast_in_dim.19.flags_ref, f32[12,4,24,256]{3,2,1,0:T(8,128)S(1)} %shard_map.149.rest_ref, f32[12,16,256]{2,1,0:T(8,128)S(1)} %convert_element_type.56.halo_ref.halo1_ref, ...), custom_call_target="tpu_custom_call" | custom-call | tf_op jit(solution)/shard_map/pallas_call | solution.py:501
  28.1 0.0 copy-start
  28.1 0.0 copy-start.1
  28.2 0.0 copy-start.2
  28.2 0.0 collective-permute-done.5
  28.2 0.4 %collective-permute-done.4 = f16[12,40,256]{2,1,0:T(8,128)(2,1)S(1)} collective-permute-done((f16[12,40,256]{2,1,0:T(8,128)(2,1)S(1)}, f16[12,40,256]{2,1,0:T(8,128)(2,1)S(1)}, u32[]{:S(2)}, u32[]{:S(2)}) %collective-permute-start.4) | collective-permute-done | bytes 245792 | tf_op jit(solution)/shard_map/ppermute | solution.py:477
  28.7 0.0 collective-permute-done.6
  28.7 0.0 collective-permute-done.7
  28.7 2.1 %collective-permute-done.8 = bf16[256,128]{1,0:T(8,128)(2,1)S(1)} collective-permute-done((bf16[256,128]{1,0:T(8,128)(2,1)S(1)}, bf16[256,128]{1,0:T(8,128)(2,1)S(1)}, u32[]{:S(2)}, u32[]{:S(2)}) %collective-permute-start.8) | collective-permute-done | bytes 65568 | tf_op jit(solution)/shard_map/ppermute | solution.py:581
  30.8 0.0 copy-done
  30.8 1.0 %shard_map.154.incoming_ref = f32[128,128]{1,0:T(8,128)S(1)} custom-call(s32[8,128]{1,0:T(8,128)S(1)} %pad.12.index_ref, s32[8,128]{1,0:T(8,128)S(1)} %pad.13.block_ref, bf16[1024,128]{1,0:T(8,128)(2,1)S(1)} %pad_maximum_fusion.rows_ref, bf16[8,128,128]{2,1,0:T(8,128)(2,1)S(1)} %copy-done), custom_call_target="tpu_custom_call" | custom-call | tf_op jit(solution)/shard_map/pallas_call | solution.py:501
  31.8 0.0 copy-done.1
  31.8 0.0 copy-done.2
  31.9 2.7 %shard_map.155 = (f32[120,128]{1,0:T(8,128)}, f32[12,4,16,256]{3,2,1,0:T(8,128)}, f32[12,4,16,256]{3,2,1,0:T(8,128)}) custom-call(f32[3,8,256]{2,1,0:T(8,128)S(1)} %shard_map.152.flags_ref, f32[12,4,16,256]{3,2,1,0:T(8,128)S(1)} %get-tuple-element.39.rest_ref, f32[12,4,16,256]{3,2,1,0:T(8,128)S(1)} %get-tuple-element.40.total_ref, ...), custom_call_target="tpu_custom_call" | custom-call | tf_op jit(solution)/shard_map/pallas_call | solution.py:607
  (22 shorter events, 0.3 us)
Async XLA Ops:
  2.4 4.1 %copy-start.3 = (bf16[1,1,120,128]{3,2,1,0:T(8,128)(2,1)S(1)}, bf16[1,1,120,128]{3,2,1,0:T(8,128)(2,1)}, u32[]{:S(2)}) copy-start(bf16[1,1,120,128]{3,2,1,0:T(8,128)(2,1)} %param.22) | copy-start | bytes 92164
  2.6 8.1 %collective-permute-start.1 = (f16[19,4,4,256]{3,2,1,0:T(4,128)(2,1)S(1)}, f16[19,4,4,256]{3,2,1,0:T(4,128)(2,1)S(1)}, u32[]{:S(2)}, u32[]{:S(2)}) collective-permute-start(f16[19,4,4,256]{3,2,1,0:T(4,128)(2,1)S(1)} %get-tuple-element.48), channel_id=1, source_target_pairs={{1,2},{2,1},{3,0},{0,3},{5,6},{6,5},{7,4},{4,7},{9,10},{10,9},{11,... | collective-permute-start | bytes 466952 | tf_op jit(solution)/shard_map/ppermute | solution.py:477
  5.1 7.7 %collective-permute-start.3 = (f16[12,16,256]{2,1,0:T(8,128)(2,1)S(1)}, f16[12,16,256]{2,1,0:T(8,128)(2,1)S(1)}, u32[]{:S(2)}, u32[]{:S(2)}) collective-permute-start(f16[12,16,256]{2,1,0:T(8,128)(2,1)S(1)} %fusion), channel_id=1, source_target_pairs={{4,8},{8,4},{12,16},{16,12},{20,24},{24,20},{5,9},{9,5},{13,17},{1... | collective-permute-start | bytes 294920 | tf_op jit(solution)/shard_map/ppermute | solution.py:477
  5.8 4.9 %collective-permute-start = (f16[19,4,4,256]{3,2,1,0:T(4,128)(2,1)S(1)}, f16[19,4,4,256]{3,2,1,0:T(4,128)(2,1)S(1)}, u32[]{:S(2)}, u32[]{:S(2)}) collective-permute-start(f16[19,4,4,256]{3,2,1,0:T(4,128)(2,1)S(1)} %get-tuple-element.31), channel_id=1, source_target_pairs={{0,1},{1,0},{2,3},{3,2},{4,5},{5,4},{6,7},{7,6},{8,9},{9,8},{10,11... | collective-permute-start | bytes 466952 | tf_op jit(solution)/shard_map/ppermute | solution.py:477
  6.6 8.5 %collective-permute-start.2 = (f16[256,256]{1,0:T(8,128)(2,1)S(1)}, f16[256,256]{1,0:T(8,128)(2,1)S(1)}, u32[]{:S(2)}, u32[]{:S(2)}) collective-permute-start(f16[256,256]{1,0:T(8,128)(2,1)S(1)} %maximum_maximum_fusion), channel_id=1, source_target_pairs={{0,4},{4,0},{8,12},{12,8},{16,20},{20,16},{24,28},{28,24},{1,5},{5... | collective-permute-start | bytes 393224 | tf_op jit(solution)/shard_map/ppermute | solution.py:477
  13.4 14.8 %collective-permute-start.5 = (f16[12,40,256]{2,1,0:T(8,128)(2,1)S(1)}, f16[12,40,256]{2,1,0:T(8,128)(2,1)S(1)}, u32[]{:S(2)}, u32[]{:S(2)}) collective-permute-start(f16[12,40,256]{2,1,0:T(8,128)(2,1)S(1)} %convert_element_type.57), channel_id=1, source_target_pairs={{4,8},{8,4},{12,16},{16,12},{20,24},{24,20},{5,9},{9,5},{13,17},{1... | collective-permute-start | bytes 737288 | tf_op jit(solution)/shard_map/ppermute | solution.py:477
  15.2 9.0 %copy-start.4 = (s32[1,1,120,4]{2,3,1,0:T(4,128)S(1)}, s32[1,1,120,4]{2,3,1,0:T(4,128)}, u32[]{:S(2)}) copy-start(s32[1,1,120,4]{2,3,1,0:T(4,128)} %param.20) | copy-start | bytes 5764
  15.2 9.0 %copy-start.5 = (s32[1,1,120,4]{2,3,1,0:T(4,128)S(1)}, s32[1,1,120,4]{2,3,1,0:T(4,128)}, u32[]{:S(2)}) copy-start(s32[1,1,120,4]{2,3,1,0:T(4,128)} %param.19) | copy-start | bytes 5764
  15.2 9.0 %copy-start.6 = (s32[1,1,120,4]{2,3,1,0:T(4,128)S(1)}, s32[1,1,120,4]{2,3,1,0:T(4,128)}, u32[]{:S(2)}) copy-start(s32[1,1,120,4]{2,3,1,0:T(4,128)} %param.21) | copy-start | bytes 5764
  15.7 12.9 %collective-permute-start.4 = (f16[12,40,256]{2,1,0:T(8,128)(2,1)S(1)}, f16[12,40,256]{2,1,0:T(8,128)(2,1)S(1)}, u32[]{:S(2)}, u32[]{:S(2)}) collective-permute-start(f16[12,40,256]{2,1,0:T(8,128)(2,1)S(1)} %convert_element_type.60), channel_id=1, source_target_pairs={{0,4},{4,0},{8,12},{12,8},{16,20},{20,16},{24,28},{28,24},{1,5},{5... | collective-permute-start | bytes 737288 | tf_op jit(solution)/shard_map/ppermute | solution.py:477
  19.7 9.0 %collective-permute-start.6 = (bf16[256,128]{1,0:T(8,128)(2,1)S(1)}, bf16[256,128]{1,0:T(8,128)(2,1)S(1)}, u32[]{:S(2)}, u32[]{:S(2)}) collective-permute-start(bf16[256,128]{1,0:T(8,128)(2,1)S(1)} %pad_maximum_fusion.1), channel_id=1, source_target_pairs={{0,8},{4,12},{8,0},{12,4},{16,24},{20,28},{24,16},{28,20},{1,9},{5... | collective-permute-start | bytes 196616 | tf_op jit(solution)/shard_map/ppermute | solution.py:581
  21.3 7.3 %collective-permute-start.7 = (bf16[256,128]{1,0:T(8,128)(2,1)S(1)}, bf16[256,128]{1,0:T(8,128)(2,1)S(1)}, u32[]{:S(2)}, u32[]{:S(2)}) collective-permute-start(bf16[256,128]{1,0:T(8,128)(2,1)S(1)} %pad_maximum_fusion.1), channel_id=1, source_target_pairs={{0,16},{4,20},{8,24},{12,28},{16,0},{20,4},{24,8},{28,12},{1,17},{... | collective-permute-start | bytes 196616 | tf_op jit(solution)/shard_map/ppermute | solution.py:581
  22.4 8.3 %collective-permute-start.8 = (bf16[256,128]{1,0:T(8,128)(2,1)S(1)}, bf16[256,128]{1,0:T(8,128)(2,1)S(1)}, u32[]{:S(2)}, u32[]{:S(2)}) collective-permute-start(bf16[256,128]{1,0:T(8,128)(2,1)S(1)} %pad_maximum_fusion.1), channel_id=1, source_target_pairs={{0,24},{4,28},{8,16},{12,20},{16,8},{20,12},{24,0},{28,4},{1,25},{... | collective-permute-start | bytes 196616 | tf_op jit(solution)/shard_map/ppermute | solution.py:581
  28.1 2.6 %copy-start = (bf16[8,128,128]{2,1,0:T(8,128)(2,1)S(1)}, bf16[8,128,128]{2,1,0:T(8,128)(2,1)}, u32[]{:S(2)}) copy-start(bf16[8,128,128]{2,1,0:T(8,128)(2,1)} %view_ref.1) | copy-start | bytes 786436
  28.1 3.7 %copy-start.1 = (f32[1,1,120,128]{3,2,1,0:T(8,128)S(1)}, f32[1,1,120,128]{3,2,1,0:T(8,128)}, u32[]{:S(2)}) copy-start(f32[1,1,120,128]{3,2,1,0:T(8,128)} %param.24) | copy-start | bytes 184324
  28.2 3.7 %copy-start.2 = (f32[1,1,120,128]{3,2,1,0:T(8,128)S(1)}, f32[1,1,120,128]{3,2,1,0:T(8,128)}, u32[]{:S(2)}) copy-start(f32[1,1,120,128]{3,2,1,0:T(8,128)} %param.25) | copy-start | bytes 184324

commit v5 on v4

--- a/solution.py
+++ b/solution.py
@@ -343,76 +343,127 @@
     )
 
 
-def last_kernel(
-    flags_ref, rest_ref, total_ref, halo1_ref, halo0_ref, store_ref, kinds_ref, wing_ref, cond_ref, coef_ref,
-    live_ref, incoming_ref, emission_ref, reflect_ref,
-    panel_ref, solution_ref, residual_ref,
-    end_ref, out_ref, base_ref, fixed_ref, add_ref, beside_ref, mix_ref, sems,
+def end_part(
+    first, flags_ref, halo_ref, store_ref, kinds_ref, wing_ref, cond_ref, coef_ref,
+    delta_ref, base_ref, fixed_ref, add_ref, beside_ref, mix_ref, early, emit,
 ):
     nf, ca, cz, cr = store_ref.shape
-    ends = (0, ca - 1)
-    beside_ends = (1, ca - 2)
-    copies = []
-
-    def send(near, far):
-        copies.append(pltpu.make_async_copy(near, far, sems.at[len(copies)]))
-        copies[-1].start()
-
-    send(total_ref.at[:, 1 : ca - 1], solution_ref.at[:, 1 : ca - 1])
-    even = tall(flags_ref[0], 2 * cz + ROWS) > 0.5
+    even = flags_ref[0] > 0.5
+
+    def choose(low, high):
+        mask = tall(even, low.shape[0])
+        return jnp.where(mask, low, high) if first else jnp.where(mask, high, low)
+
     place = lax.broadcasted_iota(jnp.int32, (ROWS, cr), 0)
     outer = (place <= 1) | (place >= 6)
     for f in range(nf):
         cond = cond_ref[f]
         wide = tall(cond, cz)
-        h1, h0 = halo1_ref[f], halo0_ref[f]
-        for e, halo in enumerate((jnp.where(even, h1, h0), jnp.where(even, h0, h1))):
-            old = halo[2 * cz :]
-            moved = jnp.where(place < 4, pltpu.roll(old, ROWS - 2, 0), pltpu.roll(old, 2, 0))
-            fix = cond * jnp.where(outer, moved, 0.0)
-            rest = wide * (halo[:cz] + BETA[1] * inward(fix, cz))
-            base_ref[f, e] = rest + wide * halo[cz : 2 * cz]
-            fixed_ref[f, e, :cz] = jnp.zeros_like(rest)
-            fixed_ref[f, e, cz:] = BETA[1] * fix
-            beside_ref[f, e] = fix + cond * old
-            add_ref[f, e, :cz] = BETA[2] * rest
-            end_ref[e, f] = total_ref[f, ends[e]] + BETA[2] * rest
-    for e in range(2):
-        send(end_ref.at[e], solution_ref.at[:, ends[e]])
-
-    slots, values = panel_ref.shape
-    wall = [end_ref[0, 0]] + [total_ref[0, a] for a in range(1, ca - 1)] + [end_ref[1, 0]]
-    wall = jnp.concatenate(wall, axis=0)[:, cr - 1 : cr]
-    wall = jnp.broadcast_to(wall, (ca * cz, values))
-    wall = jnp.concatenate([wall] * (-(-slots // (ca * cz))), axis=0)[:slots]
-    panel = lax.broadcasted_iota(jnp.int32, (slots, values), 0)
-    fresh = emission_ref[...] * wall + reflect_ref[...] * incoming_ref[:slots]
-    panel_ref[...] = jnp.where(panel < live_ref[:1], fresh, 0.0)
-
-    def wing_emit(f, e, image):
-        add_ref[f, e, cz:] = ALPHA[2] * fixed_ref[f, e, cz:] + BETA[2] * (beside_ref[f, e] - image)
+        old = halo_ref[f, 2 * cz :]
+        moved = jnp.where(place < 4, pltpu.roll(old, ROWS - 2, 0), pltpu.roll(old, 2, 0))
+        fix = cond * jnp.where(outer, moved, 0.0)
+        rest = wide * (halo_ref[f, :cz] + BETA[1] * inward(fix, cz))
+        base_ref[f] = rest + wide * halo_ref[f, cz : 2 * cz]
+        fixed_ref[f, 0, :cz] = jnp.zeros_like(rest)
+        fixed_ref[f, 0, cz:] = BETA[1] * fix
+        beside_ref[f] = fix + cond * old
+        add_ref[f, 0, :cz] = BETA[2] * rest
+        delta_ref[0, f] = BETA[2] * rest
+    early()
+
+    def wing_emit(f, a, image):
+        add_ref[f, 0, cz:] = ALPHA[2] * fixed_ref[f, 0, cz:] + BETA[2] * (beside_ref[f] - image)
+
+    def wing_choice(f, a):
+        return choose(wing_store(wing_ref, f, 0), wing_store(wing_ref, f, ca - 1))
+
+    def wing_kinds(a, t):
+        return choose(wing_ref[nf + nf // 2, 0], wing_ref[nf + nf // 2, ca - 1])
 
     apply_local(
-        fixed_ref, lambda f, e: wing_store(wing_ref, f, ends[e]), lambda e, t: wing_ref[nf + nf // 2, ends[e]],
-        cond_ref, coef_ref[...], mix_ref, (cz, cz + ROWS), wing_emit, linked=False,
-    )
-
-    def emit(f, e, image):
+        fixed_ref, wing_choice, wing_kinds, cond_ref, coef_ref[...], mix_ref, (cz, cz + ROWS), wing_emit, linked=False
+    )
+
+    def own_emit(f, a, image):
         cond = cond_ref[f]
-        out_ref[f, ends[e]] = rest_ref[f, ends[e]] + base_ref[f, e] - image
-        inner = add_ref[f, e, :cz] + inward(BETA[2] * cond * fixed_ref[f, e, cz:], cz)
-        out_ref[f, beside_ends[e]] = rest_ref[f, beside_ends[e]] + tall(cond, cz) * inner
-        if e == 1:
-            for a in range(2, ca - 2):
-                out_ref[f, a] = rest_ref[f, a]
-            if f % GROUP == GROUP - 1:
-                some = pl.ds(f + 1 - GROUP, GROUP)
-                send(out_ref.at[some], residual_ref.at[some])
+        delta_ref[1, f] = base_ref[f] - image
+        inner = add_ref[f, 0, :cz] + inward(BETA[2] * cond * fixed_ref[f, 0, cz:], cz)
+        delta_ref[2, f] = tall(cond, cz) * inner
+        emit(f)
+
+    def kinds(a, t):
+        rows = slice(t * ROWS, (t + 1) * ROWS)
+        return choose(kinds_ref[0, rows].astype(f32), kinds_ref[ca - 1, rows].astype(f32))
 
     apply_local(
-        add_ref, lambda f, e: store_ref[f, ends[e]],
-        lambda e, t: kinds_ref[ends[e], t * ROWS : (t + 1) * ROWS].astype(f32),
-        cond_ref, coef_ref[...], mix_ref, (0, cz), emit, linked=False,
+        add_ref, lambda f, a: choose(store_ref[f, 0], store_ref[f, ca - 1]), kinds,
+        cond_ref, coef_ref[...], mix_ref, (0, cz), own_emit, linked=False,
+    )
+
+
+def end_kernel(
+    flags_ref, halo_ref, store_ref, kinds_ref, wing_ref, cond_ref, coef_ref,
+    delta_ref, base_ref, fixed_ref, add_ref, beside_ref, mix_ref,
+):
+    end_part(
+        False, flags_ref, halo_ref, store_ref, kinds_ref, wing_ref, cond_ref, coef_ref,
+        delta_ref, base_ref, fixed_ref, add_ref, beside_ref, mix_ref, lambda: None, lambda f: None,
+    )
+
+
+def last_kernel(
+    flags_ref, rest_ref, total_ref, halo_ref, other_ref, store_ref, kinds_ref, wing_ref, cond_ref, coef_ref,
+    live_ref, incoming_ref, emission_ref, reflect_ref,
+    panel_hbm, solution_ref, residual_ref,
+    panel_ref, end_ref, out_ref, delta_ref, base_ref, fixed_ref, add_ref, beside_ref, mix_ref, sems,
+):
+    nf, ca, cz, cr = store_ref.shape
+    even = tall(flags_ref[0], cz) > 0.5
+    copies = []
+
+    def send(near, far):
+        copies.append(pltpu.make_async_copy(near, far, sems.at[len(copies)]))
+        copies[-1].start()
+
+    send(total_ref.at[:, 1 : ca - 1], solution_ref.at[:, 1 : ca - 1])
+
+    def both(i, f):
+        one, other = delta_ref[i, f], other_ref[i, f]
+        return jnp.where(even, one, other), jnp.where(even, other, one)
+
+    def early():
+        for f in range(nf):
+            low, high = both(0, f)
+            end_ref[0, f] = total_ref[f, 0] + low
+            end_ref[1, f] = total_ref[f, ca - 1] + high
+        send(end_ref.at[0], solution_ref.at[:, 0])
+        send(end_ref.at[1], solution_ref.at[:, ca - 1])
+        slots, values = panel_ref.shape
+        wall = [end_ref[0, 0]] + [total_ref[0, a] for a in range(1, ca - 1)] + [end_ref[1, 0]]
+        wall = jnp.concatenate(wall, axis=0)[:, cr - 1 : cr]
+        wall = jnp.broadcast_to(wall, (ca * cz, values))
+        wall = jnp.concatenate([wall] * (-(-slots // (ca * cz))), axis=0)[:slots]
+        panel = lax.broadcasted_iota(jnp.int32, (slots, values), 0)
+        fresh = emission_ref[...] * wall + reflect_ref[...] * incoming_ref[:slots]
+        panel_ref[...] = jnp.where(panel < live_ref[:1], fresh, 0.0)
+        send(panel_ref, panel_hbm)
+
+    def emit(f):
+        low, high = both(1, f)
+        out_ref[f, 0] = rest_ref[f, 0] + low
+        out_ref[f, ca - 1] = rest_ref[f, ca - 1] + high
+        low, high = both(2, f)
+        out_ref[f, 1] = rest_ref[f, 1] + low
+        for a in range(2, ca - 2):
+            out_ref[f, a] = rest_ref[f, a]
+        out_ref[f, ca - 2] = rest_ref[f, ca - 2] + high
+        if f % GROUP == GROUP - 1:
+            some = pl.ds(f + 1 - GROUP, GROUP)
+            send(out_ref.at[some], residual_ref.at[some])
+
+    end_part(
+        True, flags_ref, halo_ref, store_ref, kinds_ref, wing_ref, cond_ref, coef_ref,
+        delta_ref, base_ref, fixed_ref, add_ref, beside_ref, mix_ref, early, emit,
     )
     for copy in copies:
         copy.wait()
@@ -459,10 +510,6 @@
         for k in range(visible):
             out = out + moved[k * slots : (k + 1) * slots]
     out_ref[...] = out
-
-
-def relay_kernel(flags_ref, out_ref):
-    out_ref[...] = flags_ref[...]
 
 
 def pairs(count, first, closed):
@@ -529,19 +576,21 @@
     to_right, to_left = sides[:, :, half:], sides[:, :, :half]
     far = jnp.where(azim_even, to_left, to_right).astype(LINK)
     near = jnp.where(azim_even, to_right, to_left).astype(LINK)
-    far_in = swap(far, "azim", 1, True)
-    message1 = after(edges, far)[0].astype(LINK)
-    halo1 = swap(message1, "axial", 1)
-    near_in = swap(after(near, message1), "azim", 0)
-
     slots, visible = vis_owner.shape[2:]
     tile = -(-slots // 16) * 16
     panels = jnp.pad(radiosity_old[0, 0], ((0, tile - slots), (0, 0)))
     fold = cr // values
     folded = panels.astype(f32) * RAD_SCALE
     folded = jnp.concatenate(jnp.split(folded, fold, axis=0), axis=1)
-    layer0 = after(edges, message1)[1].reshape(nf * cz, cr)
-    message = swap(jnp.concatenate([layer0, folded], axis=0).astype(LINK), "axial", 0)
+    far = far
+    far_in = swap(far, "azim", 1, True)
+    layer0 = after(edges, far)[1].reshape(nf * cz, cr)
+    message0 = jnp.concatenate([layer0, folded], axis=0).astype(LINK)
+    message = swap(message0, "axial", 0)
+    near = after(near, message0)
+    near_in = swap(near, "azim", 0)
+    message1 = after(edges, near)[0].astype(LINK)
+    halo1 = swap(message1, "axial", 1)
 
     from_right = jnp.where(azim_even, near_in, far_in)
     from_left = jnp.where(azim_even, far_in, near_in)
@@ -559,28 +608,28 @@
             (one, here((nf, cz, cr), f32), one),
         ).astype(LINK)
 
-    halo1 = after(halo1, rest).astype(f32)
-    message1 = side(True, halo1)
-    second1 = swap(message1, "axial", 1).astype(f32)
-    message = after(message, message1)
+    message = after(message, rest)
     halo0 = message[: nf * cz].reshape(nf, cz, cr).astype(f32)
     message0 = side(False, halo0)
     second0 = swap(message0, "axial", 0).astype(f32)
+    halo1 = after(halo1, message0).astype(f32)
+    message1 = side(True, halo1)
+    second1 = swap(message1, "axial", 1).astype(f32)
     rest3, total = call(
         later_kernel,
         (plain, plain),
-        (flags, after(rest, message0), halo1, halo0, source, storage, materials, wings, cond, coef),
+        (flags, after(rest, message1), halo1, halo0, source, storage, materials, wings, cond, coef),
         (plain, full, full, full),
     )
 
-    partner = after(message, message0)[nf * cz :].astype(f32) * (1.0 / RAD_SCALE)
+    partner = after(message, message1)[nf * cz :].astype(f32) * (1.0 / RAD_SCALE)
     partner = jnp.concatenate(jnp.split(partner, fold, axis=1), axis=0).astype(bf16)
     if owners <= 8 and owners & (owners - 1) == 0:
         pair = jnp.concatenate([panels, partner], axis=0)
         others = [
             lax.ppermute(pair, "axial", [(i, i ^ step) for i in range(owners)]) for step in range(2, owners, 2)
         ]
-        panels = jnp.concatenate([after(pair, second1), *others], axis=0)
+        panels = jnp.concatenate([after(pair, second0), *others], axis=0)
         owner = vis_owner[0, 0].T ^ me
     else:
         pair = jnp.stack([panels, partner])
@@ -601,21 +650,24 @@
     )
 
     live = jnp.broadcast_to(after(counts, rest3), (ROWS, values))
-    checked = call(relay_kernel, (here(flags.shape, f32),), (after(flags, second0),))
     shape = jax.ShapeDtypeStruct
-    pair_full = here((nf, 2, cz + ROWS, cr), f32)
+    one = here((nf, 1, cz + ROWS, cr), f32)
+    deltas = here((3, nf, cz, cr), f32)
+    parts = (here((nf, cz, cr), f32), one, one, here((nf, ROWS, cr), f32), one)
+    delta0 = call(
+        end_kernel, (deltas,), (flags, second0, storage, materials, wings, cond, coef), parts
+    )
     panel_new, solution_out, residual = pl.pallas_call(
         last_kernel,
         out_shape=(shape((slots, values), f32), shape(plain.shape, f32), shape(plain.shape, f32)),
         in_specs=[VMEM] * 14,
-        out_specs=(VMEM, HBM, HBM),
+        out_specs=(HBM, HBM, HBM),
         scratch_shapes=[
-            layers, plain, here((nf, 2, cz, cr), f32), pair_full, pair_full, here((nf, 2, ROWS, cr), f32), pair_full,
-            pltpu.SemaphoreType.DMA((3 + nf // GROUP,)),
+            here((slots, values), f32), layers, plain, deltas, *parts, pltpu.SemaphoreType.DMA((4 + nf // GROUP,))
         ],
         compiler_params=PARAMS, cost_estimate=CHEAP,
     )(
-        checked, rest3, total, second1, second0, storage, materials, wings, cond, coef,
+        flags, rest3, total, second1, delta0, storage, materials, wings, cond, coef,
         live, incoming, emission[0, 0], reflect[0, 0],
     )
     return (solution_out, residual, panel_new[None, None])

time: 34.7 us -> 30.8 us (0.89)
  the two profiles are of different devices: /device:TPU:0 before, /device:TPU:2 now
where the time goes in v5:
time: 30.8 us; the launch traced here: 30.6 us
  starting transfers between devices  14.6 us (47%)
  Pallas kernels  11 us (36%)
  waiting for transfers between devices  1.96 us (6%)
  between operations  1.7 us (6%)
  other arithmetic  0.8 us (3%)
  local copies, waits for them, and re-layouts  0.46 us (1%)
    ppermute x6, starting transfers between devices, swap(): return lax.ppermute(array, axis, pairs(lax.axis_size(axis), first, closed))  10.2 us
    pallas_call x6, Pallas kernels, call(): pl.pallas_call(kernel, out_shape=outs[0] if single else tuple(outs), in_s...  7.68 us
    ppermute x3, starting transfers between devices, body(): lax.ppermute(pair, 'axial', [(i, i ^ step) for i in range(owners)])  4.45 us
    ppermute x6, waiting for transfers between devices, swap(): return lax.ppermute(array, axis, pairs(lax.axis_size(axis), first, closed))  1.95 us
    pallas_call x1, Pallas kernels, body(): pl.pallas_call(last_kernel, out_shape=(shape((slots, values), f32), shape...  1.71 us
    pallas_call x1, Pallas kernels, body(): pl.pallas_call(ends_kernel, out_shape=(plain, plain, here((ca, cz, cr), j...  1.63 us
  transfers between devices with their start and end apart: 9, of which 2 were waited for; matrix products, arithmetic and copies ran while one was open for 2% of the time, Pallas kernels for 25%

profile of v5, /device:TPU:2, one launch (start us, length us, event | category | flops | bytes accessed | tf_op | source)
XLA Modules:
  0.0 30.6 jit_solution(9287925434503426938)
XLA Ops:
  0.7 0.1 add_convert_fusion
  0.7 0.1 broadcast_in_dim.19.flags_ref
  0.8 0.0 copy-start.3
  0.8 1.6 %shard_map.148 = (f32[12,4,16,256]{3,2,1,0:T(8,128)S(1)}, f32[12,4,16,256]{3,2,1,0:T(8,128)S(1)}, s32[4,16,256]{2,1,0:T(8,128)S(1)}, f32[2,12,16,256]{3,2,1,0:T(...) custom-call(f32[3,8,256]{2,1,0:T(8,128)S(1)} %broadcast_in_dim.19.flags_ref, ...), custom_call_target="tpu_custom_call" | custom-call | tf_op jit(solution)/shard_map/pallas_call | solution.py:564
  2.4 0.2 select_convert_fusion.1
  2.6 1.0 %collective-permute-start.1 = (f16[19,4,4,256]{3,2,1,0:T(4,128)(2,1)S(1)}, f16[19,4,4,256]{3,2,1,0:T(4,128)(2,1)S(1)}, u32[]{:S(2)}, u32[]{:S(2)}) collective-permute-start(f16[19,4,4,256]{3,2,1,0:T(4,128)(2,1)S(1)} %get-tuple-element.46), channel_id=1, source_target_pairs={{1,2},{2,1},{3,0},{0,3},{5,6},{6,5},{7,4},{4,7},{9,10},{10,9},{11,... | collective-permute-start | bytes 466952 | tf_op jit(solution)/shard_map/ppermute | solution.py:524
  3.7 0.0 copy-done.3
  3.8 0.6 %collective-permute-start.3 = (f16[256,256]{1,0:T(8,128)(2,1)S(1)}, f16[256,256]{1,0:T(8,128)(2,1)S(1)}, u32[]{:S(2)}, u32[]{:S(2)}) collective-permute-start(f16[256,256]{1,0:T(8,128)(2,1)S(1)} %maximum_maximum_fusion), channel_id=1, source_target_pairs={{0,4},{4,0},{8,12},{12,8},{16,20},{20,16},{24,28},{28,24},{1,5},{5... | collective-permute-start | bytes 393224 | tf_op jit(solution)/shard_map/ppermute | solution.py:524
  4.4 0.4 %collective-permute-start = (f16[19,4,4,256]{3,2,1,0:T(4,128)(2,1)S(1)}, f16[19,4,4,256]{3,2,1,0:T(4,128)(2,1)S(1)}, u32[]{:S(2)}, u32[]{:S(2)}) collective-permute-start(f16[19,4,4,256]{3,2,1,0:T(4,128)(2,1)S(1)} %get-tuple-element.30), channel_id=1, source_target_pairs={{0,1},{1,0},{2,3},{3,2},{4,5},{5,4},{6,7},{7,6},{8,9},{9,8},{10,11... | collective-permute-start | bytes 466952 | tf_op jit(solution)/shard_map/ppermute | solution.py:524
  4.8 4.4 %collective-permute-start.2 = (f16[12,16,256]{2,1,0:T(8,128)(2,1)S(1)}, f16[12,16,256]{2,1,0:T(8,128)(2,1)S(1)}, u32[]{:S(2)}, u32[]{:S(2)}) collective-permute-start(f16[12,16,256]{2,1,0:T(8,128)(2,1)S(1)} %fusion), channel_id=1, source_target_pairs={{4,8},{8,4},{12,16},{16,12},{20,24},{24,20},{5,9},{9,5},{13,17},{1... | collective-permute-start | bytes 294920 | tf_op jit(solution)/shard_map/ppermute | solution.py:524
  9.2 0.0 collective-permute-done
  9.2 0.0 collective-permute-done.1
  9.2 0.1 broadcast_select_fusion.1
  9.3 0.2 maximum_convert_fusion.wing_ref
  9.5 1.8 %shard_map.149.rest_ref = f32[12,4,24,256]{3,2,1,0:T(8,128)S(1)} custom-call(f32[12,4,16,256]{3,2,1,0:T(8,128)S(1)} %get-tuple-element.24.source_ref, f32[12,4,16,256]{3,2,1,0:T(8,128)S(1)} %get-tuple-element.25.store_ref, s32[4,16,256]{2,1,0:T(8,128)S(1)} %get-tuple-element.26.kinds_ref, f32[19,4,8,256]{3,2,1,0:T(8,128)S(1)} %maximum_convert_fusion.wing_ref, ...), custom_call_target="tpu_custom_call" | custom-call | tf_op jit(solution)/shard_map/pallas_call | solution.py:548
  11.3 0.0 collective-permute-done.3
  11.4 0.5 %shard_map.150 = f32[12,40,256]{2,1,0:T(8,128)S(1)} custom-call(f32[3,8,256]{2,1,0:T(8,128)S(1)} %broadcast_in_dim.19.flags_ref, f32[12,4,24,256]{3,2,1,0:T(8,128)S(1)} %shard_map.149.rest_ref, f32[12,16,256]{2,1,0:T(8,128)S(1)} %convert.26.halo_ref.halo0_ref, f32[12,4,16,256]{3,2,1,0:T(8,128)S(1)} %get-tuple-element.24.source_ref, ...), custom_call_target="tpu_custom_call" | custom-call | tf_op jit(solution)/shard_map/pallas_call | solution.py:548
  12.0 0.1 collective-permute-start.5
  12.0 0.3 %collective-permute-done.2 = f16[12,16,256]{2,1,0:T(8,128)(2,1)S(1)} collective-permute-done((f16[12,16,256]{2,1,0:T(8,128)(2,1)S(1)}, f16[12,16,256]{2,1,0:T(8,128)(2,1)S(1)}, u32[]{:S(2)}, u32[]{:S(2)}) %collective-permute-start.2) | collective-permute-done | bytes 98336 | tf_op jit(solution)/shard_map/ppermute | solution.py:524
  12.4 0.0 copy-start.4
  12.4 0.0 copy-start.5
  12.4 0.0 copy-start.6
  12.4 0.5 %shard_map.151 = f32[12,40,256]{2,1,0:T(8,128)S(1)} custom-call(f32[3,8,256]{2,1,0:T(8,128)S(1)} %broadcast_in_dim.19.flags_ref, f32[12,4,24,256]{3,2,1,0:T(8,128)S(1)} %shard_map.149.rest_ref, f32[12,16,256]{2,1,0:T(8,128)S(1)} %convert_element_type.59.halo_ref.halo1_ref, f32[12,4,16,256]{3,2,1,0:T(8,128)S(1)} %get-tuple-element.24.source_ref, ...), custom_call_target="tpu_custom_call" | custom-call | tf_op jit(solution)/shard_map/pallas_call | solution.py:548
  13.0 1.6 %collective-permute-start.6 = (bf16[256,128]{1,0:T(8,128)(2,1)S(1)}, bf16[256,128]{1,0:T(8,128)(2,1)S(1)}, u32[]{:S(2)}, u32[]{:S(2)}) collective-permute-start(bf16[256,128]{1,0:T(8,128)(2,1)S(1)} %pad_maximum_fusion.1), channel_id=1, source_target_pairs={{0,8},{4,12},{8,0},{12,4},{16,24},{20,28},{24,16},{28,20},{1,9},{5... | collective-permute-start | bytes 196616 | tf_op jit(solution)/shard_map/ppermute | solution.py:630
  14.7 2.5 %collective-permute-start.7 = (bf16[256,128]{1,0:T(8,128)(2,1)S(1)}, bf16[256,128]{1,0:T(8,128)(2,1)S(1)}, u32[]{:S(2)}, u32[]{:S(2)}) collective-permute-start(bf16[256,128]{1,0:T(8,128)(2,1)S(1)} %pad_maximum_fusion.1), channel_id=1, source_target_pairs={{0,16},{4,20},{8,24},{12,28},{16,0},{20,4},{24,8},{28,12},{1,17},{... | collective-permute-start | bytes 196616 | tf_op jit(solution)/shard_map/ppermute | solution.py:630
  17.1 0.3 %collective-permute-start.8 = (bf16[256,128]{1,0:T(8,128)(2,1)S(1)}, bf16[256,128]{1,0:T(8,128)(2,1)S(1)}, u32[]{:S(2)}, u32[]{:S(2)}) collective-permute-start(bf16[256,128]{1,0:T(8,128)(2,1)S(1)} %pad_maximum_fusion.1), channel_id=1, source_target_pairs={{0,24},{4,28},{8,16},{12,20},{16,8},{20,12},{24,0},{28,4},{1,25},{... | collective-permute-start | bytes 196616 | tf_op jit(solution)/shard_map/ppermute | solution.py:630
  17.5 3.7 %collective-permute-start.4 = (f16[12,40,256]{2,1,0:T(8,128)(2,1)S(1)}, f16[12,40,256]{2,1,0:T(8,128)(2,1)S(1)}, u32[]{:S(2)}, u32[]{:S(2)}) collective-permute-start(f16[12,40,256]{2,1,0:T(8,128)(2,1)S(1)} %convert_element_type.60), channel_id=1, source_target_pairs={{4,8},{8,4},{12,16},{16,12},{20,24},{24,20},{5,9},{9,5},{13,17},{1... | collective-permute-start | bytes 737288 | tf_op jit(solution)/shard_map/ppermute | solution.py:524
  21.2 0.0 copy-done.4
  21.2 0.0 copy-done.5
  21.2 0.0 copy-done.6
  21.9 3.3 %shard_map.152 = (f32[12,4,16,256]{3,2,1,0:T(8,128)S(1)}, f32[12,4,16,256]{3,2,1,0:T(8,128)S(1)}) custom-call(f32[3,8,256]{2,1,0:T(8,128)S(1)} %broadcast_in_dim.19.flags_ref, f32[12,4,24,256]{3,2,1,0:T(8,128)S(1)} %shard_map.149.rest_ref, f32[12,16,256]{2,1,0:T(8,128)S(1)} %convert_element_type.59.halo_ref.halo1_ref, ...), custom_call_target="tpu_custom_call" | custom-call | tf_op jit(solution)/shard_map/pallas_call | solution.py:548
  25.2 0.0 collective-permute-done.5
  25.2 0.0 copy-start
  25.2 0.6 %shard_map.153.other_ref = f32[3,12,16,256]{3,2,1,0:T(8,128)S(1)} custom-call(f32[3,8,256]{2,1,0:T(8,128)S(1)} %broadcast_in_dim.19.flags_ref, f32[12,40,256]{2,1,0:T(8,128)S(1)} %convert_element_type.62.halo_ref, f32[12,4,16,256]{3,2,1,0:T(8,128)S(1)} %get-tuple-element.25.store_ref, s32[4,16,256]{2,1,0:T(8,128)S(1)} %get-tuple-element.26.kinds_ref, ...), custom_call_target="tpu_custom_call" | custom-call | tf_op jit(solution)/shard_map/pallas_call | solution.py:548
  25.8 0.0 copy-start.1
  25.8 0.0 copy-start.2
  25.8 0.0 collective-permute-done.6
  25.8 0.0 collective-permute-done.7
  25.8 0.0 collective-permute-done.8
  25.9 0.3 copy-done
  26.2 1.0 %shard_map.154.incoming_ref = f32[128,128]{1,0:T(8,128)S(1)} custom-call(s32[8,128]{1,0:T(8,128)S(1)} %pad.12.index_ref, s32[8,128]{1,0:T(8,128)S(1)} %pad.13.block_ref, bf16[1024,128]{1,0:T(8,128)(2,1)S(1)} %pad_maximum_fusion.rows_ref, bf16[8,128,128]{2,1,0:T(8,128)(2,1)S(1)} %copy-done), custom_call_target="tpu_custom_call" | custom-call | tf_op jit(solution)/shard_map/pallas_call | solution.py:548
  27.2 1.6 %collective-permute-done.4 = f16[12,40,256]{2,1,0:T(8,128)(2,1)S(1)} collective-permute-done((f16[12,40,256]{2,1,0:T(8,128)(2,1)S(1)}, f16[12,40,256]{2,1,0:T(8,128)(2,1)S(1)}, u32[]{:S(2)}, u32[]{:S(2)}) %collective-permute-start.4) | collective-permute-done | bytes 245792 | tf_op jit(solution)/shard_map/ppermute | solution.py:524
  28.8 0.0 copy-done.1
  28.9 0.0 copy-done.2
  28.9 1.7 %shard_map.155 = (f32[120,128]{1,0:T(8,128)}, f32[12,4,16,256]{3,2,1,0:T(8,128)}, f32[12,4,16,256]{3,2,1,0:T(8,128)}) custom-call(f32[3,8,256]{2,1,0:T(8,128)S(1)} %broadcast_in_dim.19.flags_ref, f32[12,4,16,256]{3,2,1,0:T(8,128)S(1)} %get-tuple-element.37.rest_ref, f32[12,4,16,256]{3,2,1,0:T(8,128)S(1)} %get-tuple-element.38.total_ref, ...), custom_call_target="tpu_custom_call" | custom-call | tf_op jit(solution)/shard_map/pallas_call | solution.py:660
  (21 shorter events, 0.3 us)
Async XLA Ops:
  0.8 2.9 %copy-start.3 = (bf16[1,1,120,128]{3,2,1,0:T(8,128)(2,1)S(1)}, bf16[1,1,120,128]{3,2,1,0:T(8,128)(2,1)}, u32[]{:S(2)}) copy-start(bf16[1,1,120,128]{3,2,1,0:T(8,128)(2,1)} %param.22) | copy-start | bytes 92164
  2.6 6.6 %collective-permute-start.1 = (f16[19,4,4,256]{3,2,1,0:T(4,128)(2,1)S(1)}, f16[19,4,4,256]{3,2,1,0:T(4,128)(2,1)S(1)}, u32[]{:S(2)}, u32[]{:S(2)}) collective-permute-start(f16[19,4,4,256]{3,2,1,0:T(4,128)(2,1)S(1)} %get-tuple-element.46), channel_id=1, source_target_pairs={{1,2},{2,1},{3,0},{0,3},{5,6},{6,5},{7,4},{4,7},{9,10},{10,9},{11,... | collective-permute-start | bytes 466952 | tf_op jit(solution)/shard_map/ppermute | solution.py:524
  3.8 7.6 %collective-permute-start.3 = (f16[256,256]{1,0:T(8,128)(2,1)S(1)}, f16[256,256]{1,0:T(8,128)(2,1)S(1)}, u32[]{:S(2)}, u32[]{:S(2)}) collective-permute-start(f16[256,256]{1,0:T(8,128)(2,1)S(1)} %maximum_maximum_fusion), channel_id=1, source_target_pairs={{0,4},{4,0},{8,12},{12,8},{16,20},{20,16},{24,28},{28,24},{1,5},{5... | collective-permute-start | bytes 393224 | tf_op jit(solution)/shard_map/ppermute | solution.py:524
  4.4 4.9 %collective-permute-start = (f16[19,4,4,256]{3,2,1,0:T(4,128)(2,1)S(1)}, f16[19,4,4,256]{3,2,1,0:T(4,128)(2,1)S(1)}, u32[]{:S(2)}, u32[]{:S(2)}) collective-permute-start(f16[19,4,4,256]{3,2,1,0:T(4,128)(2,1)S(1)} %get-tuple-element.30), channel_id=1, source_target_pairs={{0,1},{1,0},{2,3},{3,2},{4,5},{5,4},{6,7},{7,6},{8,9},{9,8},{10,11... | collective-permute-start | bytes 466952 | tf_op jit(solution)/shard_map/ppermute | solution.py:524
  4.8 7.6 %collective-permute-start.2 = (f16[12,16,256]{2,1,0:T(8,128)(2,1)S(1)}, f16[12,16,256]{2,1,0:T(8,128)(2,1)S(1)}, u32[]{:S(2)}, u32[]{:S(2)}) collective-permute-start(f16[12,16,256]{2,1,0:T(8,128)(2,1)S(1)} %fusion), channel_id=1, source_target_pairs={{4,8},{8,4},{12,16},{16,12},{20,24},{24,20},{5,9},{9,5},{13,17},{1... | collective-permute-start | bytes 294920 | tf_op jit(solution)/shard_map/ppermute | solution.py:524
  12.0 13.2 %collective-permute-start.5 = (f16[12,40,256]{2,1,0:T(8,128)(2,1)S(1)}, f16[12,40,256]{2,1,0:T(8,128)(2,1)S(1)}, u32[]{:S(2)}, u32[]{:S(2)}) collective-permute-start(f16[12,40,256]{2,1,0:T(8,128)(2,1)S(1)} %convert_element_type.58), channel_id=1, source_target_pairs={{0,4},{4,0},{8,12},{12,8},{16,20},{20,16},{24,28},{28,24},{1,5},{5... | collective-permute-start | bytes 737288 | tf_op jit(solution)/shard_map/ppermute | solution.py:524
  12.4 8.8 %copy-start.4 = (s32[1,1,120,4]{2,3,1,0:T(4,128)S(1)}, s32[1,1,120,4]{2,3,1,0:T(4,128)}, u32[]{:S(2)}) copy-start(s32[1,1,120,4]{2,3,1,0:T(4,128)} %param.20) | copy-start | bytes 5764
  12.4 8.8 %copy-start.5 = (s32[1,1,120,4]{2,3,1,0:T(4,128)S(1)}, s32[1,1,120,4]{2,3,1,0:T(4,128)}, u32[]{:S(2)}) copy-start(s32[1,1,120,4]{2,3,1,0:T(4,128)} %param.19) | copy-start | bytes 5764
  12.4 8.8 %copy-start.6 = (s32[1,1,120,4]{2,3,1,0:T(4,128)S(1)}, s32[1,1,120,4]{2,3,1,0:T(4,128)}, u32[]{:S(2)}) copy-start(s32[1,1,120,4]{2,3,1,0:T(4,128)} %param.21) | copy-start | bytes 5764
  13.0 12.8 %collective-permute-start.6 = (bf16[256,128]{1,0:T(8,128)(2,1)S(1)}, bf16[256,128]{1,0:T(8,128)(2,1)S(1)}, u32[]{:S(2)}, u32[]{:S(2)}) collective-permute-start(bf16[256,128]{1,0:T(8,128)(2,1)S(1)} %pad_maximum_fusion.1), channel_id=1, source_target_pairs={{0,8},{4,12},{8,0},{12,4},{16,24},{20,28},{24,16},{28,20},{1,9},{5... | collective-permute-start | bytes 196616 | tf_op jit(solution)/shard_map/ppermute | solution.py:630
  14.7 11.1 %collective-permute-start.7 = (bf16[256,128]{1,0:T(8,128)(2,1)S(1)}, bf16[256,128]{1,0:T(8,128)(2,1)S(1)}, u32[]{:S(2)}, u32[]{:S(2)}) collective-permute-start(bf16[256,128]{1,0:T(8,128)(2,1)S(1)} %pad_maximum_fusion.1), channel_id=1, source_target_pairs={{0,16},{4,20},{8,24},{12,28},{16,0},{20,4},{24,8},{28,12},{1,17},{... | collective-permute-start | bytes 196616 | tf_op jit(solution)/shard_map/ppermute | solution.py:630
  17.1 8.7 %collective-permute-start.8 = (bf16[256,128]{1,0:T(8,128)(2,1)S(1)}, bf16[256,128]{1,0:T(8,128)(2,1)S(1)}, u32[]{:S(2)}, u32[]{:S(2)}) collective-permute-start(bf16[256,128]{1,0:T(8,128)(2,1)S(1)} %pad_maximum_fusion.1), channel_id=1, source_target_pairs={{0,24},{4,28},{8,16},{12,20},{16,8},{20,12},{24,0},{28,4},{1,25},{... | collective-permute-start | bytes 196616 | tf_op jit(solution)/shard_map/ppermute | solution.py:630
  17.5 11.3 %collective-permute-start.4 = (f16[12,40,256]{2,1,0:T(8,128)(2,1)S(1)}, f16[12,40,256]{2,1,0:T(8,128)(2,1)S(1)}, u32[]{:S(2)}, u32[]{:S(2)}) collective-permute-start(f16[12,40,256]{2,1,0:T(8,128)(2,1)S(1)} %convert_element_type.60), channel_id=1, source_target_pairs={{4,8},{8,4},{12,16},{16,12},{20,24},{24,20},{5,9},{9,5},{13,17},{1... | collective-permute-start | bytes 737288 | tf_op jit(solution)/shard_map/ppermute | solution.py:524
  25.2 1.0 %copy-start = (bf16[8,128,128]{2,1,0:T(8,128)(2,1)S(1)}, bf16[8,128,128]{2,1,0:T(8,128)(2,1)}, u32[]{:S(2)}) copy-start(bf16[8,128,128]{2,1,0:T(8,128)(2,1)} %view_ref.1) | copy-start | bytes 786436
  25.8 3.1 %copy-start.1 = (f32[1,1,120,128]{3,2,1,0:T(8,128)S(1)}, f32[1,1,120,128]{3,2,1,0:T(8,128)}, u32[]{:S(2)}) copy-start(f32[1,1,120,128]{3,2,1,0:T(8,128)} %param.24) | copy-start | bytes 184324
  25.8 3.1 %copy-start.2 = (f32[1,1,120,128]{3,2,1,0:T(8,128)S(1)}, f32[1,1,120,128]{3,2,1,0:T(8,128)}, u32[]{:S(2)}) copy-start(f32[1,1,120,128]{3,2,1,0:T(8,128)} %param.25) | copy-start | bytes 184324

commit v6 on v5

--- a/solution.py
+++ b/solution.py
@@ -120,7 +120,7 @@
 
 
 def ends_kernel(
-    flags_ref, source_hbm, store_hbm, kinds_hbm, cond_hbm, mix_hbm,
+    source_hbm, store_hbm, kinds_hbm, cond_hbm, mix_hbm,
     source_ref, store_ref, kinds_ref, edge_ref, side_ref, cond_ref, coef_ref,
     cond_row, mix_rows, sems,
 ):
@@ -134,7 +134,6 @@
     copies = [pltpu.make_async_copy(far, near, sems.at[i]) for i, (far, near) in enumerate(pairs_of)]
     for copy in copies:
         copy.start()
-    even = tall(flags_ref[0], cz) > 0.5
     place = lax.broadcasted_iota(jnp.int32, (ROWS, cr), 0)
 
     copies[0].wait()
@@ -156,9 +155,8 @@
     for f in range(nf):
         if f % part == 0:
             copies[2 + f // part].wait()
-        low, high = source_ref[f, 0] * INV_CENTER, source_ref[f, ca - 1] * INV_CENTER
-        edge_ref[0, f] = jnp.where(even, low, high)
-        edge_ref[1, f] = jnp.where(even, high, low)
+        edge_ref[0, f] = source_ref[f, 0] * INV_CENTER
+        edge_ref[1, f] = source_ref[f, ca - 1] * INV_CENTER
         for a in range(ca):
             side_ref[f, a] = both(source_ref, f, a) * INV_CENTER
     for copy in copies[2 + COPIES :]:
@@ -210,6 +208,20 @@
     return jnp.where((place >= 2) & (place <= 5), moved, beside)
 
 
+KEPT = 6
+
+
+def put_beside(message_ref, start, rows):
+    message_ref[start : start + 1] = rows[:1]
+    message_ref[start + 1 : start + 5] = rows[2:6]
+    message_ref[start + 5 : start + 6] = rows[7:]
+
+
+def get_beside(message_ref, start):
+    first, inner, last = (message_ref[start + a : start + b] for a, b in ((0, 1), (1, 5), (5, 6)))
+    return jnp.concatenate([first, first, inner, last, last], axis=0)
+
+
 def side_kernel(
     first, flags_ref, rest_ref, halo_ref, source_ref, store_ref, kinds_ref, wing_ref, cond_ref, coef_ref,
     message_ref, dir_ref, next_ref, mix_ref,
@@ -232,17 +244,18 @@
         )
         dir_ref[f, 0, :cz] = direction
         dir_ref[f, 0, cz:] = beside
-        message_ref[f, :cz] = direction
-        message_ref[f, cz : 2 * cz] = own
-        message_ref[f, 2 * cz :] = beside_rows(wing, beside)
+        message_ref[2 * f * cz : (2 * f + 1) * cz] = direction
+        message_ref[(2 * f + 1) * cz : 2 * (f + 1) * cz] = own
+        put_beside(message_ref, 2 * nf * cz + KEPT * f, beside_rows(wing, beside))
 
     def kinds(a, t):
         rows = slice(t * ROWS, (t + 1) * ROWS)
         return choose(kinds_ref[0, rows].astype(f32), kinds_ref[ca - 1, rows].astype(f32))
 
     def emit(f, a, image):
-        rest = message_ref[f, cz : 2 * cz] - image + tall(cond_ref[f], cz) * next_ref[f]
-        message_ref[f, cz : 2 * cz] = ALPHA[2] * dir_ref[f, 0, :cz] + BETA[2] * rest
+        third = pl.ds((2 * f + 1) * cz, cz)
+        rest = message_ref[third] - image + tall(cond_ref[f], cz) * next_ref[f]
+        message_ref[third] = ALPHA[2] * dir_ref[f, 0, :cz] + BETA[2] * rest
 
     apply_local(
         dir_ref, lambda f, a: choose(store_ref[f, 0], store_ref[f, ca - 1]), kinds,
@@ -359,11 +372,11 @@
     for f in range(nf):
         cond = cond_ref[f]
         wide = tall(cond, cz)
-        old = halo_ref[f, 2 * cz :]
+        old = get_beside(halo_ref, 2 * nf * cz + KEPT * f)
         moved = jnp.where(place < 4, pltpu.roll(old, ROWS - 2, 0), pltpu.roll(old, 2, 0))
         fix = cond * jnp.where(outer, moved, 0.0)
-        rest = wide * (halo_ref[f, :cz] + BETA[1] * inward(fix, cz))
-        base_ref[f] = rest + wide * halo_ref[f, cz : 2 * cz]
+        rest = wide * (halo_ref[2 * f * cz : (2 * f + 1) * cz] + BETA[1] * inward(fix, cz))
+        base_ref[f] = rest + wide * halo_ref[(2 * f + 1) * cz : 2 * (f + 1) * cz]
         fixed_ref[f, 0, :cz] = jnp.zeros_like(rest)
         fixed_ref[f, 0, cz:] = BETA[1] * fix
         beside_ref[f] = fix + cond * old
@@ -567,11 +580,12 @@
             plain, plain, here((ca, cz, cr), jnp.int32), layers, here((nf + nf // 2 + 1, ca, ROWS, cr), f32),
             here((nf, ROWS, cr), f32), here((mats * nf * ROWS, 3 * nf * ROWS), bf16),
         ),
-        in_specs=[VMEM] + [HBM] * 5,
+        in_specs=[HBM] * 5,
         out_specs=(VMEM,) * 7,
         scratch_shapes=[here(x.shape, x.dtype) for x in small] + [pltpu.SemaphoreType.DMA((2 * COPIES + 3,))],
         compiler_params=PARAMS, cost_estimate=CHEAP,
-    )(flags, *(pltpu.with_memory_space_constraint(x, pltpu.HBM) for x in (source, storage, materials, *small)))
+    )(*(pltpu.with_memory_space_constraint(x, pltpu.HBM) for x in (source, storage, materials, *small)))
+    edges = jnp.where(is_even, edges, edges[::-1])
     half = ROWS // 2
     to_right, to_left = sides[:, :, half:], sides[:, :, :half]
     far = jnp.where(azim_even, to_left, to_right).astype(LINK)
@@ -603,7 +617,7 @@
         one = here((nf, 1, cz + ROWS, cr), f32)
         return call(
             functools.partial(side_kernel, first),
-            (here((nf, 2 * cz + ROWS, cr), f32),),
+            (here((nf * (2 * cz + KEPT), cr), f32),),
             (flags, rest, halo, source, storage, materials, wings, cond, coef),
             (one, here((nf, cz, cr), f32), one),
         ).astype(LINK)

time: 30.8 us -> 30.4 us (0.987)
  no operation moved by 1% of the time
where the time goes in v6:
time: 30.4 us; the launch traced here: 30.2 us
  starting transfers between devices  14.8 us (49%)
  Pallas kernels  10.8 us (36%)
  between operations  1.7 us (6%)
  waiting for transfers between devices  1.67 us (5%)
  other arithmetic  0.81 us (3%)
  local copies, waits for them, and re-layouts  0.46 us (2%)
    ppermute x6, starting transfers between devices, swap(): return lax.ppermute(array, axis, pairs(lax.axis_size(axis), first, closed))  10.3 us
    pallas_call x6, Pallas kernels, call(): pl.pallas_call(kernel, out_shape=outs[0] if single else tuple(outs), in_s...  7.56 us
    ppermute x3, starting transfers between devices, body(): lax.ppermute(pair, 'axial', [(i, i ^ step) for i in range(owners)])  4.45 us
    ppermute x6, waiting for transfers between devices, swap(): return lax.ppermute(array, axis, pairs(lax.axis_size(axis), first, closed))  1.66 us
    pallas_call x1, Pallas kernels, body(): pl.pallas_call(ends_kernel, out_shape=(plain, plain, here((ca, cz, cr), j...  1.63 us
    pallas_call x1, Pallas kernels, body(): pl.pallas_call(last_kernel, out_shape=(shape((slots, values), f32), shape...  1.59 us
  transfers between devices with their start and end apart: 9, of which 2 were waited for; matrix products, arithmetic and copies ran while one was open for 2% of the time, Pallas kernels for 25%

profile of v6, /device:TPU:2, one launch (start us, length us, event | category | flops | bytes accessed | tf_op | source)
XLA Modules:
  0.0 30.2 jit_solution(12960847995843399563)
XLA Ops:
  0.6 1.6 %shard_map.148 = (f32[12,4,16,256]{3,2,1,0:T(8,128)S(1)}, f32[12,4,16,256]{3,2,1,0:T(8,128)S(1)}, s32[4,16,256]{2,1,0:T(8,128)S(1)}, f32[2,12,16,256]{3,2,1,0:T(...) custom-call(f32[12,4,16,256]{3,2,1,0:T(8,128)} %source_hbm.1, ...), custom_call_target="tpu_custom_call" | custom-call | tf_op jit(solution)/shard_map/pallas_call | solution.py:577
  2.3 0.0 copy-start.3
  2.3 0.2 select_convert_fusion.1
  2.5 1.0 %collective-permute-start.1 = (f16[19,4,4,256]{3,2,1,0:T(4,128)(2,1)S(1)}, f16[19,4,4,256]{3,2,1,0:T(4,128)(2,1)S(1)}, u32[]{:S(2)}, u32[]{:S(2)}) collective-permute-start(f16[19,4,4,256]{3,2,1,0:T(4,128)(2,1)S(1)} %get-tuple-element.46), channel_id=1, source_target_pairs={{1,2},{2,1},{3,0},{0,3},{5,6},{6,5},{7,4},{4,7},{9,10},{10,9},{11,... | collective-permute-start | bytes 466952 | tf_op jit(solution)/shard_map/ppermute | solution.py:537
  3.5 0.0 copy-done.3
  3.6 0.6 %collective-permute-start.3 = (f16[256,256]{1,0:T(8,128)(2,1)S(1)}, f16[256,256]{1,0:T(8,128)(2,1)S(1)}, u32[]{:S(2)}, u32[]{:S(2)}) collective-permute-start(f16[256,256]{1,0:T(8,128)(2,1)S(1)} %maximum_maximum_fusion), channel_id=1, source_target_pairs={{0,4},{4,0},{8,12},{12,8},{16,20},{20,16},{24,28},{28,24},{1,5},{5... | collective-permute-start | bytes 393224 | tf_op jit(solution)/shard_map/ppermute | solution.py:537
  4.2 0.4 %collective-permute-start = (f16[19,4,4,256]{3,2,1,0:T(4,128)(2,1)S(1)}, f16[19,4,4,256]{3,2,1,0:T(4,128)(2,1)S(1)}, u32[]{:S(2)}, u32[]{:S(2)}) collective-permute-start(f16[19,4,4,256]{3,2,1,0:T(4,128)(2,1)S(1)} %get-tuple-element.30), channel_id=1, source_target_pairs={{0,1},{1,0},{2,3},{3,2},{4,5},{5,4},{6,7},{7,6},{8,9},{9,8},{10,11... | collective-permute-start | bytes 466952 | tf_op jit(solution)/shard_map/ppermute | solution.py:537
  4.7 4.4 %collective-permute-start.2 = (f16[12,16,256]{2,1,0:T(8,128)(2,1)S(1)}, f16[12,16,256]{2,1,0:T(8,128)(2,1)S(1)}, u32[]{:S(2)}, u32[]{:S(2)}) collective-permute-start(f16[12,16,256]{2,1,0:T(8,128)(2,1)S(1)} %fusion), channel_id=1, source_target_pairs={{4,8},{8,4},{12,16},{16,12},{20,24},{24,20},{5,9},{9,5},{13,17},{1... | collective-permute-start | bytes 294920 | tf_op jit(solution)/shard_map/ppermute | solution.py:537
  9.1 0.1 add_convert_fusion
  9.2 0.0 collective-permute-done
  9.2 0.0 collective-permute-done.1
  9.2 0.1 broadcast_select_fusion.1
  9.3 0.2 maximum_convert_fusion.wing_ref
  9.5 1.8 %shard_map.149.rest_ref = f32[12,4,24,256]{3,2,1,0:T(8,128)S(1)} custom-call(f32[12,4,16,256]{3,2,1,0:T(8,128)S(1)} %get-tuple-element.24.source_ref, f32[12,4,16,256]{3,2,1,0:T(8,128)S(1)} %get-tuple-element.25.store_ref, s32[4,16,256]{2,1,0:T(8,128)S(1)} %get-tuple-element.26.kinds_ref, f32[19,4,8,256]{3,2,1,0:T(8,128)S(1)} %maximum_convert_fusion.wing_ref, ...), custom_call_target="tpu_custom_call" | custom-call | tf_op jit(solution)/shard_map/pallas_call | solution.py:561
  11.2 0.0 collective-permute-done.3
  11.3 0.1 broadcast_in_dim.19.flags_ref
  11.4 0.6 %shard_map.150 = f32[456,256]{1,0:T(8,128)S(1)} custom-call(f32[3,8,256]{2,1,0:T(8,128)S(1)} %broadcast_in_dim.19.flags_ref, f32[12,4,24,256]{3,2,1,0:T(8,128)S(1)} %shard_map.149.rest_ref, f32[12,16,256]{2,1,0:T(8,128)S(1)} %convert.26.halo_ref.halo0_ref, f32[12,4,16,256]{3,2,1,0:T(8,128)S(1)} %get-tuple-element.24.source_ref, ...), custom_call_target="tpu_custom_call" | custom-call | tf_op jit(solution)/shard_map/pallas_call | solution.py:561
  12.0 0.1 collective-permute-start.5
  12.0 0.2 collective-permute-done.2
  12.3 0.0 copy-start.4
  12.3 0.0 copy-start.5
  12.3 0.0 copy-start.6
  12.3 0.6 %shard_map.151 = f32[456,256]{1,0:T(8,128)S(1)} custom-call(f32[3,8,256]{2,1,0:T(8,128)S(1)} %broadcast_in_dim.19.flags_ref, f32[12,4,24,256]{3,2,1,0:T(8,128)S(1)} %shard_map.149.rest_ref, f32[12,16,256]{2,1,0:T(8,128)S(1)} %convert_element_type.59.halo_ref.halo1_ref, f32[12,4,16,256]{3,2,1,0:T(8,128)S(1)} %get-tuple-element.24.source_ref, ...), custom_call_target="tpu_custom_call" | custom-call | tf_op jit(solution)/shard_map/pallas_call | solution.py:561
  13.0 1.6 %collective-permute-start.6 = (bf16[256,128]{1,0:T(8,128)(2,1)S(1)}, bf16[256,128]{1,0:T(8,128)(2,1)S(1)}, u32[]{:S(2)}, u32[]{:S(2)}) collective-permute-start(bf16[256,128]{1,0:T(8,128)(2,1)S(1)} %pad_maximum_fusion.1), channel_id=1, source_target_pairs={{0,8},{4,12},{8,0},{12,4},{16,24},{20,28},{24,16},{28,20},{1,9},{5... | collective-permute-start | bytes 196616 | tf_op jit(solution)/shard_map/ppermute | solution.py:644
  14.6 2.5 %collective-permute-start.7 = (bf16[256,128]{1,0:T(8,128)(2,1)S(1)}, bf16[256,128]{1,0:T(8,128)(2,1)S(1)}, u32[]{:S(2)}, u32[]{:S(2)}) collective-permute-start(bf16[256,128]{1,0:T(8,128)(2,1)S(1)} %pad_maximum_fusion.1), channel_id=1, source_target_pairs={{0,16},{4,20},{8,24},{12,28},{16,0},{20,4},{24,8},{28,12},{1,17},{... | collective-permute-start | bytes 196616 | tf_op jit(solution)/shard_map/ppermute | solution.py:644
  17.1 0.3 %collective-permute-start.8 = (bf16[256,128]{1,0:T(8,128)(2,1)S(1)}, bf16[256,128]{1,0:T(8,128)(2,1)S(1)}, u32[]{:S(2)}, u32[]{:S(2)}) collective-permute-start(bf16[256,128]{1,0:T(8,128)(2,1)S(1)} %pad_maximum_fusion.1), channel_id=1, source_target_pairs={{0,24},{4,28},{8,16},{12,20},{16,8},{20,12},{24,0},{28,4},{1,25},{... | collective-permute-start | bytes 196616 | tf_op jit(solution)/shard_map/ppermute | solution.py:644
  17.4 3.8 %collective-permute-start.4 = (f16[456,256]{1,0:T(8,128)(2,1)S(1)}, f16[456,256]{1,0:T(8,128)(2,1)S(1)}, u32[]{:S(2)}, u32[]{:S(2)}) collective-permute-start(f16[456,256]{1,0:T(8,128)(2,1)S(1)} %convert_element_type.60), channel_id=1, source_target_pairs={{4,8},{8,4},{12,16},{16,12},{20,24},{24,20},{5,9},{9,5},{13,17},{1... | collective-permute-start | bytes 700424 | tf_op jit(solution)/shard_map/ppermute | solution.py:537
  21.2 0.0 copy-done.4
  21.2 0.0 copy-done.5
  21.3 0.0 copy-done.6
  21.9 3.1 %shard_map.152 = (f32[12,4,16,256]{3,2,1,0:T(8,128)S(1)}, f32[12,4,16,256]{3,2,1,0:T(8,128)S(1)}) custom-call(f32[3,8,256]{2,1,0:T(8,128)S(1)} %broadcast_in_dim.19.flags_ref, f32[12,4,24,256]{3,2,1,0:T(8,128)S(1)} %shard_map.149.rest_ref, f32[12,16,256]{2,1,0:T(8,128)S(1)} %convert_element_type.59.halo_ref.halo1_ref, ...), custom_call_target="tpu_custom_call" | custom-call | tf_op jit(solution)/shard_map/pallas_call | solution.py:561
  25.1 0.0 collective-permute-done.5
  25.1 0.0 copy-start
  25.1 0.6 %shard_map.153.other_ref = f32[3,12,16,256]{3,2,1,0:T(8,128)S(1)} custom-call(f32[3,8,256]{2,1,0:T(8,128)S(1)} %broadcast_in_dim.19.flags_ref, f32[456,256]{1,0:T(8,128)S(1)} %convert_element_type.62.halo_ref, f32[12,4,16,256]{3,2,1,0:T(8,128)S(1)} %get-tuple-element.25.store_ref, s32[4,16,256]{2,1,0:T(8,128)S(1)} %get-tuple-element.26.kinds_ref, ...), custom_call_target="tpu_custom_call" | custom-call | tf_op jit(solution)/shard_map/pallas_call | solution.py:561
  25.7 0.0 copy-start.1
  25.7 0.0 copy-start.2
  25.7 0.0 collective-permute-done.6
  25.7 0.0 collective-permute-done.7
  25.7 0.0 collective-permute-done.8
  25.8 0.3 copy-done
  26.1 1.0 %shard_map.154.incoming_ref = f32[128,128]{1,0:T(8,128)S(1)} custom-call(s32[8,128]{1,0:T(8,128)S(1)} %pad.12.index_ref, s32[8,128]{1,0:T(8,128)S(1)} %pad.13.block_ref, bf16[1024,128]{1,0:T(8,128)(2,1)S(1)} %pad_maximum_fusion.rows_ref, bf16[8,128,128]{2,1,0:T(8,128)(2,1)S(1)} %copy-done), custom_call_target="tpu_custom_call" | custom-call | tf_op jit(solution)/shard_map/pallas_call | solution.py:561
  27.1 1.4 %collective-permute-done.4 = f16[456,256]{1,0:T(8,128)(2,1)S(1)} collective-permute-done((f16[456,256]{1,0:T(8,128)(2,1)S(1)}, f16[456,256]{1,0:T(8,128)(2,1)S(1)}, u32[]{:S(2)}, u32[]{:S(2)}) %collective-permute-start.4) | collective-permute-done | bytes 233504 | tf_op jit(solution)/shard_map/ppermute | solution.py:537
  28.6 0.0 copy-done.1
  28.6 0.0 copy-done.2
  28.6 1.6 %shard_map.155 = (f32[120,128]{1,0:T(8,128)}, f32[12,4,16,256]{3,2,1,0:T(8,128)}, f32[12,4,16,256]{3,2,1,0:T(8,128)}) custom-call(f32[3,8,256]{2,1,0:T(8,128)S(1)} %broadcast_in_dim.19.flags_ref, f32[12,4,16,256]{3,2,1,0:T(8,128)S(1)} %get-tuple-element.37.rest_ref, f32[12,4,16,256]{3,2,1,0:T(8,128)S(1)} %get-tuple-element.38.total_ref, ...), custom_call_target="tpu_custom_call" | custom-call | tf_op jit(solution)/shard_map/pallas_call | solution.py:674
  (22 shorter events, 0.4 us)
Async XLA Ops:
  2.3 1.3 %copy-start.3 = (bf16[1,1,120,128]{3,2,1,0:T(8,128)(2,1)S(1)}, bf16[1,1,120,128]{3,2,1,0:T(8,128)(2,1)}, u32[]{:S(2)}) copy-start(bf16[1,1,120,128]{3,2,1,0:T(8,128)(2,1)} %param.22) | copy-start | bytes 92164
  2.5 6.7 %collective-permute-start.1 = (f16[19,4,4,256]{3,2,1,0:T(4,128)(2,1)S(1)}, f16[19,4,4,256]{3,2,1,0:T(4,128)(2,1)S(1)}, u32[]{:S(2)}, u32[]{:S(2)}) collective-permute-start(f16[19,4,4,256]{3,2,1,0:T(4,128)(2,1)S(1)} %get-tuple-element.46), channel_id=1, source_target_pairs={{1,2},{2,1},{3,0},{0,3},{5,6},{6,5},{7,4},{4,7},{9,10},{10,9},{11,... | collective-permute-start | bytes 466952 | tf_op jit(solution)/shard_map/ppermute | solution.py:537
  3.6 7.6 %collective-permute-start.3 = (f16[256,256]{1,0:T(8,128)(2,1)S(1)}, f16[256,256]{1,0:T(8,128)(2,1)S(1)}, u32[]{:S(2)}, u32[]{:S(2)}) collective-permute-start(f16[256,256]{1,0:T(8,128)(2,1)S(1)} %maximum_maximum_fusion), channel_id=1, source_target_pairs={{0,4},{4,0},{8,12},{12,8},{16,20},{20,16},{24,28},{28,24},{1,5},{5... | collective-permute-start | bytes 393224 | tf_op jit(solution)/shard_map/ppermute | solution.py:537
  4.2 4.9 %collective-permute-start = (f16[19,4,4,256]{3,2,1,0:T(4,128)(2,1)S(1)}, f16[19,4,4,256]{3,2,1,0:T(4,128)(2,1)S(1)}, u32[]{:S(2)}, u32[]{:S(2)}) collective-permute-start(f16[19,4,4,256]{3,2,1,0:T(4,128)(2,1)S(1)} %get-tuple-element.30), channel_id=1, source_target_pairs={{0,1},{1,0},{2,3},{3,2},{4,5},{5,4},{6,7},{7,6},{8,9},{9,8},{10,11... | collective-permute-start | bytes 466952 | tf_op jit(solution)/shard_map/ppermute | solution.py:537
  4.7 7.6 %collective-permute-start.2 = (f16[12,16,256]{2,1,0:T(8,128)(2,1)S(1)}, f16[12,16,256]{2,1,0:T(8,128)(2,1)S(1)}, u32[]{:S(2)}, u32[]{:S(2)}) collective-permute-start(f16[12,16,256]{2,1,0:T(8,128)(2,1)S(1)} %fusion), channel_id=1, source_target_pairs={{4,8},{8,4},{12,16},{16,12},{20,24},{24,20},{5,9},{9,5},{13,17},{1... | collective-permute-start | bytes 294920 | tf_op jit(solution)/shard_map/ppermute | solution.py:537
  12.0 13.1 %collective-permute-start.5 = (f16[456,256]{1,0:T(8,128)(2,1)S(1)}, f16[456,256]{1,0:T(8,128)(2,1)S(1)}, u32[]{:S(2)}, u32[]{:S(2)}) collective-permute-start(f16[456,256]{1,0:T(8,128)(2,1)S(1)} %convert_element_type.58), channel_id=1, source_target_pairs={{0,4},{4,0},{8,12},{12,8},{16,20},{20,16},{24,28},{28,24},{1,5},{5... | collective-permute-start | bytes 700424 | tf_op jit(solution)/shard_map/ppermute | solution.py:537
  12.3 8.9 %copy-start.4 = (s32[1,1,120,4]{2,3,1,0:T(4,128)S(1)}, s32[1,1,120,4]{2,3,1,0:T(4,128)}, u32[]{:S(2)}) copy-start(s32[1,1,120,4]{2,3,1,0:T(4,128)} %param.20) | copy-start | bytes 5764
  12.3 8.9 %copy-start.5 = (s32[1,1,120,4]{2,3,1,0:T(4,128)S(1)}, s32[1,1,120,4]{2,3,1,0:T(4,128)}, u32[]{:S(2)}) copy-start(s32[1,1,120,4]{2,3,1,0:T(4,128)} %param.19) | copy-start | bytes 5764
  12.3 9.0 %copy-start.6 = (s32[1,1,120,4]{2,3,1,0:T(4,128)S(1)}, s32[1,1,120,4]{2,3,1,0:T(4,128)}, u32[]{:S(2)}) copy-start(s32[1,1,120,4]{2,3,1,0:T(4,128)} %param.21) | copy-start | bytes 5764
  13.0 12.7 %collective-permute-start.6 = (bf16[256,128]{1,0:T(8,128)(2,1)S(1)}, bf16[256,128]{1,0:T(8,128)(2,1)S(1)}, u32[]{:S(2)}, u32[]{:S(2)}) collective-permute-start(bf16[256,128]{1,0:T(8,128)(2,1)S(1)} %pad_maximum_fusion.1), channel_id=1, source_target_pairs={{0,8},{4,12},{8,0},{12,4},{16,24},{20,28},{24,16},{28,20},{1,9},{5... | collective-permute-start | bytes 196616 | tf_op jit(solution)/shard_map/ppermute | solution.py:644
  14.6 11.1 %collective-permute-start.7 = (bf16[256,128]{1,0:T(8,128)(2,1)S(1)}, bf16[256,128]{1,0:T(8,128)(2,1)S(1)}, u32[]{:S(2)}, u32[]{:S(2)}) collective-permute-start(bf16[256,128]{1,0:T(8,128)(2,1)S(1)} %pad_maximum_fusion.1), channel_id=1, source_target_pairs={{0,16},{4,20},{8,24},{12,28},{16,0},{20,4},{24,8},{28,12},{1,17},{... | collective-permute-start | bytes 196616 | tf_op jit(solution)/shard_map/ppermute | solution.py:644
  17.1 8.7 %collective-permute-start.8 = (bf16[256,128]{1,0:T(8,128)(2,1)S(1)}, bf16[256,128]{1,0:T(8,128)(2,1)S(1)}, u32[]{:S(2)}, u32[]{:S(2)}) collective-permute-start(bf16[256,128]{1,0:T(8,128)(2,1)S(1)} %pad_maximum_fusion.1), channel_id=1, source_target_pairs={{0,24},{4,28},{8,16},{12,20},{16,8},{20,12},{24,0},{28,4},{1,25},{... | collective-permute-start | bytes 196616 | tf_op jit(solution)/shard_map/ppermute | solution.py:644
  17.4 11.1 %collective-permute-start.4 = (f16[456,256]{1,0:T(8,128)(2,1)S(1)}, f16[456,256]{1,0:T(8,128)(2,1)S(1)}, u32[]{:S(2)}, u32[]{:S(2)}) collective-permute-start(f16[456,256]{1,0:T(8,128)(2,1)S(1)} %convert_element_type.60), channel_id=1, source_target_pairs={{4,8},{8,4},{12,16},{16,12},{20,24},{24,20},{5,9},{9,5},{13,17},{1... | collective-permute-start | bytes 700424 | tf_op jit(solution)/shard_map/ppermute | solution.py:537
  25.1 1.0 %copy-start = (bf16[8,128,128]{2,1,0:T(8,128)(2,1)S(1)}, bf16[8,128,128]{2,1,0:T(8,128)(2,1)}, u32[]{:S(2)}) copy-start(bf16[8,128,128]{2,1,0:T(8,128)(2,1)} %view_ref.1) | copy-start | bytes 786436
  25.7 2.9 %copy-start.1 = (f32[1,1,120,128]{3,2,1,0:T(8,128)S(1)}, f32[1,1,120,128]{3,2,1,0:T(8,128)}, u32[]{:S(2)}) copy-start(f32[1,1,120,128]{3,2,1,0:T(8,128)} %param.24) | copy-start | bytes 184324
  25.7 2.9 %copy-start.2 = (f32[1,1,120,128]{3,2,1,0:T(8,128)S(1)}, f32[1,1,120,128]{3,2,1,0:T(8,128)}, u32[]{:S(2)}) copy-start(f32[1,1,120,128]{3,2,1,0:T(8,128)} %param.25) | copy-start | bytes 184324

commit v7 on v6

--- a/solution.py
+++ b/solution.py
@@ -20,6 +20,9 @@
 COPIES = 4
 ROWS = 8
 LINK = jnp.float16
+SIDE_SCALE = 2.0**14
+FIRST_SCALE = 2.0**15
+SECOND_SCALE = 2.0**9
 RAD_SCALE = 8192.0
 f32, bf16 = jnp.float32, jnp.bfloat16
 
@@ -155,10 +158,10 @@
     for f in range(nf):
         if f % part == 0:
             copies[2 + f // part].wait()
-        edge_ref[0, f] = source_ref[f, 0] * INV_CENTER
-        edge_ref[1, f] = source_ref[f, ca - 1] * INV_CENTER
+        edge_ref[0, f] = source_ref[f, 0] * (INV_CENTER * FIRST_SCALE)
+        edge_ref[1, f] = source_ref[f, ca - 1] * (INV_CENTER * FIRST_SCALE)
         for a in range(ca):
-            side_ref[f, a] = both(source_ref, f, a) * INV_CENTER
+            side_ref[f, a] = both(source_ref, f, a) * (INV_CENTER * SIDE_SCALE)
     for copy in copies[2 + COPIES :]:
         copy.wait()
     outer = (place < 2) | (place >= ROWS - 2)
@@ -166,9 +169,9 @@
         for a in range(ca):
             side_ref[nf + f, a] = jnp.where(
                 outer, both(store_ref, f, a), swapped(both(store_ref, nf // 2 + f, a))
-            )
+            ) * SIDE_SCALE
     for a in range(ca):
-        side_ref[nf + nf // 2, a] = both(kinds_ref, a).astype(f32)
+        side_ref[nf + nf // 2, a] = both(kinds_ref, a).astype(f32) * SIDE_SCALE
 
 
 def wing_store(wing_ref, f, a):
@@ -236,7 +239,7 @@
     for f in range(nf):
         rest = choose(rest_ref[f, 0], rest_ref[f, ca - 1])
         wing = choose(wing_ref[f, 0], wing_ref[f, ca - 1])
-        own = rest[:cz] + tall(cond_ref[f], cz) * halo_ref[f]
+        own = rest[:cz] + tall(cond_ref[f] * (1.0 / FIRST_SCALE), cz) * halo_ref[f]
         direction = (ALPHA[1] * INV_CENTER) * choose(source_ref[f, 0], source_ref[f, ca - 1]) + BETA[1] * own
         beside = ALPHA[1] * wing + BETA[1] * rest[cz:]
         next_ref[f] = (ALPHA[1] * INV_CENTER) * choose(source_ref[f, 1], source_ref[f, ca - 2]) + BETA[1] * choose(
@@ -244,9 +247,9 @@
         )
         dir_ref[f, 0, :cz] = direction
         dir_ref[f, 0, cz:] = beside
-        message_ref[2 * f * cz : (2 * f + 1) * cz] = direction
+        message_ref[2 * f * cz : (2 * f + 1) * cz] = direction * SECOND_SCALE
         message_ref[(2 * f + 1) * cz : 2 * (f + 1) * cz] = own
-        put_beside(message_ref, 2 * nf * cz + KEPT * f, beside_rows(wing, beside))
+        put_beside(message_ref, 2 * nf * cz + KEPT * f, beside_rows(wing, beside) * SECOND_SCALE)
 
     def kinds(a, t):
         rows = slice(t * ROWS, (t + 1) * ROWS)
@@ -255,7 +258,7 @@
     def emit(f, a, image):
         third = pl.ds((2 * f + 1) * cz, cz)
         rest = message_ref[third] - image + tall(cond_ref[f], cz) * next_ref[f]
-        message_ref[third] = ALPHA[2] * dir_ref[f, 0, :cz] + BETA[2] * rest
+        message_ref[third] = (ALPHA[2] * SECOND_SCALE) * dir_ref[f, 0, :cz] + (BETA[2] * SECOND_SCALE) * rest
 
     apply_local(
         dir_ref, lambda f, a: choose(store_ref[f, 0], store_ref[f, ca - 1]), kinds,
@@ -270,7 +273,7 @@
     nf, ca, cz, cr = store_ref.shape
     even = tall(flags_ref[0], cz) > 0.5
     for f in range(nf):
-        cond = tall(cond_ref[f], cz)
+        cond = tall(cond_ref[f] * (1.0 / FIRST_SCALE), cz)
         arrived = {
             0: cond * jnp.where(even, halo1_ref[f], halo0_ref[f]),
             ca - 1: cond * jnp.where(even, halo0_ref[f], halo1_ref[f]),
@@ -372,11 +375,12 @@
     for f in range(nf):
         cond = cond_ref[f]
         wide = tall(cond, cz)
-        old = get_beside(halo_ref, 2 * nf * cz + KEPT * f)
+        scaled = wide * (1.0 / SECOND_SCALE)
+        old = get_beside(halo_ref, 2 * nf * cz + KEPT * f) * (1.0 / SECOND_SCALE)
         moved = jnp.where(place < 4, pltpu.roll(old, ROWS - 2, 0), pltpu.roll(old, 2, 0))
         fix = cond * jnp.where(outer, moved, 0.0)
-        rest = wide * (halo_ref[2 * f * cz : (2 * f + 1) * cz] + BETA[1] * inward(fix, cz))
-        base_ref[f] = rest + wide * halo_ref[(2 * f + 1) * cz : 2 * (f + 1) * cz]
+        rest = scaled * halo_ref[2 * f * cz : (2 * f + 1) * cz] + BETA[1] * wide * inward(fix, cz)
+        base_ref[f] = rest + scaled * halo_ref[(2 * f + 1) * cz : 2 * (f + 1) * cz]
         fixed_ref[f, 0, :cz] = jnp.zeros_like(rest)
         fixed_ref[f, 0, cz:] = BETA[1] * fix
         beside_ref[f] = fix + cond * old
@@ -608,7 +612,7 @@
 
     from_right = jnp.where(azim_even, near_in, far_in)
     from_left = jnp.where(azim_even, far_in, near_in)
-    wings = jnp.concatenate([from_right, from_left], axis=2).astype(f32)
+    wings = jnp.concatenate([from_right, from_left], axis=2).astype(f32) * (1.0 / SIDE_SCALE)
 
     full = here((nf, ca, cz + ROWS, cr), f32)
     rest = call(first_kernel, (full,), (source, storage, materials, wings, cond, coef), (full, full))

time: 30.4 us -> 30.5 us (level)
  no operation moved by 1% of the time
where the time goes in v7:
time: 30.5 us; the launch traced here: 30.2 us
  starting transfers between devices  14.8 us (49%)
  Pallas kernels  10.9 us (36%)
  between operations  1.7 us (6%)
  waiting for transfers between devices  1.61 us (5%)
  other arithmetic  0.81 us (3%)
  local copies, waits for them, and re-layouts  0.44 us (1%)
    ppermute x6, starting transfers between devices, swap(): return lax.ppermute(array, axis, pairs(lax.axis_size(axis), first, closed))  10.3 us
    pallas_call x6, Pallas kernels, call(): pl.pallas_call(kernel, out_shape=outs[0] if single else tuple(outs), in_s...  7.64 us
    ppermute x3, starting transfers between devices, body(): lax.ppermute(pair, 'axial', [(i, i ^ step) for i in range(owners)])  4.45 us
    pallas_call x1, Pallas kernels, body(): pl.pallas_call(ends_kernel, out_shape=(plain, plain, here((ca, cz, cr), j...  1.64 us
    pallas_call x1, Pallas kernels, body(): pl.pallas_call(last_kernel, out_shape=(shape((slots, values), f32), shape...  1.61 us
    ppermute x6, waiting for transfers between devices, swap(): return lax.ppermute(array, axis, pairs(lax.axis_size(axis), first, closed))  1.6 us
  transfers between devices with their start and end apart: 9, of which 2 were waited for; matrix products, arithmetic and copies ran while one was open for 2% of the time, Pallas kernels for 25%

profile of v7, /device:TPU:2, one launch (start us, length us, event | category | flops | bytes accessed | tf_op | source)
XLA Modules:
  0.0 30.2 jit_solution(8425244688374463540)
XLA Ops:
  0.6 1.6 %shard_map.148 = (f32[12,4,16,256]{3,2,1,0:T(8,128)S(1)}, f32[12,4,16,256]{3,2,1,0:T(8,128)S(1)}, s32[4,16,256]{2,1,0:T(8,128)S(1)}, f32[2,12,16,256]{3,2,1,0:T(...) custom-call(f32[12,4,16,256]{3,2,1,0:T(8,128)} %source_hbm.1, ...), custom_call_target="tpu_custom_call" | custom-call | tf_op jit(solution)/shard_map/pallas_call | solution.py:581
  2.3 0.0 copy-start.3
  2.3 0.2 select_convert_fusion.1
  2.5 1.0 %collective-permute-start.1 = (f16[19,4,4,256]{3,2,1,0:T(4,128)(2,1)S(1)}, f16[19,4,4,256]{3,2,1,0:T(4,128)(2,1)S(1)}, u32[]{:S(2)}, u32[]{:S(2)}) collective-permute-start(f16[19,4,4,256]{3,2,1,0:T(4,128)(2,1)S(1)} %get-tuple-element.46), channel_id=1, source_target_pairs={{1,2},{2,1},{3,0},{0,3},{5,6},{6,5},{7,4},{4,7},{9,10},{10,9},{11,... | collective-permute-start | bytes 466952 | tf_op jit(solution)/shard_map/ppermute | solution.py:541
  3.6 0.0 copy-done.3
  3.7 0.6 %collective-permute-start.3 = (f16[256,256]{1,0:T(8,128)(2,1)S(1)}, f16[256,256]{1,0:T(8,128)(2,1)S(1)}, u32[]{:S(2)}, u32[]{:S(2)}) collective-permute-start(f16[256,256]{1,0:T(8,128)(2,1)S(1)} %maximum_maximum_fusion), channel_id=1, source_target_pairs={{0,4},{4,0},{8,12},{12,8},{16,20},{20,16},{24,28},{28,24},{1,5},{5... | collective-permute-start | bytes 393224 | tf_op jit(solution)/shard_map/ppermute | solution.py:541
  4.3 0.4 %collective-permute-start = (f16[19,4,4,256]{3,2,1,0:T(4,128)(2,1)S(1)}, f16[19,4,4,256]{3,2,1,0:T(4,128)(2,1)S(1)}, u32[]{:S(2)}, u32[]{:S(2)}) collective-permute-start(f16[19,4,4,256]{3,2,1,0:T(4,128)(2,1)S(1)} %get-tuple-element.30), channel_id=1, source_target_pairs={{0,1},{1,0},{2,3},{3,2},{4,5},{5,4},{6,7},{7,6},{8,9},{9,8},{10,11... | collective-permute-start | bytes 466952 | tf_op jit(solution)/shard_map/ppermute | solution.py:541
  4.7 4.4 %collective-permute-start.2 = (f16[12,16,256]{2,1,0:T(8,128)(2,1)S(1)}, f16[12,16,256]{2,1,0:T(8,128)(2,1)S(1)}, u32[]{:S(2)}, u32[]{:S(2)}) collective-permute-start(f16[12,16,256]{2,1,0:T(8,128)(2,1)S(1)} %fusion), channel_id=1, source_target_pairs={{4,8},{8,4},{12,16},{16,12},{20,24},{24,20},{5,9},{9,5},{13,17},{1... | collective-permute-start | bytes 294920 | tf_op jit(solution)/shard_map/ppermute | solution.py:541
  9.1 0.1 add_convert_fusion
  9.2 0.0 collective-permute-done
  9.2 0.0 collective-permute-done.1
  9.2 0.1 broadcast_select_fusion.1
  9.3 0.2 convert_multiply_fusion.wing_ref
  9.5 1.8 %shard_map.149.rest_ref = f32[12,4,24,256]{3,2,1,0:T(8,128)S(1)} custom-call(f32[12,4,16,256]{3,2,1,0:T(8,128)S(1)} %get-tuple-element.24.source_ref, f32[12,4,16,256]{3,2,1,0:T(8,128)S(1)} %get-tuple-element.25.store_ref, s32[4,16,256]{2,1,0:T(8,128)S(1)} %get-tuple-element.26.kinds_ref, f32[19,4,8,256]{3,2,1,0:T(8,128)S(1)} %convert_multiply_fusion.wing_ref, ...), custom_call_target="tpu_custom_call" | custom-call | tf_op jit(solution)/shard_map/pallas_call | solution.py:565
  11.2 0.0 collective-permute-done.3
  11.3 0.1 broadcast_in_dim.19.flags_ref
  11.4 0.6 %shard_map.150 = f32[456,256]{1,0:T(8,128)S(1)} custom-call(f32[3,8,256]{2,1,0:T(8,128)S(1)} %broadcast_in_dim.19.flags_ref, f32[12,4,24,256]{3,2,1,0:T(8,128)S(1)} %shard_map.149.rest_ref, f32[12,16,256]{2,1,0:T(8,128)S(1)} %convert.26.halo_ref.halo0_ref, f32[12,4,16,256]{3,2,1,0:T(8,128)S(1)} %get-tuple-element.24.source_ref, ...), custom_call_target="tpu_custom_call" | custom-call | tf_op jit(solution)/shard_map/pallas_call | solution.py:565
  12.0 0.1 collective-permute-start.5
  12.1 0.2 collective-permute-done.2
  12.3 0.0 copy-start.4
  12.3 0.0 copy-start.5
  12.3 0.0 copy-start.6
  12.3 0.6 %shard_map.151 = f32[456,256]{1,0:T(8,128)S(1)} custom-call(f32[3,8,256]{2,1,0:T(8,128)S(1)} %broadcast_in_dim.19.flags_ref, f32[12,4,24,256]{3,2,1,0:T(8,128)S(1)} %shard_map.149.rest_ref, f32[12,16,256]{2,1,0:T(8,128)S(1)} %convert_element_type.59.halo_ref.halo1_ref, f32[12,4,16,256]{3,2,1,0:T(8,128)S(1)} %get-tuple-element.24.source_ref, ...), custom_call_target="tpu_custom_call" | custom-call | tf_op jit(solution)/shard_map/pallas_call | solution.py:565
  13.0 1.6 %collective-permute-start.6 = (bf16[256,128]{1,0:T(8,128)(2,1)S(1)}, bf16[256,128]{1,0:T(8,128)(2,1)S(1)}, u32[]{:S(2)}, u32[]{:S(2)}) collective-permute-start(bf16[256,128]{1,0:T(8,128)(2,1)S(1)} %pad_maximum_fusion.1), channel_id=1, source_target_pairs={{0,8},{4,12},{8,0},{12,4},{16,24},{20,28},{24,16},{28,20},{1,9},{5... | collective-permute-start | bytes 196616 | tf_op jit(solution)/shard_map/ppermute | solution.py:648
  14.6 2.5 %collective-permute-start.7 = (bf16[256,128]{1,0:T(8,128)(2,1)S(1)}, bf16[256,128]{1,0:T(8,128)(2,1)S(1)}, u32[]{:S(2)}, u32[]{:S(2)}) collective-permute-start(bf16[256,128]{1,0:T(8,128)(2,1)S(1)} %pad_maximum_fusion.1), channel_id=1, source_target_pairs={{0,16},{4,20},{8,24},{12,28},{16,0},{20,4},{24,8},{28,12},{1,17},{... | collective-permute-start | bytes 196616 | tf_op jit(solution)/shard_map/ppermute | solution.py:648
  17.1 0.3 %collective-permute-start.8 = (bf16[256,128]{1,0:T(8,128)(2,1)S(1)}, bf16[256,128]{1,0:T(8,128)(2,1)S(1)}, u32[]{:S(2)}, u32[]{:S(2)}) collective-permute-start(bf16[256,128]{1,0:T(8,128)(2,1)S(1)} %pad_maximum_fusion.1), channel_id=1, source_target_pairs={{0,24},{4,28},{8,16},{12,20},{16,8},{20,12},{24,0},{28,4},{1,25},{... | collective-permute-start | bytes 196616 | tf_op jit(solution)/shard_map/ppermute | solution.py:648
  17.4 3.8 %collective-permute-start.4 = (f16[456,256]{1,0:T(8,128)(2,1)S(1)}, f16[456,256]{1,0:T(8,128)(2,1)S(1)}, u32[]{:S(2)}, u32[]{:S(2)}) collective-permute-start(f16[456,256]{1,0:T(8,128)(2,1)S(1)} %convert_element_type.60), channel_id=1, source_target_pairs={{4,8},{8,4},{12,16},{16,12},{20,24},{24,20},{5,9},{9,5},{13,17},{1... | collective-permute-start | bytes 700424 | tf_op jit(solution)/shard_map/ppermute | solution.py:541
  21.3 0.0 copy-done.4
  21.3 0.0 copy-done.5
  21.3 0.0 copy-done.6
  22.0 3.1 %shard_map.152 = (f32[12,4,16,256]{3,2,1,0:T(8,128)S(1)}, f32[12,4,16,256]{3,2,1,0:T(8,128)S(1)}) custom-call(f32[3,8,256]{2,1,0:T(8,128)S(1)} %broadcast_in_dim.19.flags_ref, f32[12,4,24,256]{3,2,1,0:T(8,128)S(1)} %shard_map.149.rest_ref, f32[12,16,256]{2,1,0:T(8,128)S(1)} %convert_element_type.59.halo_ref.halo1_ref, ...), custom_call_target="tpu_custom_call" | custom-call | tf_op jit(solution)/shard_map/pallas_call | solution.py:565
  25.1 0.0 collective-permute-done.5
  25.2 0.0 copy-start
  25.2 0.6 %shard_map.153.other_ref = f32[3,12,16,256]{3,2,1,0:T(8,128)S(1)} custom-call(f32[3,8,256]{2,1,0:T(8,128)S(1)} %broadcast_in_dim.19.flags_ref, f32[456,256]{1,0:T(8,128)S(1)} %convert_element_type.62.halo_ref, f32[12,4,16,256]{3,2,1,0:T(8,128)S(1)} %get-tuple-element.25.store_ref, s32[4,16,256]{2,1,0:T(8,128)S(1)} %get-tuple-element.26.kinds_ref, ...), custom_call_target="tpu_custom_call" | custom-call | tf_op jit(solution)/shard_map/pallas_call | solution.py:565
  25.8 0.0 copy-start.1
  25.8 0.0 copy-start.2
  25.8 0.0 collective-permute-done.6
  25.8 0.0 collective-permute-done.7
  25.8 0.0 collective-permute-done.8
  25.9 0.3 copy-done
  26.1 1.0 %shard_map.154.incoming_ref = f32[128,128]{1,0:T(8,128)S(1)} custom-call(s32[8,128]{1,0:T(8,128)S(1)} %pad.12.index_ref, s32[8,128]{1,0:T(8,128)S(1)} %pad.13.block_ref, bf16[1024,128]{1,0:T(8,128)(2,1)S(1)} %pad_maximum_fusion.rows_ref, bf16[8,128,128]{2,1,0:T(8,128)(2,1)S(1)} %copy-done), custom_call_target="tpu_custom_call" | custom-call | tf_op jit(solution)/shard_map/pallas_call | solution.py:565
  27.2 1.4 %collective-permute-done.4 = f16[456,256]{1,0:T(8,128)(2,1)S(1)} collective-permute-done((f16[456,256]{1,0:T(8,128)(2,1)S(1)}, f16[456,256]{1,0:T(8,128)(2,1)S(1)}, u32[]{:S(2)}, u32[]{:S(2)}) %collective-permute-start.4) | collective-permute-done | bytes 233504 | tf_op jit(solution)/shard_map/ppermute | solution.py:541
  28.6 0.0 copy-done.1
  28.6 0.0 copy-done.2
  28.6 1.6 %shard_map.155 = (f32[120,128]{1,0:T(8,128)}, f32[12,4,16,256]{3,2,1,0:T(8,128)}, f32[12,4,16,256]{3,2,1,0:T(8,128)}) custom-call(f32[3,8,256]{2,1,0:T(8,128)S(1)} %broadcast_in_dim.19.flags_ref, f32[12,4,16,256]{3,2,1,0:T(8,128)S(1)} %get-tuple-element.37.rest_ref, f32[12,4,16,256]{3,2,1,0:T(8,128)S(1)} %get-tuple-element.38.total_ref, ...), custom_call_target="tpu_custom_call" | custom-call | tf_op jit(solution)/shard_map/pallas_call | solution.py:678
  (22 shorter events, 0.4 us)
Async XLA Ops:
  2.3 1.3 %copy-start.3 = (bf16[1,1,120,128]{3,2,1,0:T(8,128)(2,1)S(1)}, bf16[1,1,120,128]{3,2,1,0:T(8,128)(2,1)}, u32[]{:S(2)}) copy-start(bf16[1,1,120,128]{3,2,1,0:T(8,128)(2,1)} %param.22) | copy-start | bytes 92164
  2.5 6.7 %collective-permute-start.1 = (f16[19,4,4,256]{3,2,1,0:T(4,128)(2,1)S(1)}, f16[19,4,4,256]{3,2,1,0:T(4,128)(2,1)S(1)}, u32[]{:S(2)}, u32[]{:S(2)}) collective-permute-start(f16[19,4,4,256]{3,2,1,0:T(4,128)(2,1)S(1)} %get-tuple-element.46), channel_id=1, source_target_pairs={{1,2},{2,1},{3,0},{0,3},{5,6},{6,5},{7,4},{4,7},{9,10},{10,9},{11,... | collective-permute-start | bytes 466952 | tf_op jit(solution)/shard_map/ppermute | solution.py:541
  3.7 7.6 %collective-permute-start.3 = (f16[256,256]{1,0:T(8,128)(2,1)S(1)}, f16[256,256]{1,0:T(8,128)(2,1)S(1)}, u32[]{:S(2)}, u32[]{:S(2)}) collective-permute-start(f16[256,256]{1,0:T(8,128)(2,1)S(1)} %maximum_maximum_fusion), channel_id=1, source_target_pairs={{0,4},{4,0},{8,12},{12,8},{16,20},{20,16},{24,28},{28,24},{1,5},{5... | collective-permute-start | bytes 393224 | tf_op jit(solution)/shard_map/ppermute | solution.py:541
  4.3 4.9 %collective-permute-start = (f16[19,4,4,256]{3,2,1,0:T(4,128)(2,1)S(1)}, f16[19,4,4,256]{3,2,1,0:T(4,128)(2,1)S(1)}, u32[]{:S(2)}, u32[]{:S(2)}) collective-permute-start(f16[19,4,4,256]{3,2,1,0:T(4,128)(2,1)S(1)} %get-tuple-element.30), channel_id=1, source_target_pairs={{0,1},{1,0},{2,3},{3,2},{4,5},{5,4},{6,7},{7,6},{8,9},{9,8},{10,11... | collective-permute-start | bytes 466952 | tf_op jit(solution)/shard_map/ppermute | solution.py:541
  4.7 7.6 %collective-permute-start.2 = (f16[12,16,256]{2,1,0:T(8,128)(2,1)S(1)}, f16[12,16,256]{2,1,0:T(8,128)(2,1)S(1)}, u32[]{:S(2)}, u32[]{:S(2)}) collective-permute-start(f16[12,16,256]{2,1,0:T(8,128)(2,1)S(1)} %fusion), channel_id=1, source_target_pairs={{4,8},{8,4},{12,16},{16,12},{20,24},{24,20},{5,9},{9,5},{13,17},{1... | collective-permute-start | bytes 294920 | tf_op jit(solution)/shard_map/ppermute | solution.py:541
  12.0 13.1 %collective-permute-start.5 = (f16[456,256]{1,0:T(8,128)(2,1)S(1)}, f16[456,256]{1,0:T(8,128)(2,1)S(1)}, u32[]{:S(2)}, u32[]{:S(2)}) collective-permute-start(f16[456,256]{1,0:T(8,128)(2,1)S(1)} %convert_element_type.58), channel_id=1, source_target_pairs={{0,4},{4,0},{8,12},{12,8},{16,20},{20,16},{24,28},{28,24},{1,5},{5... | collective-permute-start | bytes 700424 | tf_op jit(solution)/shard_map/ppermute | solution.py:541
  12.3 9.0 %copy-start.4 = (s32[1,1,120,4]{2,3,1,0:T(4,128)S(1)}, s32[1,1,120,4]{2,3,1,0:T(4,128)}, u32[]{:S(2)}) copy-start(s32[1,1,120,4]{2,3,1,0:T(4,128)} %param.20) | copy-start | bytes 5764
  12.3 9.0 %copy-start.5 = (s32[1,1,120,4]{2,3,1,0:T(4,128)S(1)}, s32[1,1,120,4]{2,3,1,0:T(4,128)}, u32[]{:S(2)}) copy-start(s32[1,1,120,4]{2,3,1,0:T(4,128)} %param.19) | copy-start | bytes 5764
  12.3 9.0 %copy-start.6 = (s32[1,1,120,4]{2,3,1,0:T(4,128)S(1)}, s32[1,1,120,4]{2,3,1,0:T(4,128)}, u32[]{:S(2)}) copy-start(s32[1,1,120,4]{2,3,1,0:T(4,128)} %param.21) | copy-start | bytes 5764
  13.0 12.8 %collective-permute-start.6 = (bf16[256,128]{1,0:T(8,128)(2,1)S(1)}, bf16[256,128]{1,0:T(8,128)(2,1)S(1)}, u32[]{:S(2)}, u32[]{:S(2)}) collective-permute-start(bf16[256,128]{1,0:T(8,128)(2,1)S(1)} %pad_maximum_fusion.1), channel_id=1, source_target_pairs={{0,8},{4,12},{8,0},{12,4},{16,24},{20,28},{24,16},{28,20},{1,9},{5... | collective-permute-start | bytes 196616 | tf_op jit(solution)/shard_map/ppermute | solution.py:648
  14.6 11.2 %collective-permute-start.7 = (bf16[256,128]{1,0:T(8,128)(2,1)S(1)}, bf16[256,128]{1,0:T(8,128)(2,1)S(1)}, u32[]{:S(2)}, u32[]{:S(2)}) collective-permute-start(bf16[256,128]{1,0:T(8,128)(2,1)S(1)} %pad_maximum_fusion.1), channel_id=1, source_target_pairs={{0,16},{4,20},{8,24},{12,28},{16,0},{20,4},{24,8},{28,12},{1,17},{... | collective-permute-start | bytes 196616 | tf_op jit(solution)/shard_map/ppermute | solution.py:648
  17.1 8.7 %collective-permute-start.8 = (bf16[256,128]{1,0:T(8,128)(2,1)S(1)}, bf16[256,128]{1,0:T(8,128)(2,1)S(1)}, u32[]{:S(2)}, u32[]{:S(2)}) collective-permute-start(bf16[256,128]{1,0:T(8,128)(2,1)S(1)} %pad_maximum_fusion.1), channel_id=1, source_target_pairs={{0,24},{4,28},{8,16},{12,20},{16,8},{20,12},{24,0},{28,4},{1,25},{... | collective-permute-start | bytes 196616 | tf_op jit(solution)/shard_map/ppermute | solution.py:648
  17.4 11.1 %collective-permute-start.4 = (f16[456,256]{1,0:T(8,128)(2,1)S(1)}, f16[456,256]{1,0:T(8,128)(2,1)S(1)}, u32[]{:S(2)}, u32[]{:S(2)}) collective-permute-start(f16[456,256]{1,0:T(8,128)(2,1)S(1)} %convert_element_type.60), channel_id=1, source_target_pairs={{4,8},{8,4},{12,16},{16,12},{20,24},{24,20},{5,9},{9,5},{13,17},{1... | collective-permute-start | bytes 700424 | tf_op jit(solution)/shard_map/ppermute | solution.py:541
  25.2 1.0 %copy-start = (bf16[8,128,128]{2,1,0:T(8,128)(2,1)S(1)}, bf16[8,128,128]{2,1,0:T(8,128)(2,1)}, u32[]{:S(2)}) copy-start(bf16[8,128,128]{2,1,0:T(8,128)(2,1)} %view_ref.1) | copy-start | bytes 786436
  25.8 2.8 %copy-start.1 = (f32[1,1,120,128]{3,2,1,0:T(8,128)S(1)}, f32[1,1,120,128]{3,2,1,0:T(8,128)}, u32[]{:S(2)}) copy-start(f32[1,1,120,128]{3,2,1,0:T(8,128)} %param.24) | copy-start | bytes 184324
  25.8 2.8 %copy-start.2 = (f32[1,1,120,128]{3,2,1,0:T(8,128)S(1)}, f32[1,1,120,128]{3,2,1,0:T(8,128)}, u32[]{:S(2)}) copy-start(f32[1,1,120,128]{3,2,1,0:T(8,128)} %param.25) | copy-start | bytes 184324

commit v8 on v7

--- a/solution.py
+++ b/solution.py
@@ -600,7 +600,6 @@
     fold = cr // values
     folded = panels.astype(f32) * RAD_SCALE
     folded = jnp.concatenate(jnp.split(folded, fold, axis=0), axis=1)
-    far = far
     far_in = swap(far, "azim", 1, True)
     layer0 = after(edges, far)[1].reshape(nf * cz, cr)
     message0 = jnp.concatenate([layer0, folded], axis=0).astype(LINK)
@@ -641,7 +640,8 @@
     )
 
     partner = after(message, message1)[nf * cz :].astype(f32) * (1.0 / RAD_SCALE)
-    partner = jnp.concatenate(jnp.split(partner, fold, axis=1), axis=0).astype(bf16)
+    partner = jnp.concatenate(jnp.split(partner, fold, axis=1), axis=0).astype(bf16)[:slots]
+    panels = panels[:slots]
     if owners <= 8 and owners & (owners - 1) == 0:
         pair = jnp.concatenate([panels, partner], axis=0)
         others = [
@@ -651,15 +651,14 @@
         owner = vis_owner[0, 0].T ^ me
     else:
         pair = jnp.stack([panels, partner])
-        panels = jnp.where(is_even, pair, pair[::-1]).reshape(2 * tile, values)
+        panels = jnp.where(is_even, pair, pair[::-1]).reshape(2 * slots, values)
         groups = [list(range(k, owners, 2)) for k in range(2)]
         panels = lax.all_gather(panels, "axial", axis=0, tiled=True, axis_index_groups=groups)
-        panels = panels.reshape(owners // 2, 2 * tile, values).reshape(owners * tile, values)
         owner = vis_owner[0, 0].T
     pad = ((0, -visible % ROWS), (0, -slots % 128))
-    index = jnp.pad(owner * tile + vis_slot[0, 0].T, pad, constant_values=-1)
+    index = jnp.pad(owner * slots + vis_slot[0, 0].T, pad, constant_values=-1)
     block = jnp.pad(vis_block[0, 0].T, pad)
-    chunk = tile * 8 if owners % 8 == 0 else tile * owners
+    chunk = slots * 8 if owners % 8 == 0 else slots * owners
     incoming = call(
         functools.partial(panel_kernel, chunk, visible),
         (here((index.shape[1], values), f32),),

time: 30.5 us -> 30.1 us (0.987)
  waiting for transfers between devices: 1.61 us -> 1.3 us
  transfers between devices with their start and end apart: 9 -> 9, of which waited for: 2 -> 2; matrix products, arithmetic and copies ran while one was open for 2% -> 2% of each run, Pallas kernels for 25% -> 26%
where the time goes in v8:
time: 30.1 us; the launch traced here: 29.9 us
  starting transfers between devices  14.7 us (49%)
  Pallas kernels  10.9 us (36%)
  between operations  1.69 us (6%)
  waiting for transfers between devices  1.3 us (4%)
  other arithmetic  0.81 us (3%)
  local copies, waits for them, and re-layouts  0.44 us (1%)
    ppermute x6, starting transfers between devices, swap(): return lax.ppermute(array, axis, pairs(lax.axis_size(axis), first, closed))  10.3 us
    pallas_call x6, Pallas kernels, call(): pl.pallas_call(kernel, out_shape=outs[0] if single else tuple(outs), in_s...  7.65 us
    ppermute x3, starting transfers between devices, body(): lax.ppermute(pair, 'axial', [(i, i ^ step) for i in range(owners)])  4.45 us
    pallas_call x1, Pallas kernels, body(): pl.pallas_call(ends_kernel, out_shape=(plain, plain, here((ca, cz, cr), j...  1.64 us
    pallas_call x1, Pallas kernels, body(): pl.pallas_call(last_kernel, out_shape=(shape((slots, values), f32), shape...  1.61 us
    ppermute x6, waiting for transfers between devices, swap(): return lax.ppermute(array, axis, pairs(lax.axis_size(axis), first, closed))  1.3 us
  transfers between devices with their start and end apart: 9, of which 2 were waited for; matrix products, arithmetic and copies ran while one was open for 2% of the time, Pallas kernels for 26%

profile of v8, /device:TPU:2, one launch (start us, length us, event | category | flops | bytes accessed | tf_op | source)
XLA Modules:
  0.0 29.9 jit_solution(15798676692070002594)
XLA Ops:
  0.6 1.6 %shard_map.148 = (f32[12,4,16,256]{3,2,1,0:T(8,128)S(1)}, f32[12,4,16,256]{3,2,1,0:T(8,128)S(1)}, s32[4,16,256]{2,1,0:T(8,128)S(1)}, f32[2,12,16,256]{3,2,1,0:T(...) custom-call(f32[12,4,16,256]{3,2,1,0:T(8,128)} %source_hbm.1, ...), custom_call_target="tpu_custom_call" | custom-call | tf_op jit(solution)/shard_map/pallas_call | solution.py:581
  2.3 0.0 copy-start.3
  2.3 0.2 select_convert_fusion.1
  2.5 1.0 %collective-permute-start.1 = (f16[19,4,4,256]{3,2,1,0:T(4,128)(2,1)S(1)}, f16[19,4,4,256]{3,2,1,0:T(4,128)(2,1)S(1)}, u32[]{:S(2)}, u32[]{:S(2)}) collective-permute-start(f16[19,4,4,256]{3,2,1,0:T(4,128)(2,1)S(1)} %get-tuple-element.46), channel_id=1, source_target_pairs={{1,2},{2,1},{3,0},{0,3},{5,6},{6,5},{7,4},{4,7},{9,10},{10,9},{11,... | collective-permute-start | bytes 466952 | tf_op jit(solution)/shard_map/ppermute | solution.py:541
  3.6 0.0 copy-done.3
  3.7 0.6 %collective-permute-start.3 = (f16[256,256]{1,0:T(8,128)(2,1)S(1)}, f16[256,256]{1,0:T(8,128)(2,1)S(1)}, u32[]{:S(2)}, u32[]{:S(2)}) collective-permute-start(f16[256,256]{1,0:T(8,128)(2,1)S(1)} %maximum_maximum_fusion), channel_id=1, source_target_pairs={{0,4},{4,0},{8,12},{12,8},{16,20},{20,16},{24,28},{28,24},{1,5},{5... | collective-permute-start | bytes 393224 | tf_op jit(solution)/shard_map/ppermute | solution.py:541
  4.3 0.4 %collective-permute-start = (f16[19,4,4,256]{3,2,1,0:T(4,128)(2,1)S(1)}, f16[19,4,4,256]{3,2,1,0:T(4,128)(2,1)S(1)}, u32[]{:S(2)}, u32[]{:S(2)}) collective-permute-start(f16[19,4,4,256]{3,2,1,0:T(4,128)(2,1)S(1)} %get-tuple-element.30), channel_id=1, source_target_pairs={{0,1},{1,0},{2,3},{3,2},{4,5},{5,4},{6,7},{7,6},{8,9},{9,8},{10,11... | collective-permute-start | bytes 466952 | tf_op jit(solution)/shard_map/ppermute | solution.py:541
  4.7 4.4 %collective-permute-start.2 = (f16[12,16,256]{2,1,0:T(8,128)(2,1)S(1)}, f16[12,16,256]{2,1,0:T(8,128)(2,1)S(1)}, u32[]{:S(2)}, u32[]{:S(2)}) collective-permute-start(f16[12,16,256]{2,1,0:T(8,128)(2,1)S(1)} %fusion), channel_id=1, source_target_pairs={{4,8},{8,4},{12,16},{16,12},{20,24},{24,20},{5,9},{9,5},{13,17},{1... | collective-permute-start | bytes 294920 | tf_op jit(solution)/shard_map/ppermute | solution.py:541
  9.1 0.1 add_convert_fusion
  9.2 0.0 collective-permute-done
  9.2 0.0 collective-permute-done.1
  9.2 0.1 broadcast_select_fusion.1
  9.3 0.2 convert_multiply_fusion.wing_ref
  9.4 1.8 %shard_map.149.rest_ref = f32[12,4,24,256]{3,2,1,0:T(8,128)S(1)} custom-call(f32[12,4,16,256]{3,2,1,0:T(8,128)S(1)} %get-tuple-element.24.source_ref, f32[12,4,16,256]{3,2,1,0:T(8,128)S(1)} %get-tuple-element.25.store_ref, s32[4,16,256]{2,1,0:T(8,128)S(1)} %get-tuple-element.26.kinds_ref, f32[19,4,8,256]{3,2,1,0:T(8,128)S(1)} %convert_multiply_fusion.wing_ref, ...), custom_call_target="tpu_custom_call" | custom-call | tf_op jit(solution)/shard_map/pallas_call | solution.py:565
  11.2 0.0 collective-permute-done.3
  11.3 0.1 broadcast_in_dim.19.flags_ref
  11.4 0.6 %shard_map.150 = f32[456,256]{1,0:T(8,128)S(1)} custom-call(f32[3,8,256]{2,1,0:T(8,128)S(1)} %broadcast_in_dim.19.flags_ref, f32[12,4,24,256]{3,2,1,0:T(8,128)S(1)} %shard_map.149.rest_ref, f32[12,16,256]{2,1,0:T(8,128)S(1)} %convert.26.halo_ref.halo0_ref, f32[12,4,16,256]{3,2,1,0:T(8,128)S(1)} %get-tuple-element.24.source_ref, ...), custom_call_target="tpu_custom_call" | custom-call | tf_op jit(solution)/shard_map/pallas_call | solution.py:565
  12.0 0.1 collective-permute-start.5
  12.0 0.2 collective-permute-done.2
  12.3 0.0 copy-start.4
  12.3 0.0 copy-start.5
  12.3 0.0 copy-start.6
  12.3 0.6 %shard_map.151 = f32[456,256]{1,0:T(8,128)S(1)} custom-call(f32[3,8,256]{2,1,0:T(8,128)S(1)} %broadcast_in_dim.19.flags_ref, f32[12,4,24,256]{3,2,1,0:T(8,128)S(1)} %shard_map.149.rest_ref, f32[12,16,256]{2,1,0:T(8,128)S(1)} %convert_element_type.59.halo_ref.halo1_ref, f32[12,4,16,256]{3,2,1,0:T(8,128)S(1)} %get-tuple-element.24.source_ref, ...), custom_call_target="tpu_custom_call" | custom-call | tf_op jit(solution)/shard_map/pallas_call | solution.py:565
  13.0 1.6 %collective-permute-start.6 = (bf16[240,128]{1,0:T(8,128)(2,1)S(1)}, bf16[240,128]{1,0:T(8,128)(2,1)S(1)}, u32[]{:S(2)}, u32[]{:S(2)}) collective-permute-start(bf16[240,128]{1,0:T(8,128)(2,1)S(1)} %fusion.1), channel_id=1, source_target_pairs={{0,8},{4,12},{8,0},{12,4},{16,24},{20,28},{24,16},{28,20},{1,9},{5... | collective-permute-start | bytes 184328 | tf_op jit(solution)/shard_map/ppermute | solution.py:648
  14.6 2.5 %collective-permute-start.7 = (bf16[240,128]{1,0:T(8,128)(2,1)S(1)}, bf16[240,128]{1,0:T(8,128)(2,1)S(1)}, u32[]{:S(2)}, u32[]{:S(2)}) collective-permute-start(bf16[240,128]{1,0:T(8,128)(2,1)S(1)} %fusion.1), channel_id=1, source_target_pairs={{0,16},{4,20},{8,24},{12,28},{16,0},{20,4},{24,8},{28,12},{1,17},{... | collective-permute-start | bytes 184328 | tf_op jit(solution)/shard_map/ppermute | solution.py:648
  17.1 0.3 %collective-permute-start.8 = (bf16[240,128]{1,0:T(8,128)(2,1)S(1)}, bf16[240,128]{1,0:T(8,128)(2,1)S(1)}, u32[]{:S(2)}, u32[]{:S(2)}) collective-permute-start(bf16[240,128]{1,0:T(8,128)(2,1)S(1)} %fusion.1), channel_id=1, source_target_pairs={{0,24},{4,28},{8,16},{12,20},{16,8},{20,12},{24,0},{28,4},{1,25},{... | collective-permute-start | bytes 184328 | tf_op jit(solution)/shard_map/ppermute | solution.py:648
  17.4 3.8 %collective-permute-start.4 = (f16[456,256]{1,0:T(8,128)(2,1)S(1)}, f16[456,256]{1,0:T(8,128)(2,1)S(1)}, u32[]{:S(2)}, u32[]{:S(2)}) collective-permute-start(f16[456,256]{1,0:T(8,128)(2,1)S(1)} %convert_element_type.60), channel_id=1, source_target_pairs={{4,8},{8,4},{12,16},{16,12},{20,24},{24,20},{5,9},{9,5},{13,17},{1... | collective-permute-start | bytes 700424 | tf_op jit(solution)/shard_map/ppermute | solution.py:541
  21.2 0.0 copy-done.4
  21.2 0.0 copy-done.5
  21.3 0.0 copy-done.6
  22.0 3.1 %shard_map.152 = (f32[12,4,16,256]{3,2,1,0:T(8,128)S(1)}, f32[12,4,16,256]{3,2,1,0:T(8,128)S(1)}) custom-call(f32[3,8,256]{2,1,0:T(8,128)S(1)} %broadcast_in_dim.19.flags_ref, f32[12,4,24,256]{3,2,1,0:T(8,128)S(1)} %shard_map.149.rest_ref, f32[12,16,256]{2,1,0:T(8,128)S(1)} %convert_element_type.59.halo_ref.halo1_ref, ...), custom_call_target="tpu_custom_call" | custom-call | tf_op jit(solution)/shard_map/pallas_call | solution.py:565
  25.1 0.0 collective-permute-done.5
  25.2 0.0 copy-start
  25.2 0.6 %shard_map.153.other_ref = f32[3,12,16,256]{3,2,1,0:T(8,128)S(1)} custom-call(f32[3,8,256]{2,1,0:T(8,128)S(1)} %broadcast_in_dim.19.flags_ref, f32[456,256]{1,0:T(8,128)S(1)} %convert_element_type.62.halo_ref, f32[12,4,16,256]{3,2,1,0:T(8,128)S(1)} %get-tuple-element.25.store_ref, s32[4,16,256]{2,1,0:T(8,128)S(1)} %get-tuple-element.26.kinds_ref, ...), custom_call_target="tpu_custom_call" | custom-call | tf_op jit(solution)/shard_map/pallas_call | solution.py:565
  25.8 0.0 copy-start.1
  25.8 0.0 copy-start.2
  25.8 0.0 collective-permute-done.6
  25.8 0.0 collective-permute-done.7
  25.8 0.0 collective-permute-done.8
  25.8 0.3 copy-done
  26.1 1.0 %shard_map.154.incoming_ref = f32[128,128]{1,0:T(8,128)S(1)} custom-call(s32[8,128]{1,0:T(8,128)S(1)} %pad.12.index_ref, s32[8,128]{1,0:T(8,128)S(1)} %pad.13.block_ref, bf16[960,128]{1,0:T(8,128)(2,1)S(1)} %pad_maximum_fusion.rows_ref, bf16[8,128,128]{2,1,0:T(8,128)(2,1)S(1)} %copy-done), custom_call_target="tpu_custom_call" | custom-call | tf_op jit(solution)/shard_map/pallas_call | solution.py:565
  27.2 1.1 %collective-permute-done.4 = f16[456,256]{1,0:T(8,128)(2,1)S(1)} collective-permute-done((f16[456,256]{1,0:T(8,128)(2,1)S(1)}, f16[456,256]{1,0:T(8,128)(2,1)S(1)}, u32[]{:S(2)}, u32[]{:S(2)}) %collective-permute-start.4) | collective-permute-done | bytes 233504 | tf_op jit(solution)/shard_map/ppermute | solution.py:541
  28.3 0.0 copy-done.1
  28.3 0.0 copy-done.2
  28.3 1.6 %shard_map.155 = (f32[120,128]{1,0:T(8,128)}, f32[12,4,16,256]{3,2,1,0:T(8,128)}, f32[12,4,16,256]{3,2,1,0:T(8,128)}) custom-call(f32[3,8,256]{2,1,0:T(8,128)S(1)} %broadcast_in_dim.19.flags_ref, f32[12,4,16,256]{3,2,1,0:T(8,128)S(1)} %get-tuple-element.37.rest_ref, f32[12,4,16,256]{3,2,1,0:T(8,128)S(1)} %get-tuple-element.38.total_ref, ...), custom_call_target="tpu_custom_call" | custom-call | tf_op jit(solution)/shard_map/pallas_call | solution.py:677
  (21 shorter events, 0.4 us)
Async XLA Ops:
  2.3 1.3 %copy-start.3 = (bf16[1,1,120,128]{3,2,1,0:T(8,128)(2,1)S(1)}, bf16[1,1,120,128]{3,2,1,0:T(8,128)(2,1)}, u32[]{:S(2)}) copy-start(bf16[1,1,120,128]{3,2,1,0:T(8,128)(2,1)} %param.22) | copy-start | bytes 92164
  2.5 6.7 %collective-permute-start.1 = (f16[19,4,4,256]{3,2,1,0:T(4,128)(2,1)S(1)}, f16[19,4,4,256]{3,2,1,0:T(4,128)(2,1)S(1)}, u32[]{:S(2)}, u32[]{:S(2)}) collective-permute-start(f16[19,4,4,256]{3,2,1,0:T(4,128)(2,1)S(1)} %get-tuple-element.46), channel_id=1, source_target_pairs={{1,2},{2,1},{3,0},{0,3},{5,6},{6,5},{7,4},{4,7},{9,10},{10,9},{11,... | collective-permute-start | bytes 466952 | tf_op jit(solution)/shard_map/ppermute | solution.py:541
  3.7 7.6 %collective-permute-start.3 = (f16[256,256]{1,0:T(8,128)(2,1)S(1)}, f16[256,256]{1,0:T(8,128)(2,1)S(1)}, u32[]{:S(2)}, u32[]{:S(2)}) collective-permute-start(f16[256,256]{1,0:T(8,128)(2,1)S(1)} %maximum_maximum_fusion), channel_id=1, source_target_pairs={{0,4},{4,0},{8,12},{12,8},{16,20},{20,16},{24,28},{28,24},{1,5},{5... | collective-permute-start | bytes 393224 | tf_op jit(solution)/shard_map/ppermute | solution.py:541
  4.3 4.9 %collective-permute-start = (f16[19,4,4,256]{3,2,1,0:T(4,128)(2,1)S(1)}, f16[19,4,4,256]{3,2,1,0:T(4,128)(2,1)S(1)}, u32[]{:S(2)}, u32[]{:S(2)}) collective-permute-start(f16[19,4,4,256]{3,2,1,0:T(4,128)(2,1)S(1)} %get-tuple-element.30), channel_id=1, source_target_pairs={{0,1},{1,0},{2,3},{3,2},{4,5},{5,4},{6,7},{7,6},{8,9},{9,8},{10,11... | collective-permute-start | bytes 466952 | tf_op jit(solution)/shard_map/ppermute | solution.py:541
  4.7 7.6 %collective-permute-start.2 = (f16[12,16,256]{2,1,0:T(8,128)(2,1)S(1)}, f16[12,16,256]{2,1,0:T(8,128)(2,1)S(1)}, u32[]{:S(2)}, u32[]{:S(2)}) collective-permute-start(f16[12,16,256]{2,1,0:T(8,128)(2,1)S(1)} %fusion), channel_id=1, source_target_pairs={{4,8},{8,4},{12,16},{16,12},{20,24},{24,20},{5,9},{9,5},{13,17},{1... | collective-permute-start | bytes 294920 | tf_op jit(solution)/shard_map/ppermute | solution.py:541
  12.0 13.2 %collective-permute-start.5 = (f16[456,256]{1,0:T(8,128)(2,1)S(1)}, f16[456,256]{1,0:T(8,128)(2,1)S(1)}, u32[]{:S(2)}, u32[]{:S(2)}) collective-permute-start(f16[456,256]{1,0:T(8,128)(2,1)S(1)} %convert_element_type.58), channel_id=1, source_target_pairs={{0,4},{4,0},{8,12},{12,8},{16,20},{20,16},{24,28},{28,24},{1,5},{5... | collective-permute-start | bytes 700424 | tf_op jit(solution)/shard_map/ppermute | solution.py:541
  12.3 8.9 %copy-start.4 = (s32[1,1,120,4]{2,3,1,0:T(4,128)S(1)}, s32[1,1,120,4]{2,3,1,0:T(4,128)}, u32[]{:S(2)}) copy-start(s32[1,1,120,4]{2,3,1,0:T(4,128)} %param.20) | copy-start | bytes 5764
  12.3 8.9 %copy-start.5 = (s32[1,1,120,4]{2,3,1,0:T(4,128)S(1)}, s32[1,1,120,4]{2,3,1,0:T(4,128)}, u32[]{:S(2)}) copy-start(s32[1,1,120,4]{2,3,1,0:T(4,128)} %param.19) | copy-start | bytes 5764
  12.3 9.0 %copy-start.6 = (s32[1,1,120,4]{2,3,1,0:T(4,128)S(1)}, s32[1,1,120,4]{2,3,1,0:T(4,128)}, u32[]{:S(2)}) copy-start(s32[1,1,120,4]{2,3,1,0:T(4,128)} %param.21) | copy-start | bytes 5764
  13.0 12.8 %collective-permute-start.6 = (bf16[240,128]{1,0:T(8,128)(2,1)S(1)}, bf16[240,128]{1,0:T(8,128)(2,1)S(1)}, u32[]{:S(2)}, u32[]{:S(2)}) collective-permute-start(bf16[240,128]{1,0:T(8,128)(2,1)S(1)} %fusion.1), channel_id=1, source_target_pairs={{0,8},{4,12},{8,0},{12,4},{16,24},{20,28},{24,16},{28,20},{1,9},{5... | collective-permute-start | bytes 184328 | tf_op jit(solution)/shard_map/ppermute | solution.py:648
  14.6 11.2 %collective-permute-start.7 = (bf16[240,128]{1,0:T(8,128)(2,1)S(1)}, bf16[240,128]{1,0:T(8,128)(2,1)S(1)}, u32[]{:S(2)}, u32[]{:S(2)}) collective-permute-start(bf16[240,128]{1,0:T(8,128)(2,1)S(1)} %fusion.1), channel_id=1, source_target_pairs={{0,16},{4,20},{8,24},{12,28},{16,0},{20,4},{24,8},{28,12},{1,17},{... | collective-permute-start | bytes 184328 | tf_op jit(solution)/shard_map/ppermute | solution.py:648
  17.1 8.7 %collective-permute-start.8 = (bf16[240,128]{1,0:T(8,128)(2,1)S(1)}, bf16[240,128]{1,0:T(8,128)(2,1)S(1)}, u32[]{:S(2)}, u32[]{:S(2)}) collective-permute-start(bf16[240,128]{1,0:T(8,128)(2,1)S(1)} %fusion.1), channel_id=1, source_target_pairs={{0,24},{4,28},{8,16},{12,20},{16,8},{20,12},{24,0},{28,4},{1,25},{... | collective-permute-start | bytes 184328 | tf_op jit(solution)/shard_map/ppermute | solution.py:648
  17.4 10.8 %collective-permute-start.4 = (f16[456,256]{1,0:T(8,128)(2,1)S(1)}, f16[456,256]{1,0:T(8,128)(2,1)S(1)}, u32[]{:S(2)}, u32[]{:S(2)}) collective-permute-start(f16[456,256]{1,0:T(8,128)(2,1)S(1)} %convert_element_type.60), channel_id=1, source_target_pairs={{4,8},{8,4},{12,16},{16,12},{20,24},{24,20},{5,9},{9,5},{13,17},{1... | collective-permute-start | bytes 700424 | tf_op jit(solution)/shard_map/ppermute | solution.py:541
  25.2 1.0 %copy-start = (bf16[8,128,128]{2,1,0:T(8,128)(2,1)S(1)}, bf16[8,128,128]{2,1,0:T(8,128)(2,1)}, u32[]{:S(2)}) copy-start(bf16[8,128,128]{2,1,0:T(8,128)(2,1)} %view_ref.1) | copy-start | bytes 786436
  25.8 2.5 %copy-start.1 = (f32[1,1,120,128]{3,2,1,0:T(8,128)S(1)}, f32[1,1,120,128]{3,2,1,0:T(8,128)}, u32[]{:S(2)}) copy-start(f32[1,1,120,128]{3,2,1,0:T(8,128)} %param.24) | copy-start | bytes 184324
  25.8 2.5 %copy-start.2 = (f32[1,1,120,128]{3,2,1,0:T(8,128)S(1)}, f32[1,1,120,128]{3,2,1,0:T(8,128)}, u32[]{:S(2)}) copy-start(f32[1,1,120,128]{3,2,1,0:T(8,128)} %param.25) | copy-start | bytes 184324
